TPU v7x, 256 devices: a whole 4x4x8 slice. The times are simulated.
256 devices in a mesh: ctx: 32 (over y, x, core), head: 8 (over z).
Axes of the slice: x: 4, y: 4, z: 8, core: 2. Of those that a mesh axis runs over, the one named last changes fastest.
Arguments:
- queries: bfloat16 [8192, 4096], P('ctx', 'head'), may hold values from -6 to 6
- keys: bfloat16 [8192, 4096], P('ctx', 'head'), may hold values from -6 to 6
- values: bfloat16 [8192, 4096], P('ctx', 'head'), may hold values from -6 to 6
- doc_ids: int32 [8192], P('ctx'), may hold values from 0 to 3, never falling along the last dimension, each value on 1 to 4096 neighbouring positions
- w_out: bfloat16 [4096, 8192], P('head'), may hold values from -0.09375 to 0.09375
Outputs:
- mixed: bfloat16 [8192, 8192], P(('ctx', 'head'))
Inputs may be any that keep to these rules, and one draw needn't show every extreme that they name: `doc_ids`: never falls along the sequence; each of the 4 documents holds 1 to 4096 consecutive tokens, and one holds exactly 4096.
All inputs are finite; a program needn't handle non-finite values.
Results may differ from a plain program's by a relative error of at most 0.022.
Values may be sent and summed in bfloat16 or wider, within the bound.
No kernel may reach another device: no remote copies, remote signals or barrier semaphores. Data moves between devices by JAX's collectives and lax.ppermute only.
A program may use at most 128 MiB of HBM per device.

v0:
```python
import math

import jax
import jax.numpy as jnp
from jax import lax
from jax.sharding import PartitionSpec as P

DH = 128
SPAN = 256
ITERS = 10


ridge_lambda = 0.02
upper_end = 1.0 + ridge_lambda
center = (upper_end + ridge_lambda) / 2.0
radius = (upper_end - ridge_lambda) / 2.0
highest = lax.Precision.HIGHEST


def normalize(block):
    return (
        block
        * lax.rsqrt(jnp.mean(block * block, axis=-1, keepdims=True) + 1e-06)
        * (1.0 / math.sqrt(block.shape[-1]))
    )


def shards(queries, keys, values, doc_ids, w_out):
    rows_dev, width = queries.shape
    heads = width // DH
    nblocks = rows_dev // SPAN

    def per_head(array):
        return array.astype(jnp.float32).reshape(rows_dev, heads, DH).transpose(1, 0, 2)

    query_n = normalize(per_head(queries))
    key_n = normalize(per_head(keys))
    value_f = per_head(values)
    segment = doc_ids.astype(jnp.float32)
    last_id = segment[-1]
    member = (segment == last_id).astype(jnp.float32)
    tail_k = jnp.einsum("htd,hte->hde", key_n * member[None, :, None], key_n, precision=highest)
    tail_v = jnp.einsum("htd,hte->hde", value_f * member[None, :, None], key_n, precision=highest)
    tail_n = jnp.sum(member)
    stacked = (
        lax.all_gather(tail_k[None].astype(jnp.bfloat16), "ctx", axis=0, tiled=True).astype(
            jnp.float32
        ),
        lax.all_gather(tail_v[None].astype(jnp.bfloat16), "ctx", axis=0, tiled=True).astype(
            jnp.float32
        ),
        lax.all_gather(tail_n[None].astype(jnp.bfloat16), "ctx", axis=0, tiled=True).astype(
            jnp.float32
        ),
        lax.all_gather(last_id[None].astype(jnp.bfloat16), "ctx", axis=0, tiled=True).astype(
            jnp.float32
        ),
    )
    index = lax.axis_index("ctx")
    order = jnp.arange(lax.axis_size("ctx"))
    all_last = stacked[3]
    prior_last0 = jnp.sum(jnp.where(order == index - 1, all_last, 0.0)) + jnp.where(
        index == 0, -1.0, 0.0
    )
    weight = ((order < index) & (all_last == prior_last0)).astype(jnp.float32)
    prior_k0 = jnp.einsum("j,jhde->hde", weight, stacked[0], precision=highest)
    prior_v0 = jnp.einsum("j,jhde->hde", weight, stacked[1], precision=highest)
    prior_n0 = jnp.sum(weight * stacked[2])
    query_c = query_n.reshape(heads, nblocks, SPAN, DH)
    key_c = key_n.reshape(heads, nblocks, SPAN, DH)
    value_c = value_f.reshape(heads, nblocks, SPAN, DH)
    seg_c = segment.reshape(nblocks, SPAN)

    def advance(carry, blocks):
        state_k, state_v, state_n, state_last = carry
        key_b, value_b, seg_b = blocks
        keep = seg_b[-1] == state_last
        inside_b = (seg_b == seg_b[-1]).astype(jnp.float32)
        new_k = jnp.where(keep, state_k, 0.0) + jnp.einsum(
            "htd,hte->hde", key_b * inside_b[None, :, None], key_b, precision=highest
        )
        new_v = jnp.where(keep, state_v, 0.0) + jnp.einsum(
            "htd,hte->hde", value_b * inside_b[None, :, None], key_b, precision=highest
        )
        new_n = jnp.where(keep, state_n, 0.0) + jnp.sum(inside_b)
        return ((new_k, new_v, new_n, seg_b[-1]), (state_k, state_v, state_n, state_last))

    blocks = (key_c.transpose(1, 0, 2, 3), value_c.transpose(1, 0, 2, 3), seg_c)
    _, (prior_k, prior_v, prior_n, prior_last) = lax.scan(
        advance, (prior_k0, prior_v0, prior_n0, prior_last0), blocks
    )
    prior_mask = (seg_c == prior_last[:, None]).astype(jnp.float32)
    positions = jnp.arange(SPAN)
    causal = positions[None, :] <= positions[:, None]
    inside = (causal[None] & (seg_c[:, :, None] == seg_c[:, None, :])).astype(jnp.float32)
    counts = prior_mask * prior_n[:, None] + jnp.sum(inside, axis=-1)
    inverse = 1.0 / counts

    def scores(field):
        return jnp.einsum("hctd,hcsd->hcts", field, key_c, precision=highest) * inside[None]

    def apply(field):
        before = (
            jnp.einsum("chde,hcte->hctd", prior_k, field, precision=highest)
            * prior_mask[None, :, :, None]
        )
        within = jnp.einsum("hcts,hcsd->hctd", scores(field), key_c, precision=highest)
        return (before + within) * inverse[None, :, :, None] + ridge_lambda * field

    def turn(step, state):
        iterate, remain, search, factor = state
        iterate = iterate + search
        remain = remain - apply(search)
        factor_new = 1.0 / (2.0 * center / radius - factor)
        search = factor_new * factor * search + 2.0 * factor_new / radius * remain
        return (iterate, remain, search, factor_new)

    state = (
        jnp.zeros_like(query_c),
        query_c,
        query_c / center,
        jnp.asarray(radius / center, jnp.float32),
    )
    iterate, remain, search, factor = lax.fori_loop(0, ITERS, turn, state)
    iterate = iterate + search
    output = (
        jnp.einsum("chde,hcte->hctd", prior_v, iterate, precision=highest)
        * prior_mask[None, :, :, None]
    )
    output = output + jnp.einsum("hcts,hcsd->hctd", scores(iterate), value_c, precision=highest)
    output = normalize(output) * math.sqrt(DH)
    mixed_in = (
        output.reshape(heads, rows_dev, DH)
        .transpose(1, 0, 2)
        .reshape(rows_dev, heads * DH)
        .astype(jnp.bfloat16)
    )
    return lax.psum_scatter(
        jnp.dot(mixed_in, w_out, preferred_element_type=jnp.float32).astype(jnp.bfloat16),
        "head",
        scatter_dimension=0,
        tiled=True,
    )


def solution(mesh):
    return jax.shard_map(
        shards,
        mesh=mesh,
        in_specs=(P("ctx", "head"), P("ctx", "head"), P("ctx", "head"), P("ctx"), P("head", None)),
        out_specs=P(("ctx", "head"), None),
        check_vma=False,
    )
```

profile of v0, /device:TPU:96, one launch (start us, length us, event | category | flops | bytes accessed | tf_op | source)
XLA Modules:
  0.0 225.4 jit_solution(3515357936220532535)
XLA Ops:
  6.5 0.7 convert_element_type.73
  7.2 0.6 slice.3
  7.8 1.3 broadcast_select_fusion
  9.1 1.1 copy.29
  10.3 1.4 convolution_convert_fusion.2
  11.8 1.1 copy.47
  12.9 1.4 convolution_convert_fusion.1
  14.3 0.6 slice.9
  14.9 1.3 dynamic-slice
  16.3 1.4 dynamic-update-slice
  17.7 0.6 convert_reduce_fusion.1
  18.3 1.4 dynamic-update-slice.1
  19.7 67.7 %all-reduce.2 = (bf16[32]{0:T(256)(128)(2,1)S(1)}, bf16[32]{0:T(256)(128)(2,1)S(1)}) all-reduce(bf16[32]{0:T(256)(128)(2,1)S(1)} %dynamic-update-slice, bf16[32]{0:T(256)(128)(2,1)S(1)} %dynamic-update-slice.1), channel_id=1, replica_groups=mesh['ctx'=32,'head'=8] {'ctx'}, use_global_device_ids=true, to_apply=%add | all-reduce | flops 64 | bytes 256
  87.4 1.1 copy.28
  88.6 0.2 copy.33
  89.0 0.2 copy.32
  89.2 0.2 copy.31
  89.4 0.7 fusion.55
  90.7 0.2 convert_reduce_fusion
  90.9 0.7 select_reduce_fusion
  91.6 0.7 add_divide_fusion
  92.3 0.1 fusion.50
  92.4 4.6 %fusion.14 = f32[1,4,128,128]{3,0,2,1:T(1,128)S(1)} fusion(bf16[32,4,128,128]{3,2,1,0:T(8,128)(2,1)} %bitcast.142, pred[32]{0:T(512)(128)(4,1)S(1)} %get-tuple-element.258), kind=kOutput, calls=%fused_computation.21 | convolution fusion | flops 4194304 | bytes 4456480 | tf_op jit(solution)/shard_map/j,jhde->hde/dot_general | solution.py:66
  97.0 20.9 %all-gather.7.cloned.1.call-done = bf16[128,128,128]{2,1,0:T(8,128)(2,1)} async-done(((bf16[4,128,128]{2,1,0:T(8,128)(2,1)}), bf16[128,128,128]{2,1,0:T(8,128)(2,1)}) %all-gather.7.cloned.1.call-update) | async-done | bytes 4194320 | tf_op jit(solution)/shard_map/all_gather | solution.py:49
  118.0 4.6 %fusion.12 = f32[1,4,128,128]{3,0,2,1:T(1,128)S(1)} fusion(bf16[32,4,128,128]{3,2,1,0:T(8,128)(2,1)} %bitcast.143, pred[32]{0:T(512)(128)(4,1)S(1)} %get-tuple-element.258), kind=kOutput, calls=%fused_computation.19 | convolution fusion | flops 4194304 | bytes 4456480 | tf_op jit(solution)/shard_map/j,jhde->hde/dot_general | solution.py:67
  122.6 31.8 %while.5 = (s32[]{:T(128)}, f32[4,1,256,128]{3,2,0,1:T(8,128)S(1)}, f32[4,1,256,128]{3,2,0,1:T(8,128)S(1)}, f32[4,1,256,128]{3,2,0,1:T(8,128)S(1)}, f32[]{:T(128...) while((s32[]{:T(128)}, ...), condition=%wide.region_7.8_spmd.clone, body=%wide.region_6.7_spmd.clone.sunk | while | flops 1008599040 | bytes 9178327 | solution.py:124
  122.6 0.1 convert_bitcast_fusion.4
  122.7 0.6 convolution_multiply_fusion.6
  123.3 1.0 convolution_multiply_fusion.7
  124.4 1.4 multiply_add_fusion.2
  125.8 0.1 convert_bitcast_fusion.4
  125.9 0.6 convolution_multiply_fusion.6
  126.5 1.0 convolution_multiply_fusion.7
  127.5 1.4 multiply_add_fusion.2
  129.1 0.6 convolution_multiply_fusion.6
  129.7 1.0 convolution_multiply_fusion.7
  130.7 1.4 multiply_add_fusion.2
  132.2 0.6 convolution_multiply_fusion.6
  132.8 1.0 convolution_multiply_fusion.7
  133.8 1.4 multiply_add_fusion.2
  135.4 0.6 convolution_multiply_fusion.6
  136.0 1.0 convolution_multiply_fusion.7
  137.0 1.4 multiply_add_fusion.2
  138.5 0.6 convolution_multiply_fusion.6
  139.2 1.0 convolution_multiply_fusion.7
  140.2 1.4 multiply_add_fusion.2
  141.6 0.1 convert_bitcast_fusion.4
  141.7 0.6 convolution_multiply_fusion.6
  142.3 1.0 convolution_multiply_fusion.7
  143.3 1.4 multiply_add_fusion.2
  144.9 0.6 convolution_multiply_fusion.6
  145.5 1.0 convolution_multiply_fusion.7
  146.5 1.4 multiply_add_fusion.2
  148.0 0.6 convolution_multiply_fusion.6
  148.6 1.0 convolution_multiply_fusion.7
  149.7 1.4 multiply_add_fusion.2
  151.2 0.6 convolution_multiply_fusion.6
  151.8 1.0 convolution_multiply_fusion.7
  152.8 1.4 multiply_add_fusion.2
  154.4 0.6 convolution_multiply_fusion.3
  155.0 1.0 convolution_multiply_fusion.2
  156.0 0.7 multiply_reduce_fusion
  156.9 7.7 %convolution_convert_fusion = bf16[256,8192]{1,0:T(8,128)(2,1)} fusion(bf16[256,512]{0,1:T(8,128)(2,1)S(1)} %bitcast.146, bf16[512,8192]{1,0:T(8,128)(2,1)} %param.11), kind=kOutput, calls=%fused_computation.18 | convolution fusion | flops 2149580800 | bytes 12845056 | tf_op jit(solution)/shard_map/dot_general | solution.py:139
  164.6 54.3 %reduce-scatter.2.cloned.1.call-done = bf16[32,8192]{1,0:T(8,128)(2,1)} async-done(((bf16[256,8192]{1,0:T(8,128)(2,1)}), bf16[32,8192]{1,0:T(8,128)(2,1)}) %reduce-scatter.2.cloned.1.call-update) | async-done | bytes 524304 | tf_op jit(solution)/shard_map/reduce_scatter | solution.py:138
  (29 shorter events, 1.2 us)
Async XLA Ops:
  6.5 85.9 %all-gather.5.cloned.1.call-start = ((), (), s32[]{:S(2)}) async-start(), calls=%async_computation.2 | async-start | bytes 4325376 | tf_op jit(solution)/shard_map/all_gather | solution.py:46
  10.3 81.3 %copy-start = (s32[256]{0:T(256)S(1)}, s32[256]{0:T(256)}, u32[]{:S(2)}) copy-start(s32[256]{0:T(256)} %param.10) | copy-start | bytes 3076
  11.7 106.2 %all-gather.7.cloned.1.call-start = ((), (), s32[]{:S(2)}) async-start(), calls=%async_computation.3 | async-start | bytes 4325376 | tf_op jit(solution)/shard_map/all_gather | solution.py:49
  14.3 204.6 %reduce-scatter.2.cloned.1.call-start = ((), (), s32[]{:S(2)}) async-start(), calls=%async_computation.1 | async-start | bytes 4718592 | tf_op jit(solution)/shard_map/reduce_scatter | solution.py:138
Sparse Core Ops, SparseCore 0:
  11.8 53.0 all-gather.4
  67.5 50.4 all-gather.6
  164.7 54.1 reduce-scatter.1
where the time goes:
time: 228 us; the launch traced here: 225 us
  waiting for transfers between devices  75.4 us (33%)
  blocking collectives  67.7 us (30%)
  matrix products  51.8 us (23%)
  between operations  14 us (6%)
  local copies, waits for them, and re-layouts  9.19 us (4%)
  other arithmetic  6.32 us (3%)
    unnamed x1, blocking collectives  67.7 us
    reduce_scatter x1, waiting for transfers between devices, shards(): lax.psum_scatter(jnp.dot(mixed_in, w_out, preferred_element_type=jnp.floa...  54.3 us
    all_gather x1, waiting for transfers between devices, shards(): lax.all_gather(tail_v[None].astype(jnp.bfloat16), 'ctx', axis=0, tiled=True)  20.9 us
    dot_general x10, matrix products, apply(): jnp.einsum('hcts,hcsd->hctd', scores(field), key_c, precision=highest)  13.6 us
    dot_general x11, matrix products, scores(): jnp.einsum('hctd,hcsd->hcts', field, key_c, precision=highest)  11.1 us
    dot_general x1, matrix products, shards(): jnp.dot(mixed_in, w_out, preferred_element_type=jnp.float32)  7.68 us
    unnamed x12, local copies, waits for them, and re-layouts  6.91 us
    dot_general x10, matrix products, apply(): jnp.einsum('chde,hcte->hctd', prior_k, field, precision=highest)  6.1 us
  transfers between devices with their start and end apart: 3, of which 2 were waited for; matrix products, arithmetic and copies ran while one was open for 7% of the time, Pallas kernels for 0%

commit v1 on v0

v1 whole, which is shorter than its diff:
```python
import functools
import math

import jax
import jax.numpy as jnp
from jax import lax
from jax.experimental import pallas as pl
from jax.experimental.pallas import tpu as pltpu
from jax.sharding import PartitionSpec as P

DH = 128
ITERS = 10
N_HEAD = 8

ridge_lambda = 0.02
upper_end = 1.0 + ridge_lambda
center = (upper_end + ridge_lambda) / 2.0
radius = (upper_end - ridge_lambda) / 2.0

f32 = jnp.float32
bf16 = jnp.bfloat16


def dot(a, b):
    return jnp.dot(a, b, preferred_element_type=f32)


def split(field):
    high = field.astype(bf16)
    low = (field - high.astype(f32)).astype(bf16)
    return jnp.concatenate([high, low], axis=1)


def scale_of(rows):
    return lax.rsqrt(jnp.mean(rows * rows, axis=-1, keepdims=True) + 1e-06) * (
        1.0 / math.sqrt(DH)
    )


def tails_kernel(k_ref, v_ref, doc_ref, send_ref, kt_ref):
    tokens, width = k_ref.shape
    heads = width // DH
    doc = doc_ref[...].astype(f32)
    last = jnp.max(doc)
    member_row = (doc == last).astype(f32)
    member = jnp.broadcast_to(member_row, (DH, tokens)).T
    parts = send_ref.shape[0]
    size = send_ref.shape[1] - 16
    per = DH // size
    for h in range(heads):
        cols = slice(h * DH, (h + 1) * DH)
        k = k_ref[:, cols].astype(f32)
        scale = scale_of(k) * member
        kt = k.T.astype(bf16)
        kt_ref[h * DH : (h + 1) * DH, :] = kt
        right = jnp.concatenate(
            [k * (scale * scale), v_ref[:, cols].astype(f32) * scale], axis=1
        ).astype(bf16)
        state = dot(kt, right).astype(bf16)
        send_ref[h * per : (h + 1) * per, :size, :] = state[:, :DH].reshape(per, size, DH)
        base = (heads + h) * per
        send_ref[base : base + per, :size, :] = state[:, DH:].reshape(per, size, DH)
    number = jnp.broadcast_to(jnp.sum(member_row, axis=1, keepdims=True), (8, DH))
    note = jnp.concatenate([jnp.full((8, DH), last), number], axis=0).astype(bf16)
    send_ref[:, size:, :] = jnp.broadcast_to(note[None], (parts, 16, DH))


def prefix_kernel(recv_ref, send_ref, meta_ref):
    blocks, rows, _ = recv_ref.shape
    size = rows - 16
    me = lax.axis_index("ctx")
    state = jnp.zeros((size, DH), f32)
    number = jnp.zeros((8, DH), f32)
    last = jnp.full((8, DH), -1.0, f32)
    mine_number, mine_last = number, last
    for b in range(blocks):
        mine_number = jnp.where(me == b, number, mine_number)
        mine_last = jnp.where(me == b, last, mine_last)
        send_ref[b] = state.astype(bf16)
        note = recv_ref[b, size:, :].astype(f32)
        keep = (note[:8] == last).astype(f32)
        state = state * keep[:1] + recv_ref[b, :size, :].astype(f32)
        number = number * keep + note[8:]
        last = note[:8]
    meta_ref[:8] = mine_number
    meta_ref[8:] = mine_last


def solve_kernel(
    offsets,
    pieces,
    q_ref,
    k_ref,
    v_ref,
    doc_ref,
    kt_ref,
    state_ref,
    meta_ref,
    w_ref,
    *rest,
):
    outs = rest[: len(pieces)]
    w_vmem, doc_col, right, weight, p_ref, r_ref, x_ref, w_sem = rest[len(pieces) :]
    tokens, width = q_ref.shape
    heads = width // DH
    share = tokens // N_HEAD
    load = pltpu.make_async_copy(w_ref, w_vmem, w_sem)
    load.start()
    me = lax.axis_index("head")
    starts = [pl.multiple_of(lax.rem(me + o, N_HEAD) * share, share) for o in offsets]
    rows = share * len(offsets)

    doc = doc_ref[...].astype(f32)
    doc_col[...] = jnp.broadcast_to(doc, (DH, tokens)).T
    mine = jnp.concatenate([doc_col[pl.ds(s, share), :] for s in starts], axis=0)
    inner = lax.broadcasted_iota(jnp.int32, (share, tokens), 0)
    when = jnp.concatenate([inner + s for s in starts], axis=0)
    position = lax.broadcasted_iota(jnp.int32, (rows, tokens), 1)
    wide = jnp.concatenate([mine, mine], axis=1)
    inside = ((position <= when) & (wide == doc)).astype(f32)
    prior = (mine == meta_ref[8:9, :]).astype(f32)
    counts = prior * meta_ref[0:1, :] + jnp.sum(inside, axis=1, keepdims=True)
    inverse = 1.0 / counts
    prior_inverse = prior * inverse
    inside_inverse = inside * jnp.concatenate([inverse, inverse], axis=1)
    ones = jnp.ones((8, DH), f32)

    for h in range(heads):
        cols = slice(h * DH, (h + 1) * DH)
        kt = kt_ref[cols, :]
        ktf = kt.astype(f32)
        mean = jnp.mean(ktf * ktf, axis=0, keepdims=True)
        scale = lax.rsqrt(mean + 1e-06) * (1.0 / math.sqrt(DH))
        weight[h] = inside_inverse * (scale * scale)
        state = state_ref[cols, :]
        right[h, :DH, :tokens] = kt
        right[h, DH:, :tokens] = kt
        right[h, :DH, tokens:] = state
        right[h, DH:, tokens:] = state
        q = jnp.concatenate([q_ref[pl.ds(s, share), cols] for s in starts], axis=0).astype(f32)
        q = q * scale_of(q)
        r_ref[h] = q
        p_ref[h] = q * (1.0 / center)
        x_ref[h] = q * (1.0 / center)

    factor = radius / center
    for _ in range(ITERS):
        factor_new = 1.0 / (2.0 * center / radius - factor)
        for h in range(heads):
            p = p_ref[h]
            both = dot(split(p), right[h])
            scores = (both[:, :tokens] * weight[h]).astype(bf16)
            moved = dot(scores, k_ref[:, h * DH : (h + 1) * DH])
            r = r_ref[h] - (moved + both[:, tokens:] * prior_inverse + ridge_lambda * p)
            p = (factor_new * factor) * p + (2.0 * factor_new / radius) * r
            r_ref[h] = r
            p_ref[h] = p
            x_ref[h] = x_ref[h] + p
        factor = factor_new

    ys = []
    for h in range(heads):
        cols = slice(h * DH, (h + 1) * DH)
        ktf = kt_ref[cols, :].astype(f32)
        mean = jnp.mean(ktf * ktf, axis=0, keepdims=True)
        scale = lax.rsqrt(mean + 1e-06) * (1.0 / math.sqrt(DH))
        state = state_ref[width + h * DH : width + (h + 1) * DH, :]
        right[h, :DH, tokens:] = state
        right[h, DH:, tokens:] = state
        both = dot(split(x_ref[h]), right[h])
        scores = (both[:, :tokens] * (inside * scale)).astype(bf16)
        o = dot(scores, v_ref[:, cols]) + both[:, tokens:] * prior
        o = o * lax.rsqrt(jnp.mean(o * o, axis=-1, keepdims=True) + 1e-06)
        ys.append(o.astype(bf16))
    y = jnp.concatenate(ys, axis=1)
    load.wait()
    model = w_vmem.shape[1]
    tile = 1024
    for c in range(0, model, tile):
        part = dot(y, w_vmem[:, c : c + tile]).astype(bf16)
        for out, (at, lo, hi) in zip(outs, pieces):
            if lo <= c < hi:
                out[:, c - lo : c - lo + tile] = part[at * share : (at + 1) * share]


def solve(offsets, pieces, q, k, v, doc, kt, state, meta, w):
    tokens, width = q.shape
    heads = width // DH
    share = tokens // N_HEAD
    rows = share * len(offsets)
    vmem = pl.BlockSpec(memory_space=pltpu.VMEM)
    return pl.pallas_call(
        functools.partial(solve_kernel, offsets, pieces),
        out_shape=[jax.ShapeDtypeStruct((share, hi - lo), bf16) for _, lo, hi in pieces],
        in_specs=[vmem] * 7 + [pl.BlockSpec(memory_space=pl.ANY)],
        out_specs=[vmem] * len(pieces),
        scratch_shapes=[
            pltpu.VMEM(w.shape, bf16),
            pltpu.VMEM((tokens, DH), f32),
            pltpu.VMEM((heads, 2 * DH, tokens + DH), bf16),
            pltpu.VMEM((heads, rows, tokens), f32),
            pltpu.VMEM((heads, rows, DH), f32),
            pltpu.VMEM((heads, rows, DH), f32),
            pltpu.VMEM((heads, rows, DH), f32),
            pltpu.SemaphoreType.DMA,
        ],
        compiler_params=pltpu.CompilerParams(vmem_limit_bytes=40 << 20),
        cost_estimate=pl.CostEstimate(
            flops=rows * 50_000_000, bytes_accessed=12_000_000, transcendentals=0
        ),
    )(q, k, v, doc, kt, state, meta, w)


def shards(queries, keys, values, doc_ids, w_out):
    tokens, width = queries.shape
    heads = width // DH
    model = w_out.shape[1]
    half = model // 2
    share = tokens // N_HEAD
    blocks = lax.axis_size("ctx")
    doc = doc_ids.reshape(1, tokens)
    vmem = pl.BlockSpec(memory_space=pltpu.VMEM)
    size = 2 * heads * DH // blocks
    with jax.named_scope("tails"):
        send, kt = pl.pallas_call(
            tails_kernel,
            out_shape=[
                jax.ShapeDtypeStruct((blocks, size + 16, DH), bf16),
                jax.ShapeDtypeStruct((width, tokens), bf16),
            ],
            in_specs=[vmem] * 3,
            out_specs=[vmem] * 2,
        )(keys, values, doc)
    with jax.named_scope("collect"):
        recv = lax.all_to_all(send, "ctx", 0, 0, tiled=True)
    with jax.named_scope("prefix"):
        back, meta = pl.pallas_call(
            prefix_kernel,
            out_shape=[
                jax.ShapeDtypeStruct((blocks, size, DH), bf16),
                jax.ShapeDtypeStruct((16, DH), f32),
            ],
            in_specs=[vmem],
            out_specs=[vmem] * 2,
        )(recv)
    with jax.named_scope("distribute"):
        state = lax.all_to_all(back, "ctx", 0, 0, tiled=True).reshape(2 * width, DH)

    def run(offsets):
        pieces = []
        for at in range(len(offsets)):
            pieces += [(at, 0, half), (at, half, model)]
        got = solve(
            offsets, tuple(pieces), queries, keys, values, doc, kt, state, meta, w_out
        )
        return {(o, c): got[2 * at + c] for at, o in enumerate(offsets) for c in range(2)}

    size_ring = lax.axis_size("head")

    def hop(x, step):
        return lax.ppermute(x, "head", [(i, (i + step) % size_ring) for i in range(size_ring)])

    with jax.named_scope("far_tokens"):
        part = run((4, 3, 5))
    with jax.named_scope("near_tokens"):
        part.update(run((2, 6, 1, 7, 0)))

    def add(a, b):
        return (a.astype(f32) + b.astype(f32)).astype(bf16)

    sums = []
    for step, first in ((1, 0), (-1, 1)):
        second = 1 - first
        with jax.named_scope("ring"):
            a = hop(part[4, first], step)
            b = hop(part[(3 * step) % 8, second], step)
            a = hop(add(a, part[(3 * step) % 8, first]), step)
            for distance in (2, 1):
                b = hop(add(b, part[(distance * step) % 8, second]), step)
                a = hop(add(a, part[(distance * step) % 8, first]), step)
        sums.append({first: a, second: b})
    columns = [
        (
            sums[0][c].astype(f32) + sums[1][c].astype(f32) + part[0, c].astype(f32)
        ).astype(bf16)
        for c in range(2)
    ]
    return jnp.concatenate(columns, axis=1)


def solution(mesh):
    return jax.shard_map(
        shards,
        mesh=mesh,
        in_specs=(P("ctx", "head"), P("ctx", "head"), P("ctx", "head"), P("ctx"), P("head", None)),
        out_specs=P(("ctx", "head"), None),
        check_vma=False,
    )
```

time: 228 us -> 113 us (0.50)
  matrix products: 51.8 us -> 0 us
  waiting for transfers between devices: 75.4 us -> 30.4 us
  blocking collectives: 67.7 us -> 30.5 us
  starting transfers between devices: 0.09 us -> 22.6 us
  Pallas kernels: 0 us -> 18.4 us
  between operations: 14 us -> 0.21 us
  other arithmetic: 6.32 us -> 1.66 us
    unnamed x1 -> x0, blocking collectives: 67.7 us -> none
    reduce_scatter x1 -> x0, waiting for transfers between devices: 54.3 us -> none  [shards(): lax.psum_scatter(jnp.dot(mixed_in, w_out, preferred_element_type=jnp.floa...]
    dot_general x38 -> x0, matrix products: 51.8 us -> none  [the longest x10 13.6 us: apply(): jnp.einsum('hcts,hcsd->hctd', scores(field), key_c, precision=highest)]
    all_to_all x0 -> x2, blocking collectives: none -> 30.5 us  [the longest x1 17.7 us: shards(): recv = lax.all_to_all(send, 'ctx', 0, 0, tiled=True)]
    ppermute x0 -> x14, waiting for transfers between devices: none -> 30.4 us  [hop(): lax.ppermute(x, 'head', [(i, (i + step) % size_ring) for i in range(size_...]
    ppermute x0 -> x14, starting transfers between devices: none -> 22.6 us  [hop(): lax.ppermute(x, 'head', [(i, (i + step) % size_ring) for i in range(size_...]
    all_gather x2 -> x0, waiting for transfers between devices: 21 us -> none  [the longest x1 20.9 us: shards(): lax.all_gather(tail_v[None].astype(jnp.bfloat16), 'ctx', axis=0, tiled=True)]
    pallas_call x0 -> x4, Pallas kernels: none -> 18.4 us  [the longest x2 14.3 us: solve(): pl.pallas_call(functools.partial(solve_kernel, offsets, pieces), out_shap...]
  transfers between devices with their start and end apart: 3 -> 14, of which waited for: 2 -> 4; matrix products, arithmetic and copies ran while one was open for 7% -> 1% of each run, Pallas kernels for 0% -> 7%
where the time goes in v1:
time: 113 us; the launch traced here: 112 us
  blocking collectives  30.5 us (27%)
  waiting for transfers between devices  30.4 us (27%)
  starting transfers between devices  22.6 us (20%)
  Pallas kernels  18.4 us (16%)
  local copies, waits for them, and re-layouts  8.56 us (8%)
  other arithmetic  1.66 us (1%)
    ppermute x14, waiting for transfers between devices, hop(): lax.ppermute(x, 'head', [(i, (i + step) % size_ring) for i in range(size_...  30.4 us
    ppermute x14, starting transfers between devices, hop(): lax.ppermute(x, 'head', [(i, (i + step) % size_ring) for i in range(size_...  22.6 us
    all_to_all x1, blocking collectives, shards(): recv = lax.all_to_all(send, 'ctx', 0, 0, tiled=True)  17.7 us
    pallas_call x2, Pallas kernels, solve(): pl.pallas_call(functools.partial(solve_kernel, offsets, pieces), out_shap...  14.3 us
    all_to_all x1, blocking collectives, shards(): state = lax.all_to_all(back, 'ctx', 0, 0, tiled=True).reshape(2 * width, DH)  12.8 us
    unnamed x16, local copies, waits for them, and re-layouts  8.56 us
    pallas_call x1, Pallas kernels, shards(): pl.pallas_call(tails_kernel, out_shape=[jax.ShapeDtypeStruct((blocks, siz...  2.32 us
  transfers between devices with their start and end apart: 14, of which 4 were waited for; matrix products, arithmetic and copies ran while one was open for 1% of the time, Pallas kernels for 7%

profile of v1, /device:TPU:96, one launch (start us, length us, event | category | flops | bytes accessed | tf_op | source)
XLA Modules:
  0.0 112.3 jit_solution(17235000246976851292)
XLA Ops:
  0.0 2.3 %tails.1 = (bf16[32,48,128]{2,1,0:T(8,128)(2,1)}, bf16[512,256]{1,0:T(8,128)(2,1)}) custom-call(bf16[256,512]{1,0:T(8,128)(2,1)} %k_ref.5, bf16[256,512]{1,0:T(8,128)(2,1)} %v_ref.5, s32[1,256]{1,0:T(1,128)} %bitcast.4), custom_call_target="tpu_custom_call" | custom-call | tf_op jit(solution)/shard_map/tails/pallas_call | solution.py:225
  2.3 17.7 %all_to_all.10.recv_ref = bf16[32,48,128]{2,1,0:T(8,128)(2,1)} all-to-all(bf16[32,48,128]{2,1,0:T(8,128)(2,1)} %get-tuple-element.26), channel_id=1, replica_groups=mesh['ctx'=32,'head'=8] {'ctx'}, dimensions={0} | all-to-all | bytes 786432 | tf_op jit(solution)/shard_map/collect/all_to_all | solution.py:235
  20.0 1.8 %prefix.1 = (bf16[32,32,128]{2,1,0:T(8,128)(2,1)}, f32[16,128]{1,0:T(8,128)}) custom-call(bf16[32,48,128]{2,1,0:T(8,128)(2,1)} %all_to_all.10.recv_ref), custom_call_target="tpu_custom_call" | custom-call | tf_op jit(solution)/shard_map/prefix/pallas_call | solution.py:237
  21.8 12.8 %all_to_all.11 = bf16[32,32,128]{2,1,0:T(8,128)(2,1)S(1)} all-to-all(bf16[32,32,128]{2,1,0:T(8,128)(2,1)} %get-tuple-element.27), channel_id=1, replica_groups=mesh['ctx'=32,'head'=8] {'ctx'}, dimensions={0} | all-to-all | bytes 524288 | tf_op jit(solution)/shard_map/distribute/all_to_all | solution.py:247
  34.6 0.0 copy-start
  34.6 0.9 copy-done
  35.6 0.0 copy-start.1
  35.6 0.9 copy-done.1
  36.5 0.0 copy-start.2
  36.5 0.7 copy-done.2
  37.2 0.0 copy-start.3
  37.2 3.4 %copy-done.3 = bf16[512,8192]{1,0:T(8,128)(2,1)S(1)} copy-done((bf16[512,8192]{1,0:T(8,128)(2,1)S(1)}, bf16[512,8192]{1,0:T(8,128)(2,1)}, u32[]{:S(2)}) %copy-start.3) | copy-done | bytes 8388632
  40.6 0.0 copy-start.5
  40.6 0.9 copy-done.5
  41.5 0.0 copy-start.6
  41.5 0.9 copy-done.6
  42.5 0.0 copy-start.7
  42.5 0.7 copy-done.7
  43.2 0.0 copy-start.4
  43.2 6.8 %far_tokens.1 = (bf16[32,4096]{1,0:T(8,128)(2,1)S(1)}, bf16[32,4096]{1,0:T(8,128)(2,1)S(1)}, bf16[32,4096]{1,0:T(8,128)(2,1)S(1)}, bf16[32,4096]{1,0:T(8,128)(2,...) custom-call(bf16[256,512]{1,0:T(8,128)(2,1)S(1)} %copy-done.5, bf16[256,512]{1,0:T(8,128)(2,1)S(1)} %copy-done, ...), custom_call_target="tpu_custom_call" | custom-call | flops 4800000000 | bytes 12000000 | tf_op jit(solution)/shard_map/far_tokens/pallas_call | solution.py:192
  50.0 3.4 %collective-permute-start = (bf16[32,4096]{1,0:T(8,128)(2,1)S(1)}, bf16[32,4096]{1,0:T(8,128)(2,1)S(1)}, u32[]{:S(2)}, u32[]{:S(2)}) collective-permute-start(bf16[32,4096]{1,0:T(8,128)(2,1)S(1)} %get-tuple-element.29), channel_id=1, source_target_pairs={{0,1},{1,2},{2,3},{3,4},{4,5},{5,6},{6,7},{7,0},{8,9},{9,10},{10,1... | collective-permute-start | bytes 786440 | tf_op jit(solution)/shard_map/ring/ppermute | solution.py:261
  53.4 0.0 copy-done.4
  53.4 7.5 %near_tokens.1 = (bf16[32,4096]{1,0:T(8,128)(2,1)S(1)}, bf16[32,4096]{1,0:T(8,128)(2,1)S(1)}, bf16[32,4096]{1,0:T(8,128)(2,1)S(1)}, bf16[32,4096]{1,0:T(8,128)(2...) custom-call(bf16[256,512]{1,0:T(8,128)(2,1)S(1)} %copy-done.5, ...), custom_call_target="tpu_custom_call" | custom-call | flops 8000000000 | bytes 12000000 | tf_op jit(solution)/shard_map/near_tokens/pallas_call | solution.py:192
  60.8 0.1 collective-permute-start.4
  60.9 3.2 %collective-permute-start.7 = (bf16[32,4096]{1,0:T(8,128)(2,1)S(1)}, bf16[32,4096]{1,0:T(8,128)(2,1)S(1)}, u32[]{:S(2)}, u32[]{:S(2)}) collective-permute-start(bf16[32,4096]{1,0:T(8,128)(2,1)S(1)} %get-tuple-element.37), channel_id=1, source_target_pairs={{0,1},{1,2},{2,3},{3,4},{4,5},{5,6},{6,7},{7,0},{8,9},{9,10},{10,1... | collective-permute-start | bytes 786440 | tf_op jit(solution)/shard_map/ring/ppermute | solution.py:261
  64.1 0.0 collective-permute-start.10
  64.2 0.0 collective-permute-done
  64.2 0.1 add_convert_fusion.11
  64.2 3.3 %collective-permute-start.1 = (bf16[32,4096]{1,0:T(8,128)(2,1)S(1)}, bf16[32,4096]{1,0:T(8,128)(2,1)S(1)}, u32[]{:S(2)}, u32[]{:S(2)}) collective-permute-start(bf16[32,4096]{1,0:T(8,128)(2,1)S(1)} %add_convert_fusion.11), channel_id=1, source_target_pairs={{0,1},{1,2},{2,3},{3,4},{4,5},{5,6},{6,7},{7,0},{8,9},{9,10},{10,1... | collective-permute-start | bytes 786440 | tf_op jit(solution)/shard_map/ring/ppermute | solution.py:261
  67.5 8.4 %collective-permute-done.10 = bf16[32,4096]{1,0:T(8,128)(2,1)S(1)} collective-permute-done((bf16[32,4096]{1,0:T(8,128)(2,1)S(1)}, bf16[32,4096]{1,0:T(8,128)(2,1)S(1)}, u32[]{:S(2)}, u32[]{:S(2)}) %collective-permute-start.10) | collective-permute-done | bytes 262176 | tf_op jit(solution)/shard_map/ring/ppermute | solution.py:261
  75.9 0.1 add_convert_fusion.3
  76.0 0.1 collective-permute-start.11
  76.1 0.0 collective-permute-done.4
  76.1 0.1 add_convert_fusion.8
  76.2 0.1 collective-permute-start.5
  76.3 0.0 collective-permute-done.7
  76.3 0.1 add_convert_fusion.5
  76.4 3.3 %collective-permute-start.8 = (bf16[32,4096]{1,0:T(8,128)(2,1)S(1)}, bf16[32,4096]{1,0:T(8,128)(2,1)S(1)}, u32[]{:S(2)}, u32[]{:S(2)}) collective-permute-start(bf16[32,4096]{1,0:T(8,128)(2,1)S(1)} %add_convert_fusion.5), channel_id=1, source_target_pairs={{0,1},{1,2},{2,3},{3,4},{4,5},{5,6},{6,7},{7,0},{8,9},{9,10},{10,1... | collective-permute-start | bytes 786440 | tf_op jit(solution)/shard_map/ring/ppermute | solution.py:261
  79.6 0.0 collective-permute-done.1
  79.6 0.1 add_convert_fusion.10
  79.7 2.3 %collective-permute-start.2 = (bf16[32,4096]{1,0:T(8,128)(2,1)S(1)}, bf16[32,4096]{1,0:T(8,128)(2,1)S(1)}, u32[]{:S(2)}, u32[]{:S(2)}) collective-permute-start(bf16[32,4096]{1,0:T(8,128)(2,1)S(1)} %add_convert_fusion.10), channel_id=1, source_target_pairs={{0,1},{1,2},{2,3},{3,4},{4,5},{5,6},{6,7},{7,0},{8,9},{9,10},{10,1... | collective-permute-start | bytes 786440 | tf_op jit(solution)/shard_map/ring/ppermute | solution.py:261
  82.0 8.2 %collective-permute-done.5 = bf16[32,4096]{1,0:T(8,128)(2,1)S(1)} collective-permute-done((bf16[32,4096]{1,0:T(8,128)(2,1)S(1)}, bf16[32,4096]{1,0:T(8,128)(2,1)S(1)}, u32[]{:S(2)}, u32[]{:S(2)}) %collective-permute-start.5) | collective-permute-done | bytes 262176 | tf_op jit(solution)/shard_map/ring/ppermute | solution.py:261
  90.3 0.1 add_convert_fusion.7
  90.3 0.1 collective-permute-start.6
  90.4 0.0 collective-permute-done.8
  90.4 0.1 add_convert_fusion.4
  90.5 3.3 %collective-permute-start.9 = (bf16[32,4096]{1,0:T(8,128)(2,1)S(1)}, bf16[32,4096]{1,0:T(8,128)(2,1)S(1)}, u32[]{:S(2)}, u32[]{:S(2)}) collective-permute-start(bf16[32,4096]{1,0:T(8,128)(2,1)S(1)} %add_convert_fusion.4), channel_id=1, source_target_pairs={{0,1},{1,2},{2,3},{3,4},{4,5},{5,6},{6,7},{7,0},{8,9},{9,10},{10,1... | collective-permute-start | bytes 786440 | tf_op jit(solution)/shard_map/ring/ppermute | solution.py:261
  93.8 0.0 collective-permute-done.11
  93.8 0.1 add_convert_fusion.2
  93.9 0.1 collective-permute-start.12
  93.9 0.0 collective-permute-done.2
  94.0 0.1 add_convert_fusion.9
  94.0 3.3 %collective-permute-start.3 = (bf16[32,4096]{1,0:T(8,128)(2,1)S(1)}, bf16[32,4096]{1,0:T(8,128)(2,1)S(1)}, u32[]{:S(2)}, u32[]{:S(2)}) collective-permute-start(bf16[32,4096]{1,0:T(8,128)(2,1)S(1)} %add_convert_fusion.9), channel_id=1, source_target_pairs={{0,1},{1,2},{2,3},{3,4},{4,5},{5,6},{6,7},{7,0},{8,9},{9,10},{10,1... | collective-permute-start | bytes 786440 | tf_op jit(solution)/shard_map/ring/ppermute | solution.py:261
  97.3 6.3 %collective-permute-done.12 = bf16[32,4096]{1,0:T(8,128)(2,1)S(1)} collective-permute-done((bf16[32,4096]{1,0:T(8,128)(2,1)S(1)}, bf16[32,4096]{1,0:T(8,128)(2,1)S(1)}, u32[]{:S(2)}, u32[]{:S(2)}) %collective-permute-start.12) | collective-permute-done | bytes 262176 | tf_op jit(solution)/shard_map/ring/ppermute | solution.py:261
  103.7 0.1 add_convert_fusion.1
  103.7 0.1 collective-permute-start.13
  103.8 0.0 collective-permute-done.6
  103.8 0.0 collective-permute-done.3
  103.8 0.1 add_convert_fusion.6
  103.9 0.0 collective-permute-done.9
  103.9 7.4 %collective-permute-done.13 = bf16[32,4096]{1,0:T(8,128)(2,1)S(1)} collective-permute-done((bf16[32,4096]{1,0:T(8,128)(2,1)S(1)}, bf16[32,4096]{1,0:T(8,128)(2,1)S(1)}, u32[]{:S(2)}, u32[]{:S(2)}) %collective-permute-start.13) | collective-permute-done | bytes 262176 | tf_op jit(solution)/shard_map/ring/ppermute | solution.py:261
  111.4 0.1 add_convert_fusion
  111.5 0.8 pad_maximum_fusion
Async XLA Ops:
  34.6 1.0 copy-start
  35.6 0.9 copy-start.1
  36.5 0.7 copy-start.2
  37.2 3.4 %copy-start.3 = (bf16[512,8192]{1,0:T(8,128)(2,1)S(1)}, bf16[512,8192]{1,0:T(8,128)(2,1)}, u32[]{:S(2)}) copy-start(bf16[512,8192]{1,0:T(8,128)(2,1)} %w_ref.3) | copy-start | bytes 25165828
  40.6 0.9 copy-start.5
  41.5 0.9 copy-start.6
  42.5 0.7 copy-start.7
  43.2 10.2 %copy-start.4 = (bf16[512,8192]{1,0:T(8,128)(2,1)S(1)}, bf16[512,8192]{1,0:T(8,128)(2,1)}, u32[]{:S(2)}) copy-start(bf16[512,8192]{1,0:T(8,128)(2,1)} %w_ref.3) | copy-start | bytes 25165828
  50.0 14.2 %collective-permute-start = (bf16[32,4096]{1,0:T(8,128)(2,1)S(1)}, bf16[32,4096]{1,0:T(8,128)(2,1)S(1)}, u32[]{:S(2)}, u32[]{:S(2)}) collective-permute-start(bf16[32,4096]{1,0:T(8,128)(2,1)S(1)} %get-tuple-element.29), channel_id=1, source_target_pairs={{0,1},{1,2},{2,3},{3,4},{4,5},{5,6},{6,7},{7,0},{8,9},{9,10},{10,1... | collective-permute-start | bytes 786440 | tf_op jit(solution)/shard_map/ring/ppermute | solution.py:261
  60.8 15.3 %collective-permute-start.4 = (bf16[32,4096]{1,0:T(8,128)(2,1)S(1)}, bf16[32,4096]{1,0:T(8,128)(2,1)S(1)}, u32[]{:S(2)}, u32[]{:S(2)}) collective-permute-start(bf16[32,4096]{1,0:T(8,128)(2,1)S(1)} %get-tuple-element.33), channel_id=1, source_target_pairs={{0,7},{1,0},{2,1},{3,2},{4,3},{5,4},{6,5},{7,6},{8,15},{9,8},{10,9... | collective-permute-start | bytes 786440 | tf_op jit(solution)/shard_map/ring/ppermute | solution.py:261
  60.9 15.3 %collective-permute-start.7 = (bf16[32,4096]{1,0:T(8,128)(2,1)S(1)}, bf16[32,4096]{1,0:T(8,128)(2,1)S(1)}, u32[]{:S(2)}, u32[]{:S(2)}) collective-permute-start(bf16[32,4096]{1,0:T(8,128)(2,1)S(1)} %get-tuple-element.37), channel_id=1, source_target_pairs={{0,1},{1,2},{2,3},{3,4},{4,5},{5,6},{6,7},{7,0},{8,9},{9,10},{10,1... | collective-permute-start | bytes 786440 | tf_op jit(solution)/shard_map/ring/ppermute | solution.py:261
  64.1 11.8 %collective-permute-start.10 = (bf16[32,4096]{1,0:T(8,128)(2,1)S(1)}, bf16[32,4096]{1,0:T(8,128)(2,1)S(1)}, u32[]{:S(2)}, u32[]{:S(2)}) collective-permute-start(bf16[32,4096]{1,0:T(8,128)(2,1)S(1)} %get-tuple-element.40), channel_id=1, source_target_pairs={{0,7},{1,0},{2,1},{3,2},{4,3},{5,4},{6,5},{7,6},{8,15},{9,8},{10,9... | collective-permute-start | bytes 786440 | tf_op jit(solution)/shard_map/ring/ppermute | solution.py:261
  64.2 15.4 %collective-permute-start.1 = (bf16[32,4096]{1,0:T(8,128)(2,1)S(1)}, bf16[32,4096]{1,0:T(8,128)(2,1)S(1)}, u32[]{:S(2)}, u32[]{:S(2)}) collective-permute-start(bf16[32,4096]{1,0:T(8,128)(2,1)S(1)} %add_convert_fusion.11), channel_id=1, source_target_pairs={{0,1},{1,2},{2,3},{3,4},{4,5},{5,6},{6,7},{7,0},{8,9},{9,10},{10,1... | collective-permute-start | bytes 786440 | tf_op jit(solution)/shard_map/ring/ppermute | solution.py:261
  76.0 17.8 %collective-permute-start.11 = (bf16[32,4096]{1,0:T(8,128)(2,1)S(1)}, bf16[32,4096]{1,0:T(8,128)(2,1)S(1)}, u32[]{:S(2)}, u32[]{:S(2)}) collective-permute-start(bf16[32,4096]{1,0:T(8,128)(2,1)S(1)} %add_convert_fusion.3), channel_id=1, source_target_pairs={{0,7},{1,0},{2,1},{3,2},{4,3},{5,4},{6,5},{7,6},{8,15},{9,8},{10,9... | collective-permute-start | bytes 786440 | tf_op jit(solution)/shard_map/ring/ppermute | solution.py:261
  76.2 14.1 %collective-permute-start.5 = (bf16[32,4096]{1,0:T(8,128)(2,1)S(1)}, bf16[32,4096]{1,0:T(8,128)(2,1)S(1)}, u32[]{:S(2)}, u32[]{:S(2)}) collective-permute-start(bf16[32,4096]{1,0:T(8,128)(2,1)S(1)} %add_convert_fusion.8), channel_id=1, source_target_pairs={{0,7},{1,0},{2,1},{3,2},{4,3},{5,4},{6,5},{7,6},{8,15},{9,8},{10,9... | collective-permute-start | bytes 786440 | tf_op jit(solution)/shard_map/ring/ppermute | solution.py:261
  76.4 14.1 %collective-permute-start.8 = (bf16[32,4096]{1,0:T(8,128)(2,1)S(1)}, bf16[32,4096]{1,0:T(8,128)(2,1)S(1)}, u32[]{:S(2)}, u32[]{:S(2)}) collective-permute-start(bf16[32,4096]{1,0:T(8,128)(2,1)S(1)} %add_convert_fusion.5), channel_id=1, source_target_pairs={{0,1},{1,2},{2,3},{3,4},{4,5},{5,6},{6,7},{7,0},{8,9},{9,10},{10,1... | collective-permute-start | bytes 786440 | tf_op jit(solution)/shard_map/ring/ppermute | solution.py:261
  79.7 14.2 %collective-permute-start.2 = (bf16[32,4096]{1,0:T(8,128)(2,1)S(1)}, bf16[32,4096]{1,0:T(8,128)(2,1)S(1)}, u32[]{:S(2)}, u32[]{:S(2)}) collective-permute-start(bf16[32,4096]{1,0:T(8,128)(2,1)S(1)} %add_convert_fusion.10), channel_id=1, source_target_pairs={{0,1},{1,2},{2,3},{3,4},{4,5},{5,6},{6,7},{7,0},{8,9},{9,10},{10,1... | collective-permute-start | bytes 786440 | tf_op jit(solution)/shard_map/ring/ppermute | solution.py:261
  90.3 13.5 %collective-permute-start.6 = (bf16[32,4096]{1,0:T(8,128)(2,1)S(1)}, bf16[32,4096]{1,0:T(8,128)(2,1)S(1)}, u32[]{:S(2)}, u32[]{:S(2)}) collective-permute-start(bf16[32,4096]{1,0:T(8,128)(2,1)S(1)} %add_convert_fusion.7), channel_id=1, source_target_pairs={{0,7},{1,0},{2,1},{3,2},{4,3},{5,4},{6,5},{7,6},{8,15},{9,8},{10,9... | collective-permute-start | bytes 786440 | tf_op jit(solution)/shard_map/ring/ppermute | solution.py:261
  90.5 13.4 %collective-permute-start.9 = (bf16[32,4096]{1,0:T(8,128)(2,1)S(1)}, bf16[32,4096]{1,0:T(8,128)(2,1)S(1)}, u32[]{:S(2)}, u32[]{:S(2)}) collective-permute-start(bf16[32,4096]{1,0:T(8,128)(2,1)S(1)} %add_convert_fusion.4), channel_id=1, source_target_pairs={{0,1},{1,2},{2,3},{3,4},{4,5},{5,6},{6,7},{7,0},{8,9},{9,10},{10,1... | collective-permute-start | bytes 786440 | tf_op jit(solution)/shard_map/ring/ppermute | solution.py:261
  93.9 9.8 %collective-permute-start.12 = (bf16[32,4096]{1,0:T(8,128)(2,1)S(1)}, bf16[32,4096]{1,0:T(8,128)(2,1)S(1)}, u32[]{:S(2)}, u32[]{:S(2)}) collective-permute-start(bf16[32,4096]{1,0:T(8,128)(2,1)S(1)} %add_convert_fusion.2), channel_id=1, source_target_pairs={{0,7},{1,0},{2,1},{3,2},{4,3},{5,4},{6,5},{7,6},{8,15},{9,8},{10,9... | collective-permute-start | bytes 786440 | tf_op jit(solution)/shard_map/ring/ppermute | solution.py:261
  94.0 9.8 %collective-permute-start.3 = (bf16[32,4096]{1,0:T(8,128)(2,1)S(1)}, bf16[32,4096]{1,0:T(8,128)(2,1)S(1)}, u32[]{:S(2)}, u32[]{:S(2)}) collective-permute-start(bf16[32,4096]{1,0:T(8,128)(2,1)S(1)} %add_convert_fusion.9), channel_id=1, source_target_pairs={{0,1},{1,2},{2,3},{3,4},{4,5},{5,6},{6,7},{7,0},{8,9},{9,10},{10,1... | collective-permute-start | bytes 786440 | tf_op jit(solution)/shard_map/ring/ppermute | solution.py:261
  103.7 7.7 %collective-permute-start.13 = (bf16[32,4096]{1,0:T(8,128)(2,1)S(1)}, bf16[32,4096]{1,0:T(8,128)(2,1)S(1)}, u32[]{:S(2)}, u32[]{:S(2)}) collective-permute-start(bf16[32,4096]{1,0:T(8,128)(2,1)S(1)} %add_convert_fusion.1), channel_id=1, source_target_pairs={{0,7},{1,0},{2,1},{3,2},{4,3},{5,4},{6,5},{7,6},{8,15},{9,8},{10,9... | collective-permute-start | bytes 786440 | tf_op jit(solution)/shard_map/ring/ppermute | solution.py:261

commit v2 on v1

--- a/solution.py
+++ b/solution.py
@@ -11,6 +11,10 @@
 DH = 128
 ITERS = 10
 N_HEAD = 8
+STREAMS = ((1, 0, "a"), (-1, 1, "a"), (-1, 0, "b"), (1, 1, "b"))
+LIMIT = 50
+FAR = (4, 3, 5, 2, 6, 1, 7, 0)
+NEAR = ()
 
 ridge_lambda = 0.02
 upper_end = 1.0 + ridge_lambda
@@ -86,26 +90,19 @@
     meta_ref[8:] = mine_last
 
 
-def solve_kernel(
-    offsets,
-    pieces,
-    q_ref,
-    k_ref,
-    v_ref,
-    doc_ref,
-    kt_ref,
-    state_ref,
-    meta_ref,
-    w_ref,
-    *rest,
-):
-    outs = rest[: len(pieces)]
-    w_vmem, doc_col, right, weight, p_ref, r_ref, x_ref, w_sem = rest[len(pieces) :]
+def solve_kernel(offsets, pieces, *refs):
+    hbm, refs = refs[:8], refs[8:]
+    outs, refs = refs[: len(pieces)], refs[len(pieces) :]
+    held, (doc_col, right, weight, p_ref, r_ref, x_ref, sems) = refs[:8], refs[8:]
+    loads = [pltpu.make_async_copy(a, b, sems.at[i]) for i, (a, b) in enumerate(zip(hbm, held))]
+    for load in loads:
+        load.start()
+    q_ref, k_ref, v_ref, doc_ref, kt_ref, state_ref, meta_ref, w_vmem = held
     tokens, width = q_ref.shape
     heads = width // DH
     share = tokens // N_HEAD
-    load = pltpu.make_async_copy(w_ref, w_vmem, w_sem)
-    load.start()
+    for load in loads[:-1]:
+        load.wait()
     me = lax.axis_index("head")
     starts = [pl.multiple_of(lax.rem(me + o, N_HEAD) * share, share) for o in offsets]
     rows = share * len(offsets)
@@ -173,7 +170,7 @@
         o = o * lax.rsqrt(jnp.mean(o * o, axis=-1, keepdims=True) + 1e-06)
         ys.append(o.astype(bf16))
     y = jnp.concatenate(ys, axis=1)
-    load.wait()
+    loads[-1].wait()
     model = w_vmem.shape[1]
     tile = 1024
     for c in range(0, model, tile):
@@ -189,26 +186,27 @@
     share = tokens // N_HEAD
     rows = share * len(offsets)
     vmem = pl.BlockSpec(memory_space=pltpu.VMEM)
+    args = (q, k, v, doc, kt, state, meta, w)
     return pl.pallas_call(
         functools.partial(solve_kernel, offsets, pieces),
         out_shape=[jax.ShapeDtypeStruct((share, hi - lo), bf16) for _, lo, hi in pieces],
-        in_specs=[vmem] * 7 + [pl.BlockSpec(memory_space=pl.ANY)],
+        in_specs=[pl.BlockSpec(memory_space=pltpu.HBM)] * len(args),
         out_specs=[vmem] * len(pieces),
         scratch_shapes=[
-            pltpu.VMEM(w.shape, bf16),
+            *[pltpu.VMEM(a.shape, a.dtype) for a in args],
             pltpu.VMEM((tokens, DH), f32),
             pltpu.VMEM((heads, 2 * DH, tokens + DH), bf16),
             pltpu.VMEM((heads, rows, tokens), f32),
             pltpu.VMEM((heads, rows, DH), f32),
             pltpu.VMEM((heads, rows, DH), f32),
             pltpu.VMEM((heads, rows, DH), f32),
-            pltpu.SemaphoreType.DMA,
+            pltpu.SemaphoreType.DMA((len(args),)),
         ],
-        compiler_params=pltpu.CompilerParams(vmem_limit_bytes=40 << 20),
+        compiler_params=pltpu.CompilerParams(vmem_limit_bytes=LIMIT << 20),
         cost_estimate=pl.CostEstimate(
             flops=rows * 50_000_000, bytes_accessed=12_000_000, transcendentals=0
         ),
-    )(q, k, v, doc, kt, state, meta, w)
+    )(*args)
 
 
 def shards(queries, keys, values, doc_ids, w_out):
@@ -246,7 +244,7 @@
     with jax.named_scope("distribute"):
         state = lax.all_to_all(back, "ctx", 0, 0, tiled=True).reshape(2 * width, DH)
 
-    def run(offsets):
+    def run(offsets, meta):
         pieces = []
         for at in range(len(offsets)):
             pieces += [(at, 0, half), (at, half, model)]
@@ -260,25 +258,32 @@
     def hop(x, step):
         return lax.ppermute(x, "head", [(i, (i + step) % size_ring) for i in range(size_ring)])
 
+    latest = None
+
+    def add(a, b):
+        nonlocal latest
+        if latest is not None:
+            b, _ = lax.optimization_barrier((b, latest))
+        latest = (a.astype(f32) + b.astype(f32)).astype(bf16)
+        return latest
+
     with jax.named_scope("far_tokens"):
-        part = run((4, 3, 5))
-    with jax.named_scope("near_tokens"):
-        part.update(run((2, 6, 1, 7, 0)))
-
-    def add(a, b):
-        return (a.astype(f32) + b.astype(f32)).astype(bf16)
-
-    sums = []
-    for step, first in ((1, 0), (-1, 1)):
-        second = 1 - first
-        with jax.named_scope("ring"):
-            a = hop(part[4, first], step)
-            b = hop(part[(3 * step) % 8, second], step)
-            a = hop(add(a, part[(3 * step) % 8, first]), step)
-            for distance in (2, 1):
-                b = hop(add(b, part[(distance * step) % 8, second]), step)
-                a = hop(add(a, part[(distance * step) % 8, first]), step)
-        sums.append({first: a, second: b})
+        part = run(FAR, meta)
+    moving = {}
+    with jax.named_scope("ring"):
+        for step, c, kind in STREAMS:
+            first = 4 if kind == "a" else (3 * step) % N_HEAD
+            moving[step, c] = hop(part[first, c], step)
+        for turn in range(3):
+            for step, c, kind in STREAMS:
+                distance = 3 - turn if kind == "a" else 2 - turn
+                if distance > 0:
+                    latest = None
+                    total = add(moving[step, c], part[(distance * step) % N_HEAD, c])
+                    moving[step, c] = hop(total, step)
+    order = ((1, 0), (-1, 1), (1, 1), (-1, 0))
+    moving = dict(zip(order, lax.optimization_barrier(tuple(moving[o] for o in order))))
+    sums = [{c: moving[step, c] for c in range(2)} for step in (1, -1)]
     columns = [
         (
             sums[0][c].astype(f32) + sums[1][c].astype(f32) + part[0, c].astype(f32)

time: 113 us -> 97 us (0.86)
  waiting for transfers between devices: 30.4 us -> 19.9 us
  local copies, waits for them, and re-layouts: 8.56 us -> 1.38 us
  Pallas kernels: 18.4 us -> 14.9 us
  starting transfers between devices: 22.6 us -> 25.7 us
    ppermute x14, waiting for transfers between devices: 30.4 us -> 19.9 us  [hop(): lax.ppermute(x, 'head', [(i, (i + step) % size_ring) for i in range(size_...]
    unnamed x16 -> x4, local copies, waits for them, and re-layouts: 8.56 us -> 1.38 us
    pallas_call x2 -> x1, Pallas kernels: 14.3 us -> 10.7 us  [solve(): pl.pallas_call(functools.partial(solve_kernel, offsets, pieces), out_shap...]
    ppermute x14, starting transfers between devices: 22.6 us -> 25.7 us  [hop(): lax.ppermute(x, 'head', [(i, (i + step) % size_ring) for i in range(size_...]
  transfers between devices with their start and end apart: 14 -> 14, of which waited for: 4 -> 9; matrix products, arithmetic and copies ran while one was open for 1% -> 1% of each run, Pallas kernels for 7% -> 0%
where the time goes in v2:
time: 97 us; the launch traced here: 95.7 us
  blocking collectives  31.2 us (32%)
  starting transfers between devices  25.7 us (26%)
  waiting for transfers between devices  19.9 us (21%)
  Pallas kernels  14.9 us (15%)
  other arithmetic  2.6 us (3%)
  local copies, waits for them, and re-layouts  1.38 us (1%)
    ppermute x14, starting transfers between devices, hop(): lax.ppermute(x, 'head', [(i, (i + step) % size_ring) for i in range(size_...  25.7 us
    ppermute x14, waiting for transfers between devices, hop(): lax.ppermute(x, 'head', [(i, (i + step) % size_ring) for i in range(size_...  19.9 us
    all_to_all x1, blocking collectives, shards(): recv = lax.all_to_all(send, 'ctx', 0, 0, tiled=True)  17.7 us
    all_to_all x1, blocking collectives, shards(): state = lax.all_to_all(back, 'ctx', 0, 0, tiled=True).reshape(2 * width, DH)  13.5 us
    pallas_call x1, Pallas kernels, solve(): pl.pallas_call(functools.partial(solve_kernel, offsets, pieces), out_shap...  10.7 us
    pallas_call x1, Pallas kernels, shards(): pl.pallas_call(tails_kernel, out_shape=[jax.ShapeDtypeStruct((blocks, siz...  2.32 us
  transfers between devices with their start and end apart: 14, of which 9 were waited for; matrix products, arithmetic and copies ran while one was open for 1% of the time, Pallas kernels for 0%

profile of v2, /device:TPU:96, one launch (start us, length us, event | category | flops | bytes accessed | tf_op | source)
XLA Modules:
  0.0 95.7 jit_solution(17285695492351038931)
XLA Ops:
  0.0 2.3 %tails.1 = (bf16[32,48,128]{2,1,0:T(8,128)(2,1)}, bf16[512,256]{1,0:T(8,128)(2,1)}) custom-call(bf16[256,512]{1,0:T(8,128)(2,1)} %refs_1_.1, bf16[256,512]{1,0:T(8,128)(2,1)} %refs_2_.1, s32[1,256]{1,0:T(1,128)} %bitcast.2), custom_call_target="tpu_custom_call" | custom-call | tf_op jit(solution)/shard_map/tails/pallas_call | solution.py:223
  2.3 17.7 %all_to_all.10.recv_ref = bf16[32,48,128]{2,1,0:T(8,128)(2,1)} all-to-all(bf16[32,48,128]{2,1,0:T(8,128)(2,1)} %get-tuple-element.30), channel_id=1, replica_groups=mesh['ctx'=32,'head'=8] {'ctx'}, dimensions={0} | all-to-all | bytes 786432 | tf_op jit(solution)/shard_map/collect/all_to_all | solution.py:233
  20.0 1.8 %prefix.1 = (bf16[32,32,128]{2,1,0:T(8,128)(2,1)}, f32[16,128]{1,0:T(8,128)}) custom-call(bf16[32,48,128]{2,1,0:T(8,128)(2,1)} %all_to_all.10.recv_ref), custom_call_target="tpu_custom_call" | custom-call | tf_op jit(solution)/shard_map/prefix/pallas_call | solution.py:235
  21.8 13.5 %all_to_all.11 = bf16[32,32,128]{2,1,0:T(8,128)(2,1)} all-to-all(bf16[32,32,128]{2,1,0:T(8,128)(2,1)} %get-tuple-element.31), channel_id=1, replica_groups=mesh['ctx'=32,'head'=8] {'ctx'}, dimensions={0} | all-to-all | bytes 524288 | tf_op jit(solution)/shard_map/distribute/all_to_all | solution.py:245
  35.3 0.0 copy-start
  35.3 0.7 copy-done
  36.0 0.0 copy-start.1
  36.0 0.7 copy-done.1
  36.7 10.7 %far_tokens.1 = (bf16[32,4096]{1,0:T(8,128)(2,1)S(1)}, bf16[32,4096]{1,0:T(8,128)(2,1)S(1)}, bf16[32,4096]{1,0:T(8,128)(2,1)S(1)}, bf16[32,4096]{1,0:T(8,128)(2,...) custom-call(bf16[256,512]{1,0:T(8,128)(2,1)} %refs_0_.1, ...), custom_call_target="tpu_custom_call" | custom-call | flops 12800000000 | bytes 12000000 | tf_op jit(solution)/shard_map/far_tokens/pallas_call | solution.py:190
  47.4 3.2 %collective-permute-start = (bf16[32,4096]{1,0:T(8,128)(2,1)S(1)}, bf16[32,4096]{1,0:T(8,128)(2,1)S(1)}, u32[]{:S(2)}, u32[]{:S(2)}) collective-permute-start(bf16[32,4096]{1,0:T(8,128)(2,1)S(1)} %get-tuple-element.33), channel_id=1, source_target_pairs={{0,1},{1,2},{2,3},{3,4},{4,5},{5,6},{6,7},{7,0},{8,9},{9,10},{10,1... | collective-permute-start | bytes 786440 | tf_op jit(solution)/shard_map/ring/ppermute | solution.py:259
  50.6 0.0 collective-permute-start.4
  50.6 3.2 %collective-permute-start.8 = (bf16[32,4096]{1,0:T(8,128)(2,1)S(1)}, bf16[32,4096]{1,0:T(8,128)(2,1)S(1)}, u32[]{:S(2)}, u32[]{:S(2)}) collective-permute-start(bf16[32,4096]{1,0:T(8,128)(2,1)S(1)} %get-tuple-element.41), channel_id=1, source_target_pairs={{0,1},{1,2},{2,3},{3,4},{4,5},{5,6},{6,7},{7,0},{8,9},{9,10},{10,1... | collective-permute-start | bytes 786440 | tf_op jit(solution)/shard_map/ring/ppermute | solution.py:259
  53.9 0.0 collective-permute-start.11
  53.9 3.4 %collective-permute-done = bf16[32,4096]{1,0:T(8,128)(2,1)S(1)} collective-permute-done((bf16[32,4096]{1,0:T(8,128)(2,1)S(1)}, bf16[32,4096]{1,0:T(8,128)(2,1)S(1)}, u32[]{:S(2)}, u32[]{:S(2)}) %collective-permute-start) | collective-permute-done | bytes 262176 | tf_op jit(solution)/shard_map/ring/ppermute | solution.py:259
  57.3 0.1 add_convert_fusion.11
  57.4 3.8 %collective-permute-start.1 = (bf16[32,4096]{1,0:T(8,128)(2,1)S(1)}, bf16[32,4096]{1,0:T(8,128)(2,1)S(1)}, u32[]{:S(2)}, u32[]{:S(2)}) collective-permute-start(bf16[32,4096]{1,0:T(8,128)(2,1)S(1)} %add_convert_fusion.11), channel_id=1, source_target_pairs={{0,1},{1,2},{2,3},{3,4},{4,5},{5,6},{6,7},{7,0},{8,9},{9,10},{10,1... | collective-permute-start | bytes 786440 | tf_op jit(solution)/shard_map/ring/ppermute | solution.py:259
  61.1 0.0 collective-permute-done.4
  61.1 0.1 add_convert_fusion.8
  61.2 0.1 collective-permute-start.5
  61.3 1.6 %collective-permute-done.8 = bf16[32,4096]{1,0:T(8,128)(2,1)S(1)} collective-permute-done((bf16[32,4096]{1,0:T(8,128)(2,1)S(1)}, bf16[32,4096]{1,0:T(8,128)(2,1)S(1)}, u32[]{:S(2)}, u32[]{:S(2)}) %collective-permute-start.8) | collective-permute-done | bytes 262176 | tf_op jit(solution)/shard_map/ring/ppermute | solution.py:259
  62.9 0.1 add_convert_fusion.5
  63.0 3.8 %collective-permute-start.9 = (bf16[32,4096]{1,0:T(8,128)(2,1)S(1)}, bf16[32,4096]{1,0:T(8,128)(2,1)S(1)}, u32[]{:S(2)}, u32[]{:S(2)}) collective-permute-start(bf16[32,4096]{1,0:T(8,128)(2,1)S(1)} %add_convert_fusion.5), channel_id=1, source_target_pairs={{0,1},{1,2},{2,3},{3,4},{4,5},{5,6},{6,7},{7,0},{8,9},{9,10},{10,1... | collective-permute-start | bytes 786440 | tf_op jit(solution)/shard_map/ring/ppermute | solution.py:259
  66.7 0.0 collective-permute-done.11
  66.7 0.1 add_convert_fusion.3
  66.8 0.1 collective-permute-start.12
  66.9 1.6 %collective-permute-done.1 = bf16[32,4096]{1,0:T(8,128)(2,1)S(1)} collective-permute-done((bf16[32,4096]{1,0:T(8,128)(2,1)S(1)}, bf16[32,4096]{1,0:T(8,128)(2,1)S(1)}, u32[]{:S(2)}, u32[]{:S(2)}) %collective-permute-start.1) | collective-permute-done | bytes 262176 | tf_op jit(solution)/shard_map/ring/ppermute | solution.py:259
  68.5 0.1 add_convert_fusion.10
  68.6 3.8 %collective-permute-start.2 = (bf16[32,4096]{1,0:T(8,128)(2,1)S(1)}, bf16[32,4096]{1,0:T(8,128)(2,1)S(1)}, u32[]{:S(2)}, u32[]{:S(2)}) collective-permute-start(bf16[32,4096]{1,0:T(8,128)(2,1)S(1)} %add_convert_fusion.10), channel_id=1, source_target_pairs={{0,1},{1,2},{2,3},{3,4},{4,5},{5,6},{6,7},{7,0},{8,9},{9,10},{10,1... | collective-permute-start | bytes 786440 | tf_op jit(solution)/shard_map/ring/ppermute | solution.py:259
  72.4 0.0 collective-permute-done.5
  72.4 0.1 add_convert_fusion.7
  72.4 0.1 collective-permute-start.6
  72.5 1.6 %collective-permute-done.9 = bf16[32,4096]{1,0:T(8,128)(2,1)S(1)} collective-permute-done((bf16[32,4096]{1,0:T(8,128)(2,1)S(1)}, bf16[32,4096]{1,0:T(8,128)(2,1)S(1)}, u32[]{:S(2)}, u32[]{:S(2)}) %collective-permute-start.9) | collective-permute-done | bytes 262176 | tf_op jit(solution)/shard_map/ring/ppermute | solution.py:259
  74.1 0.1 add_convert_fusion.4
  74.2 3.8 %collective-permute-start.10 = (bf16[32,4096]{1,0:T(8,128)(2,1)S(1)}, bf16[32,4096]{1,0:T(8,128)(2,1)S(1)}, u32[]{:S(2)}, u32[]{:S(2)}) collective-permute-start(bf16[32,4096]{1,0:T(8,128)(2,1)S(1)} %add_convert_fusion.4), channel_id=1, source_target_pairs={{0,1},{1,2},{2,3},{3,4},{4,5},{5,6},{6,7},{7,0},{8,9},{9,10},{10,1... | collective-permute-start | bytes 786440 | tf_op jit(solution)/shard_map/ring/ppermute | solution.py:259
  78.0 0.0 collective-permute-done.12
  78.0 0.1 add_convert_fusion.2
  78.1 0.1 collective-permute-start.13
  78.1 1.6 %collective-permute-done.2 = bf16[32,4096]{1,0:T(8,128)(2,1)S(1)} collective-permute-done((bf16[32,4096]{1,0:T(8,128)(2,1)S(1)}, bf16[32,4096]{1,0:T(8,128)(2,1)S(1)}, u32[]{:S(2)}, u32[]{:S(2)}) %collective-permute-start.2) | collective-permute-done | bytes 262176 | tf_op jit(solution)/shard_map/ring/ppermute | solution.py:259
  79.8 0.1 add_convert_fusion.9
  79.8 3.8 %collective-permute-start.3 = (bf16[32,4096]{1,0:T(8,128)(2,1)S(1)}, bf16[32,4096]{1,0:T(8,128)(2,1)S(1)}, u32[]{:S(2)}, u32[]{:S(2)}) collective-permute-start(bf16[32,4096]{1,0:T(8,128)(2,1)S(1)} %add_convert_fusion.9), channel_id=1, source_target_pairs={{0,1},{1,2},{2,3},{3,4},{4,5},{5,6},{6,7},{7,0},{8,9},{9,10},{10,1... | collective-permute-start | bytes 786440 | tf_op jit(solution)/shard_map/ring/ppermute | solution.py:259
  83.6 0.0 collective-permute-done.6
  83.6 0.1 add_convert_fusion.6
  83.7 0.1 collective-permute-start.7
  83.8 1.6 %collective-permute-done.10 = bf16[32,4096]{1,0:T(8,128)(2,1)S(1)} collective-permute-done((bf16[32,4096]{1,0:T(8,128)(2,1)S(1)}, bf16[32,4096]{1,0:T(8,128)(2,1)S(1)}, u32[]{:S(2)}, u32[]{:S(2)}) %collective-permute-start.10) | collective-permute-done | bytes 262176 | tf_op jit(solution)/shard_map/ring/ppermute | solution.py:259
  85.4 3.7 %collective-permute-done.13 = bf16[32,4096]{1,0:T(8,128)(2,1)S(1)} collective-permute-done((bf16[32,4096]{1,0:T(8,128)(2,1)S(1)}, bf16[32,4096]{1,0:T(8,128)(2,1)S(1)}, u32[]{:S(2)}, u32[]{:S(2)}) %collective-permute-start.13) | collective-permute-done | bytes 262176 | tf_op jit(solution)/shard_map/ring/ppermute | solution.py:259
  89.1 1.2 %collective-permute-done.3 = bf16[32,4096]{1,0:T(8,128)(2,1)S(1)} collective-permute-done((bf16[32,4096]{1,0:T(8,128)(2,1)S(1)}, bf16[32,4096]{1,0:T(8,128)(2,1)S(1)}, u32[]{:S(2)}, u32[]{:S(2)}) %collective-permute-start.3) | collective-permute-done | bytes 262176 | tf_op jit(solution)/shard_map/ring/ppermute | solution.py:259
  90.3 3.4 %collective-permute-done.7 = bf16[32,4096]{1,0:T(8,128)(2,1)S(1)} collective-permute-done((bf16[32,4096]{1,0:T(8,128)(2,1)S(1)}, bf16[32,4096]{1,0:T(8,128)(2,1)S(1)}, u32[]{:S(2)}, u32[]{:S(2)}) %collective-permute-start.7) | collective-permute-done | bytes 262176 | tf_op jit(solution)/shard_map/ring/ppermute | solution.py:259
  93.8 1.1 %add_convert_fusion = (bf16[32,4096]{1,0:T(8,128)(2,1)S(1)}, bf16[32,4096]{1,0:T(8,128)(2,1)S(1)}) fusion(bf16[32,4096]{1,0:T(8,128)(2,1)} %get-tuple-element.52, bf16[32,4096]{1,0:T(8,128)(2,1)S(1)} %collective-permute-done.7, bf16[32,4096]{1,0:T(8,128)(2,1)S(1)} %collective-permute-done.10, bf16[32,4096]{1,0:T(8,128)(2,1)S(1)} %get-tuple-element.49, ...), kind=kLoop, calls=%fused_computation.1 | loop fusion | flops 1572864 | bytes 2097152 | tf_op jit(solution)/shard_map/convert_element_type | solution.py:290
  94.9 0.8 pad_maximum_fusion
Async XLA Ops:
  35.3 0.7 copy-start
  36.0 0.7 copy-start.1
  47.4 9.9 %collective-permute-start = (bf16[32,4096]{1,0:T(8,128)(2,1)S(1)}, bf16[32,4096]{1,0:T(8,128)(2,1)S(1)}, u32[]{:S(2)}, u32[]{:S(2)}) collective-permute-start(bf16[32,4096]{1,0:T(8,128)(2,1)S(1)} %get-tuple-element.33), channel_id=1, source_target_pairs={{0,1},{1,2},{2,3},{3,4},{4,5},{5,6},{6,7},{7,0},{8,9},{9,10},{10,1... | collective-permute-start | bytes 786440 | tf_op jit(solution)/shard_map/ring/ppermute | solution.py:259
  50.6 10.5 %collective-permute-start.4 = (bf16[32,4096]{1,0:T(8,128)(2,1)S(1)}, bf16[32,4096]{1,0:T(8,128)(2,1)S(1)}, u32[]{:S(2)}, u32[]{:S(2)}) collective-permute-start(bf16[32,4096]{1,0:T(8,128)(2,1)S(1)} %get-tuple-element.37), channel_id=1, source_target_pairs={{0,7},{1,0},{2,1},{3,2},{4,3},{5,4},{6,5},{7,6},{8,15},{9,8},{10,9... | collective-permute-start | bytes 786440 | tf_op jit(solution)/shard_map/ring/ppermute | solution.py:259
  50.6 12.3 %collective-permute-start.8 = (bf16[32,4096]{1,0:T(8,128)(2,1)S(1)}, bf16[32,4096]{1,0:T(8,128)(2,1)S(1)}, u32[]{:S(2)}, u32[]{:S(2)}) collective-permute-start(bf16[32,4096]{1,0:T(8,128)(2,1)S(1)} %get-tuple-element.41), channel_id=1, source_target_pairs={{0,1},{1,2},{2,3},{3,4},{4,5},{5,6},{6,7},{7,0},{8,9},{9,10},{10,1... | collective-permute-start | bytes 786440 | tf_op jit(solution)/shard_map/ring/ppermute | solution.py:259
  53.9 12.9 %collective-permute-start.11 = (bf16[32,4096]{1,0:T(8,128)(2,1)S(1)}, bf16[32,4096]{1,0:T(8,128)(2,1)S(1)}, u32[]{:S(2)}, u32[]{:S(2)}) collective-permute-start(bf16[32,4096]{1,0:T(8,128)(2,1)S(1)} %get-tuple-element.44), channel_id=1, source_target_pairs={{0,7},{1,0},{2,1},{3,2},{4,3},{5,4},{6,5},{7,6},{8,15},{9,8},{10,9... | collective-permute-start | bytes 786440 | tf_op jit(solution)/shard_map/ring/ppermute | solution.py:259
  57.4 11.2 %collective-permute-start.1 = (bf16[32,4096]{1,0:T(8,128)(2,1)S(1)}, bf16[32,4096]{1,0:T(8,128)(2,1)S(1)}, u32[]{:S(2)}, u32[]{:S(2)}) collective-permute-start(bf16[32,4096]{1,0:T(8,128)(2,1)S(1)} %add_convert_fusion.11), channel_id=1, source_target_pairs={{0,1},{1,2},{2,3},{3,4},{4,5},{5,6},{6,7},{7,0},{8,9},{9,10},{10,1... | collective-permute-start | bytes 786440 | tf_op jit(solution)/shard_map/ring/ppermute | solution.py:259
  61.2 11.2 %collective-permute-start.5 = (bf16[32,4096]{1,0:T(8,128)(2,1)S(1)}, bf16[32,4096]{1,0:T(8,128)(2,1)S(1)}, u32[]{:S(2)}, u32[]{:S(2)}) collective-permute-start(bf16[32,4096]{1,0:T(8,128)(2,1)S(1)} %add_convert_fusion.8), channel_id=1, source_target_pairs={{0,7},{1,0},{2,1},{3,2},{4,3},{5,4},{6,5},{7,6},{8,15},{9,8},{10,9... | collective-permute-start | bytes 786440 | tf_op jit(solution)/shard_map/ring/ppermute | solution.py:259
  63.0 11.2 %collective-permute-start.9 = (bf16[32,4096]{1,0:T(8,128)(2,1)S(1)}, bf16[32,4096]{1,0:T(8,128)(2,1)S(1)}, u32[]{:S(2)}, u32[]{:S(2)}) collective-permute-start(bf16[32,4096]{1,0:T(8,128)(2,1)S(1)} %add_convert_fusion.5), channel_id=1, source_target_pairs={{0,1},{1,2},{2,3},{3,4},{4,5},{5,6},{6,7},{7,0},{8,9},{9,10},{10,1... | collective-permute-start | bytes 786440 | tf_op jit(solution)/shard_map/ring/ppermute | solution.py:259
  66.8 11.2 %collective-permute-start.12 = (bf16[32,4096]{1,0:T(8,128)(2,1)S(1)}, bf16[32,4096]{1,0:T(8,128)(2,1)S(1)}, u32[]{:S(2)}, u32[]{:S(2)}) collective-permute-start(bf16[32,4096]{1,0:T(8,128)(2,1)S(1)} %add_convert_fusion.3), channel_id=1, source_target_pairs={{0,7},{1,0},{2,1},{3,2},{4,3},{5,4},{6,5},{7,6},{8,15},{9,8},{10,9... | collective-permute-start | bytes 786440 | tf_op jit(solution)/shard_map/ring/ppermute | solution.py:259
  68.6 11.2 %collective-permute-start.2 = (bf16[32,4096]{1,0:T(8,128)(2,1)S(1)}, bf16[32,4096]{1,0:T(8,128)(2,1)S(1)}, u32[]{:S(2)}, u32[]{:S(2)}) collective-permute-start(bf16[32,4096]{1,0:T(8,128)(2,1)S(1)} %add_convert_fusion.10), channel_id=1, source_target_pairs={{0,1},{1,2},{2,3},{3,4},{4,5},{5,6},{6,7},{7,0},{8,9},{9,10},{10,1... | collective-permute-start | bytes 786440 | tf_op jit(solution)/shard_map/ring/ppermute | solution.py:259
  72.4 11.2 %collective-permute-start.6 = (bf16[32,4096]{1,0:T(8,128)(2,1)S(1)}, bf16[32,4096]{1,0:T(8,128)(2,1)S(1)}, u32[]{:S(2)}, u32[]{:S(2)}) collective-permute-start(bf16[32,4096]{1,0:T(8,128)(2,1)S(1)} %add_convert_fusion.7), channel_id=1, source_target_pairs={{0,7},{1,0},{2,1},{3,2},{4,3},{5,4},{6,5},{7,6},{8,15},{9,8},{10,9... | collective-permute-start | bytes 786440 | tf_op jit(solution)/shard_map/ring/ppermute | solution.py:259
  74.2 11.2 %collective-permute-start.10 = (bf16[32,4096]{1,0:T(8,128)(2,1)S(1)}, bf16[32,4096]{1,0:T(8,128)(2,1)S(1)}, u32[]{:S(2)}, u32[]{:S(2)}) collective-permute-start(bf16[32,4096]{1,0:T(8,128)(2,1)S(1)} %add_convert_fusion.4), channel_id=1, source_target_pairs={{0,1},{1,2},{2,3},{3,4},{4,5},{5,6},{6,7},{7,0},{8,9},{9,10},{10,1... | collective-permute-start | bytes 786440 | tf_op jit(solution)/shard_map/ring/ppermute | solution.py:259
  78.1 11.1 %collective-permute-start.13 = (bf16[32,4096]{1,0:T(8,128)(2,1)S(1)}, bf16[32,4096]{1,0:T(8,128)(2,1)S(1)}, u32[]{:S(2)}, u32[]{:S(2)}) collective-permute-start(bf16[32,4096]{1,0:T(8,128)(2,1)S(1)} %add_convert_fusion.2), channel_id=1, source_target_pairs={{0,7},{1,0},{2,1},{3,2},{4,3},{5,4},{6,5},{7,6},{8,15},{9,8},{10,9... | collective-permute-start | bytes 786440 | tf_op jit(solution)/shard_map/ring/ppermute | solution.py:259
  79.8 10.5 %collective-permute-start.3 = (bf16[32,4096]{1,0:T(8,128)(2,1)S(1)}, bf16[32,4096]{1,0:T(8,128)(2,1)S(1)}, u32[]{:S(2)}, u32[]{:S(2)}) collective-permute-start(bf16[32,4096]{1,0:T(8,128)(2,1)S(1)} %add_convert_fusion.9), channel_id=1, source_target_pairs={{0,1},{1,2},{2,3},{3,4},{4,5},{5,6},{6,7},{7,0},{8,9},{9,10},{10,1... | collective-permute-start | bytes 786440 | tf_op jit(solution)/shard_map/ring/ppermute | solution.py:259
  83.7 10.1 %collective-permute-start.7 = (bf16[32,4096]{1,0:T(8,128)(2,1)S(1)}, bf16[32,4096]{1,0:T(8,128)(2,1)S(1)}, u32[]{:S(2)}, u32[]{:S(2)}) collective-permute-start(bf16[32,4096]{1,0:T(8,128)(2,1)S(1)} %add_convert_fusion.6), channel_id=1, source_target_pairs={{0,7},{1,0},{2,1},{3,2},{4,3},{5,4},{6,5},{7,6},{8,15},{9,8},{10,9... | collective-permute-start | bytes 786440 | tf_op jit(solution)/shard_map/ring/ppermute | solution.py:259

commit v3 on v2

v3 whole, which is shorter than its diff:
```python
import functools
import math

import jax
import jax.numpy as jnp
from jax import lax
from jax.experimental import pallas as pl
from jax.experimental.pallas import tpu as pltpu
from jax.sharding import PartitionSpec as P

DH = 128
ITERS = 10
N_HEAD = 8
CORES = 2
ROW = 4
COLUMN = 4
NOTE = 16
LIMIT = 50
OFFSETS = (4, 3, 5, 2, 6, 1, 7, 0)

ridge_lambda = 0.02
upper_end = 1.0 + ridge_lambda
center = (upper_end + ridge_lambda) / 2.0
radius = (upper_end - ridge_lambda) / 2.0

f32 = jnp.float32
bf16 = jnp.bfloat16


def dot(a, b):
    return jnp.dot(a, b, preferred_element_type=f32)


def split(field):
    high = field.astype(bf16)
    low = (field - high.astype(f32)).astype(bf16)
    return jnp.concatenate([high, low], axis=1)


def scale_of(rows):
    return lax.rsqrt(jnp.mean(rows * rows, axis=-1, keepdims=True) + 1e-06) * (
        1.0 / math.sqrt(DH)
    )


def tails_kernel(k_ref, v_ref, doc_ref, keep_ref, give_ref, kt_ref):
    tokens, width = k_ref.shape
    heads = width // DH
    doc = doc_ref[...].astype(f32)
    last = jnp.max(doc)
    member_row = (doc == last).astype(f32)
    member = jnp.broadcast_to(member_row, (DH, tokens)).T
    first_core = lax.rem(lax.axis_index("ctx"), CORES) == 0
    for h in range(heads):
        cols = slice(h * DH, (h + 1) * DH)
        k = k_ref[:, cols].astype(f32)
        scale = scale_of(k) * member
        kt = k.T.astype(bf16)
        kt_ref[cols, :] = kt
        right = jnp.concatenate(
            [k * (scale * scale), v_ref[:, cols].astype(f32) * scale], axis=1
        ).astype(bf16)
        state = dot(kt, right)
        key_state, value_state = state[:, :DH], state[:, DH:]
        keep_ref[cols, :] = jnp.where(first_core, key_state, value_state).astype(bf16)
        give_ref[cols, :] = jnp.where(first_core, value_state, key_state).astype(bf16)
    kt_ref[width:, :] = jnp.broadcast_to(doc, (NOTE, tokens)).astype(bf16)
    number = jnp.broadcast_to(jnp.sum(member_row, axis=1, keepdims=True), (8, DH))
    sixteens = jnp.floor(number * (1.0 / 16.0))
    note = jnp.concatenate(
        [jnp.full((4, DH), last), sixteens[:4], number - 16.0 * sixteens], axis=0
    ).astype(bf16)
    keep_ref[width:, :] = note
    give_ref[width:, :] = note


def solve_kernel(pieces, *refs):
    hbm, refs = refs[:7], refs[7:]
    outs, refs = refs[: len(pieces)], refs[len(pieces) :]
    held, (right, weight, p_ref, r_ref, x_ref, y_ref, sems) = refs[:7], refs[7:]
    loads = [pltpu.make_async_copy(a, b, sems.at[i]) for i, (a, b) in enumerate(zip(hbm, held))]
    for load in loads:
        load.start()
    q_ref, k_ref, v_ref, kt_ref, mine_ref, back_ref, w_vmem = held
    tokens, width = q_ref.shape
    heads = width // DH
    share = tokens // N_HEAD
    for load in loads[:-1]:
        load.wait()

    first_core = lax.rem(lax.axis_index("ctx"), CORES) == 0
    doc = kt_ref[width : width + NOTE, :].astype(f32)[:1]
    mine = jnp.broadcast_to(doc, (DH, tokens)).T
    note = mine_ref[width : width + NOTE, :].astype(f32)
    causal = lax.broadcasted_iota(jnp.int32, (tokens, tokens), 1) <= lax.broadcasted_iota(
        jnp.int32, (tokens, tokens), 0
    )
    wide = jnp.concatenate([mine] * (tokens // DH), axis=1)
    inside = (causal & (wide == doc)).astype(f32)
    prior = (mine == note[0:1]).astype(f32)
    inverse = 1.0 / (
        prior * (16.0 * note[4:5] + note[8:9]) + jnp.sum(inside, axis=1, keepdims=True)
    )
    prior_inverse = prior * inverse
    inside_inverse = inside * jnp.concatenate([inverse] * (tokens // DH), axis=1)

    scales = []
    for h in range(heads):
        cols = slice(h * DH, (h + 1) * DH)
        kt = kt_ref[cols, :]
        ktf = kt.astype(f32)
        mean = jnp.mean(ktf * ktf, axis=0, keepdims=True)
        scale = lax.rsqrt(mean + 1e-06) * (1.0 / math.sqrt(DH))
        scales.append(scale)
        weight[h] = inside_inverse * (scale * scale)
        state = jnp.where(first_core, mine_ref[cols, :], back_ref[cols, :])
        for at in (0, DH):
            right[h, at : at + DH, :tokens] = kt
            right[h, at : at + DH, tokens:] = state
        q = q_ref[:, cols].astype(f32)
        q = q * scale_of(q)
        r_ref[h] = q
        p_ref[h] = q * (1.0 / center)
        x_ref[h] = q * (1.0 / center)

    def products(field, h, times, rows):
        both = dot(split(field), right[h])
        return dot((both[:, :tokens] * times).astype(bf16), rows), both[:, tokens:]

    factor = radius / center
    for _ in range(ITERS):
        factor_new = 1.0 / (2.0 * center / radius - factor)
        for h in range(heads):
            p = p_ref[h]
            within, far = products(p, h, weight[h], k_ref[:, h * DH : (h + 1) * DH])
            r = r_ref[h] - (within + far * prior_inverse + ridge_lambda * p)
            p = (factor_new * factor) * p + (2.0 * factor_new / radius) * r
            r_ref[h] = r
            p_ref[h] = p
            x_ref[h] = x_ref[h] + p
        factor = factor_new

    for h in range(heads):
        cols = slice(h * DH, (h + 1) * DH)
        scale = scales[h]
        state = jnp.where(first_core, back_ref[cols, :], mine_ref[cols, :])
        for at in (0, DH):
            right[h, at : at + DH, tokens:] = state
        within, far = products(x_ref[h], h, inside * scale, v_ref[:, cols])
        o = within + far * prior
        o = o * lax.rsqrt(jnp.mean(o * o, axis=-1, keepdims=True) + 1e-06)
        y_ref[:, cols] = o.astype(bf16)
    me = lax.axis_index("head")
    y = jnp.concatenate(
        [
            y_ref[pl.ds(pl.multiple_of(lax.rem(me + o, N_HEAD) * share, share), share), :]
            for o in OFFSETS
        ],
        axis=0,
    )
    loads[-1].wait()
    model = w_vmem.shape[1]
    tile = 1024
    for c in range(0, model, tile):
        part = dot(y, w_vmem[:, c : c + tile]).astype(bf16)
        for out, (at, lo, hi) in zip(outs, pieces):
            if lo <= c < hi:
                out[:, c - lo : c - lo + tile] = part[at * share : (at + 1) * share]


def solve(pieces, *args):
    tokens, width = args[0].shape
    heads = width // DH
    share = tokens // N_HEAD
    vmem = pl.BlockSpec(memory_space=pltpu.VMEM)
    return pl.pallas_call(
        functools.partial(solve_kernel, pieces),
        out_shape=[jax.ShapeDtypeStruct((share, hi - lo), bf16) for _, lo, hi in pieces],
        in_specs=[pl.BlockSpec(memory_space=pltpu.HBM)] * len(args),
        out_specs=[vmem] * len(pieces),
        scratch_shapes=[
            *[pltpu.VMEM(a.shape, a.dtype) for a in args],
            pltpu.VMEM((heads, 2 * DH, tokens + DH), bf16),
            pltpu.VMEM((heads, tokens, tokens), f32),
            pltpu.VMEM((heads, tokens, DH), f32),
            pltpu.VMEM((heads, tokens, DH), f32),
            pltpu.VMEM((heads, tokens, DH), f32),
            pltpu.VMEM((tokens, width), bf16),
            pltpu.SemaphoreType.DMA((len(args),)),
        ],
        compiler_params=pltpu.CompilerParams(vmem_limit_bytes=LIMIT << 20),
        cost_estimate=pl.CostEstimate(
            flops=12_000_000_000, bytes_accessed=12_000_000, transcendentals=0
        ),
    )(*args)


def prior_states(keep, give):
    rows = keep.shape[0]
    at = rows - NOTE
    size = lax.axis_size("ctx")
    index = lax.axis_index("ctx")
    core = lax.rem(index, CORES)
    x = lax.rem(index // CORES, ROW)
    y = index // (CORES * ROW)
    counted = lax.broadcasted_iota(jnp.int32, (rows, 1), 0)
    counted = (counted < at) | (counted >= at + 4)

    def across(array):
        return lax.ppermute(array, "ctx", [(i, i ^ 1) for i in range(size)])

    def along_x(array, step):
        def target(i):
            c, xx, yy = i % CORES, i // CORES % ROW, i // (CORES * ROW)
            return (yy * ROW + (xx + step) % ROW) * CORES + c

        return lax.ppermute(array, "ctx", [(i, target(i)) for i in range(size)])

    def along_y(array, step):
        return lax.ppermute(
            array, "ctx", [(i, (i + step * CORES * ROW) % size) for i in range(size)]
        )

    def last(array):
        return array[at : at + 1].astype(f32)

    def gated(array, gate):
        return jnp.where(gate & counted, array.astype(f32), 0.0)

    def named(state, document):
        return jnp.where(counted, state, document).astype(bf16)

    other = across(give)
    early = jnp.where(core == 0, keep, other)
    late = jnp.where(core == 0, other, keep)
    chip = named(
        gated(late, last(late) == last(late)) + gated(early, last(early) == last(late)), last(late)
    )
    one = along_x(chip, 1)
    three = along_x(chip, -1)
    two = along_x(chip, 2)
    row_last = jnp.maximum(
        jnp.maximum(last(one), last(two)), jnp.maximum(last(three), last(chip))
    )
    row = named(
        sum(gated(part, last(part) == row_last) for part in (chip, one, two, three)), row_last
    )
    row_one = along_y(row, 1)
    row_two = along_y(row, 2)
    document = jnp.where(x > 0, last(one), jnp.where(y > 0, last(row_one), -1.0))
    first = sum(
        gated(part, (last(part) == document) & there)
        for part, there in (
            (one, x >= 1),
            (two, x >= 2),
            (three, x >= 3),
            (row_one, y >= 1),
            (row_two, y >= 2),
        )
    )
    second = gated(early, last(early) == last(early)) + jnp.where(
        last(early) == document, first, 0.0
    )
    first = named(first, document)
    second = named(second, last(early))
    mine = jnp.where(core == 0, first, second)
    back = across(jnp.where(core == 0, second, first))
    return mine, back


def shards(queries, keys, values, doc_ids, w_out):
    tokens, width = queries.shape
    model = w_out.shape[1]
    half = model // 2
    doc = doc_ids.reshape(1, tokens)
    vmem = pl.BlockSpec(memory_space=pltpu.VMEM)
    with jax.named_scope("tails"):
        keep, give, kt = pl.pallas_call(
            tails_kernel,
            out_shape=[
                jax.ShapeDtypeStruct((width + NOTE, DH), bf16),
                jax.ShapeDtypeStruct((width + NOTE, DH), bf16),
                jax.ShapeDtypeStruct((width + NOTE, tokens), bf16),
            ],
            in_specs=[vmem] * 3,
            out_specs=[vmem] * 3,
        )(keys, values, doc)
    with jax.named_scope("prior_states"):
        mine, back = prior_states(keep, give)
    pieces = []
    for at in range(N_HEAD):
        pieces += [(at, 0, half), (at, half, model)]
    with jax.named_scope("solve"):
        got = solve(tuple(pieces), queries, keys, values, kt, mine, back, w_out)
    part = {(o, c): got[2 * at + c] for at, o in enumerate(OFFSETS) for c in range(2)}

    size = lax.axis_size("head")

    def hop(array, step):
        return lax.ppermute(array, "head", [(i, (i + step) % size) for i in range(size)])

    def add(*arrays):
        return sum(array.astype(f32) for array in arrays).astype(bf16)

    streams = ((1, 0, 4), (-1, 1, 4), (1, 1, 3), (-1, 0, 3))
    moving = []
    with jax.named_scope("ring"):
        for step, c, hops in streams:
            total = part[hops * step % N_HEAD, c]
            for distance in range(hops - 1, 0, -1):
                total = add(hop(total, step), part[distance * step % N_HEAD, c])
            moving.append(hop(total, step))
    moving = lax.optimization_barrier(tuple(moving))
    columns = [
        add(*[array for array, stream in zip(moving, streams) if stream[1] == c], part[0, c])
        for c in range(2)
    ]
    return jnp.concatenate(columns, axis=1)


def solution(mesh):
    return jax.shard_map(
        shards,
        mesh=mesh,
        in_specs=(P("ctx", "head"), P("ctx", "head"), P("ctx", "head"), P("ctx"), P("head", None)),
        out_specs=P(("ctx", "head"), None),
        check_vma=False,
    )
```

time: 97 us -> 91.3 us (0.941)
  blocking collectives: 31.2 us -> 0 us
  waiting for transfers between devices: 19.9 us -> 36.7 us
  starting transfers between devices: 25.7 us -> 35.3 us
  other arithmetic: 2.6 us -> 4.65 us
  local copies, waits for them, and re-layouts: 1.38 us -> 0.01 us
  Pallas kernels: 14.9 us -> 13.7 us
    all_to_all x2 -> x0, blocking collectives: 31.2 us -> none  [the longest x1 17.7 us: shards(): recv = lax.all_to_all(send, 'ctx', 0, 0, tiled=True)]
    ppermute x14 -> x21, waiting for transfers between devices: 19.9 us -> 36.7 us  [the longest x14 19.6 us: hop(): lax.ppermute(array, 'head', [(i, (i + step) % size) for i in range(size)])]
    ppermute x14 -> x21, starting transfers between devices: 25.7 us -> 35.3 us  [the longest x14 25.9 us: hop(): lax.ppermute(array, 'head', [(i, (i + step) % size) for i in range(size)])]
    select_n x0 -> x3, other arithmetic: none -> 1.47 us  [the longest x1 0.93 us: prior_states(): late = jnp.where(core == 0, other, keep)]
    unnamed x4 -> x0, local copies, waits for them, and re-layouts: 1.38 us -> none
    pallas_call x3 -> x2, Pallas kernels: 14.9 us -> 13.7 us  [the longest x1 11.3 us: solve(): pl.pallas_call(functools.partial(solve_kernel, pieces), out_shape=[jax.Sh...]
    convert_element_type x11 -> x13, other arithmetic: 1.77 us -> 2.3 us  [the longest x11 1.85 us: add(): return sum((array.astype(f32) for array in arrays)).astype(bf16)]
  transfers between devices with their start and end apart: 14 -> 21, of which waited for: 9 -> 16; matrix products, arithmetic and copies ran while one was open for 1% -> 1% of each run, Pallas kernels for 0% -> 0%
where the time goes in v3:
time: 91.3 us; the launch traced here: 90.5 us
  waiting for transfers between devices  36.7 us (40%)
  starting transfers between devices  35.3 us (39%)
  Pallas kernels  13.7 us (15%)
  other arithmetic  4.65 us (5%)
    ppermute x14, starting transfers between devices, hop(): lax.ppermute(array, 'head', [(i, (i + step) % size) for i in range(size)])  25.9 us
    ppermute x14, waiting for transfers between devices, hop(): lax.ppermute(array, 'head', [(i, (i + step) % size) for i in range(size)])  19.6 us
    pallas_call x1, Pallas kernels, solve(): pl.pallas_call(functools.partial(solve_kernel, pieces), out_shape=[jax.Sh...  11.3 us
    ppermute x3, waiting for transfers between devices, along_x(): return lax.ppermute(array, 'ctx', [(i, target(i)) for i in range(size)])  8.07 us
    ppermute x2, waiting for transfers between devices, along_y(): lax.ppermute(array, 'ctx', [(i, (i + step * CORES * ROW) % size) for i in...  6.36 us
    ppermute x2, starting transfers between devices, along_y(): lax.ppermute(array, 'ctx', [(i, (i + step * CORES * ROW) % size) for i in...  4.55 us
    ppermute x3, starting transfers between devices, along_x(): return lax.ppermute(array, 'ctx', [(i, target(i)) for i in range(size)])  4.52 us
    ppermute x2, waiting for transfers between devices, across(): return lax.ppermute(array, 'ctx', [(i, i ^ 1) for i in range(size)])  2.75 us
  transfers between devices with their start and end apart: 21, of which 16 were waited for; matrix products, arithmetic and copies ran while one was open for 1% of the time, Pallas kernels for 0%

profile of v3, /device:TPU:96, one launch (start us, length us, event | category | flops | bytes accessed | tf_op | source)
XLA Modules:
  0.0 90.5 jit_solution(10818098757482651198)
XLA Ops:
  0.0 2.4 %tails.1 = (bf16[528,128]{1,0:T(8,128)(2,1)}, bf16[528,128]{1,0:T(8,128)(2,1)}, bf16[528,256]{1,0:T(8,128)(2,1)}) custom-call(bf16[256,512]{1,0:T(8,128)(2,1)} %refs_1_.1, bf16[256,512]{1,0:T(8,128)(2,1)} %refs_2_.1, s32[1,256]{1,0:T(1,128)} %bitcast.36), custom_call_target="tpu_custom_call" | custom-call | tf_op jit(solution)/shard_map/tails/pallas_call | solution.py:278
  2.4 0.0 collective-permute-start
  2.4 1.6 %collective-permute-done = bf16[528,128]{1,0:T(8,128)(2,1)S(1)} collective-permute-done((bf16[528,128]{1,0:T(8,128)(2,1)}, bf16[528,128]{1,0:T(8,128)(2,1)S(1)}, u32[]{:S(2)}, u32[]{:S(2)}) %collective-permute-start) | collective-permute-done | bytes 135200 | tf_op jit(solution)/shard_map/prior_states/ppermute | solution.py:210
  3.9 0.9 %broadcast_select_fusion.3 = (bf16[528,128]{1,0:T(8,128)(2,1)S(1)}, bf16[528,128]{1,0:T(8,128)(2,1)S(1)}) fusion(bf16[528,128]{1,0:T(8,128)(2,1)S(1)} %collective-permute-done, bf16[528,128]{1,0:T(8,128)(2,1)} %get-tuple-element.30, pred[]{:T(512)S(6)} %eq.45), kind=kLoop, calls=%fused_computation.40 | loop fusion | flops 135168 | bytes 540673 | tf_op jit(solution)/shard_map/prior_states/jit(_where)/select_n | solution.py:235
  4.9 0.2 fusion.2
  5.1 2.8 %collective-permute-start.3 = (bf16[528,128]{1,0:T(8,128)(2,1)S(1)}, bf16[528,128]{1,0:T(8,128)(2,1)S(1)}, u32[]{:S(2)}, u32[]{:S(2)}) collective-permute-start(bf16[528,128]{1,0:T(8,128)(2,1)S(1)} %fusion.2), channel_id=1, source_target_pairs={{0,48},{8,56},{16,0},{24,8},{32,16},{40,24},{48,32},{56,40},{64,11... | collective-permute-start | bytes 405512 | tf_op jit(solution)/shard_map/prior_states/ppermute | solution.py:217
  7.9 0.8 collective-permute-start.2
  8.7 0.9 collective-permute-start.1
  9.6 4.4 %collective-permute-done.3 = bf16[528,128]{1,0:T(8,128)(2,1)S(1)} collective-permute-done((bf16[528,128]{1,0:T(8,128)(2,1)S(1)}, bf16[528,128]{1,0:T(8,128)(2,1)S(1)}, u32[]{:S(2)}, u32[]{:S(2)}) %collective-permute-start.3) | collective-permute-done | bytes 135200 | tf_op jit(solution)/shard_map/prior_states/ppermute | solution.py:217
  14.0 1.9 %collective-permute-done.2 = bf16[528,128]{1,0:T(8,128)(2,1)S(1)} collective-permute-done((bf16[528,128]{1,0:T(8,128)(2,1)S(1)}, bf16[528,128]{1,0:T(8,128)(2,1)S(1)}, u32[]{:S(2)}, u32[]{:S(2)}) %collective-permute-start.2) | collective-permute-done | bytes 135200 | tf_op jit(solution)/shard_map/prior_states/ppermute | solution.py:217
  15.9 1.8 %collective-permute-done.1 = bf16[528,128]{1,0:T(8,128)(2,1)S(1)} collective-permute-done((bf16[528,128]{1,0:T(8,128)(2,1)S(1)}, bf16[528,128]{1,0:T(8,128)(2,1)S(1)}, u32[]{:S(2)}, u32[]{:S(2)}) %collective-permute-start.1) | collective-permute-done | bytes 135200 | tf_op jit(solution)/shard_map/prior_states/ppermute | solution.py:217
  17.7 0.3 fusion.10
  18.0 1.7 %collective-permute-start.4 = (bf16[528,128]{1,0:T(8,128)(2,1)S(1)}, bf16[528,128]{1,0:T(8,128)(2,1)S(1)}, u32[]{:S(2)}, u32[]{:S(2)}) collective-permute-start(bf16[528,128]{1,0:T(8,128)(2,1)S(1)} %fusion.10), channel_id=1, source_target_pairs={{0,64},{8,72},{16,80},{24,88},{32,96},{40,104},{48,112},{56,120},{... | collective-permute-start | bytes 405512 | tf_op jit(solution)/shard_map/prior_states/ppermute | solution.py:220
  19.6 2.9 %collective-permute-start.5 = (bf16[528,128]{1,0:T(8,128)(2,1)S(1)}, bf16[528,128]{1,0:T(8,128)(2,1)S(1)}, u32[]{:S(2)}, u32[]{:S(2)}) collective-permute-start(bf16[528,128]{1,0:T(8,128)(2,1)S(1)} %fusion.10), channel_id=1, source_target_pairs={{0,128},{8,136},{16,144},{24,152},{32,160},{40,168},{48,176},{56,1... | collective-permute-start | bytes 405512 | tf_op jit(solution)/shard_map/prior_states/ppermute | solution.py:220
  22.5 2.3 %collective-permute-done.4 = bf16[528,128]{1,0:T(8,128)(2,1)S(1)} collective-permute-done((bf16[528,128]{1,0:T(8,128)(2,1)S(1)}, bf16[528,128]{1,0:T(8,128)(2,1)S(1)}, u32[]{:S(2)}, u32[]{:S(2)}) %collective-permute-start.4) | collective-permute-done | bytes 135200 | tf_op jit(solution)/shard_map/prior_states/ppermute | solution.py:220
  24.8 4.1 %collective-permute-done.5 = bf16[528,128]{1,0:T(8,128)(2,1)S(1)} collective-permute-done((bf16[528,128]{1,0:T(8,128)(2,1)S(1)}, bf16[528,128]{1,0:T(8,128)(2,1)S(1)}, u32[]{:S(2)}, u32[]{:S(2)}) %collective-permute-start.5) | collective-permute-done | bytes 135200 | tf_op jit(solution)/shard_map/prior_states/ppermute | solution.py:220
  28.9 0.4 broadcast_select_fusion
  29.3 0.3 collective-permute-start.6
  29.6 0.1 broadcast_select_fusion.1.refs_4_
  29.8 1.2 %collective-permute-done.6.refs_5_ = bf16[528,128]{1,0:T(8,128)(2,1)S(1)} collective-permute-done((bf16[528,128]{1,0:T(8,128)(2,1)S(1)}, bf16[528,128]{1,0:T(8,128)(2,1)S(1)}, u32[]{:S(2)}, u32[]{:S(2)}) %collective-permute-start.6) | collective-permute-done | bytes 135200 | tf_op jit(solution)/shard_map/prior_states/ppermute | solution.py:210
  31.0 11.3 %solve.1 = (bf16[32,4096]{1,0:T(8,128)(2,1)S(1)}, bf16[32,4096]{1,0:T(8,128)(2,1)S(1)}, bf16[32,4096]{1,0:T(8,128)(2,1)S(1)}, bf16[32,4096]{1,0:T(8,128)(2,1)S(1...) custom-call(bf16[256,512]{1,0:T(8,128)(2,1)} %refs_0_.1, ...), custom_call_target="tpu_custom_call" | custom-call | flops 12000000000 | bytes 12000000 | tf_op jit(solution)/shard_map/solve/pallas_call | solution.py:176
  42.2 3.2 %collective-permute-start.7 = (bf16[32,4096]{1,0:T(8,128)(2,1)S(1)}, bf16[32,4096]{1,0:T(8,128)(2,1)S(1)}, u32[]{:S(2)}, u32[]{:S(2)}) collective-permute-start(bf16[32,4096]{1,0:T(8,128)(2,1)S(1)} %get-tuple-element.31), channel_id=1, source_target_pairs={{0,1},{1,2},{2,3},{3,4},{4,5},{5,6},{6,7},{7,0},{8,9},{9,10},{10,1... | collective-permute-start | bytes 786440 | tf_op jit(solution)/shard_map/ring/ppermute | solution.py:300
  45.5 0.0 collective-permute-start.11
  45.5 3.2 %collective-permute-start.15 = (bf16[32,4096]{1,0:T(8,128)(2,1)S(1)}, bf16[32,4096]{1,0:T(8,128)(2,1)S(1)}, u32[]{:S(2)}, u32[]{:S(2)}) collective-permute-start(bf16[32,4096]{1,0:T(8,128)(2,1)S(1)} %get-tuple-element.39), channel_id=1, source_target_pairs={{0,1},{1,2},{2,3},{3,4},{4,5},{5,6},{6,7},{7,0},{8,9},{9,10},{10,1... | collective-permute-start | bytes 786440 | tf_op jit(solution)/shard_map/ring/ppermute | solution.py:300
  48.7 0.0 collective-permute-start.18
  48.7 3.4 %collective-permute-done.7 = bf16[32,4096]{1,0:T(8,128)(2,1)S(1)} collective-permute-done((bf16[32,4096]{1,0:T(8,128)(2,1)S(1)}, bf16[32,4096]{1,0:T(8,128)(2,1)S(1)}, u32[]{:S(2)}, u32[]{:S(2)}) %collective-permute-start.7) | collective-permute-done | bytes 262176 | tf_op jit(solution)/shard_map/ring/ppermute | solution.py:300
  52.1 0.1 add_convert_fusion.11
  52.2 4.0 %collective-permute-start.8 = (bf16[32,4096]{1,0:T(8,128)(2,1)S(1)}, bf16[32,4096]{1,0:T(8,128)(2,1)S(1)}, u32[]{:S(2)}, u32[]{:S(2)}) collective-permute-start(bf16[32,4096]{1,0:T(8,128)(2,1)S(1)} %add_convert_fusion.11), channel_id=1, source_target_pairs={{0,1},{1,2},{2,3},{3,4},{4,5},{5,6},{6,7},{7,0},{8,9},{9,10},{10,1... | collective-permute-start | bytes 786440 | tf_op jit(solution)/shard_map/ring/ppermute | solution.py:300
  56.2 0.0 collective-permute-done.11
  56.2 0.1 add_convert_fusion.8
  56.3 0.1 collective-permute-start.12
  56.3 1.4 %collective-permute-done.15 = bf16[32,4096]{1,0:T(8,128)(2,1)S(1)} collective-permute-done((bf16[32,4096]{1,0:T(8,128)(2,1)S(1)}, bf16[32,4096]{1,0:T(8,128)(2,1)S(1)}, u32[]{:S(2)}, u32[]{:S(2)}) %collective-permute-start.15) | collective-permute-done | bytes 262176 | tf_op jit(solution)/shard_map/ring/ppermute | solution.py:300
  57.7 0.1 add_convert_fusion.5
  57.8 3.8 %collective-permute-start.16 = (bf16[32,4096]{1,0:T(8,128)(2,1)S(1)}, bf16[32,4096]{1,0:T(8,128)(2,1)S(1)}, u32[]{:S(2)}, u32[]{:S(2)}) collective-permute-start(bf16[32,4096]{1,0:T(8,128)(2,1)S(1)} %add_convert_fusion.5), channel_id=1, source_target_pairs={{0,1},{1,2},{2,3},{3,4},{4,5},{5,6},{6,7},{7,0},{8,9},{9,10},{10,1... | collective-permute-start | bytes 786440 | tf_op jit(solution)/shard_map/ring/ppermute | solution.py:300
  61.6 0.0 collective-permute-done.18
  61.6 0.1 add_convert_fusion.3
  61.7 0.1 collective-permute-start.19
  61.7 1.6 %collective-permute-done.8 = bf16[32,4096]{1,0:T(8,128)(2,1)S(1)} collective-permute-done((bf16[32,4096]{1,0:T(8,128)(2,1)S(1)}, bf16[32,4096]{1,0:T(8,128)(2,1)S(1)}, u32[]{:S(2)}, u32[]{:S(2)}) %collective-permute-start.8) | collective-permute-done | bytes 262176 | tf_op jit(solution)/shard_map/ring/ppermute | solution.py:300
  63.4 0.1 add_convert_fusion.10
  63.4 3.8 %collective-permute-start.9 = (bf16[32,4096]{1,0:T(8,128)(2,1)S(1)}, bf16[32,4096]{1,0:T(8,128)(2,1)S(1)}, u32[]{:S(2)}, u32[]{:S(2)}) collective-permute-start(bf16[32,4096]{1,0:T(8,128)(2,1)S(1)} %add_convert_fusion.10), channel_id=1, source_target_pairs={{0,1},{1,2},{2,3},{3,4},{4,5},{5,6},{6,7},{7,0},{8,9},{9,10},{10,1... | collective-permute-start | bytes 786440 | tf_op jit(solution)/shard_map/ring/ppermute | solution.py:300
  67.2 0.0 collective-permute-done.12
  67.2 0.1 add_convert_fusion.7
  67.3 0.1 collective-permute-start.13
  67.4 1.6 %collective-permute-done.16 = bf16[32,4096]{1,0:T(8,128)(2,1)S(1)} collective-permute-done((bf16[32,4096]{1,0:T(8,128)(2,1)S(1)}, bf16[32,4096]{1,0:T(8,128)(2,1)S(1)}, u32[]{:S(2)}, u32[]{:S(2)}) %collective-permute-start.16) | collective-permute-done | bytes 262176 | tf_op jit(solution)/shard_map/ring/ppermute | solution.py:300
  69.0 0.1 add_convert_fusion.4
  69.0 3.8 %collective-permute-start.17 = (bf16[32,4096]{1,0:T(8,128)(2,1)S(1)}, bf16[32,4096]{1,0:T(8,128)(2,1)S(1)}, u32[]{:S(2)}, u32[]{:S(2)}) collective-permute-start(bf16[32,4096]{1,0:T(8,128)(2,1)S(1)} %add_convert_fusion.4), channel_id=1, source_target_pairs={{0,1},{1,2},{2,3},{3,4},{4,5},{5,6},{6,7},{7,0},{8,9},{9,10},{10,1... | collective-permute-start | bytes 786440 | tf_op jit(solution)/shard_map/ring/ppermute | solution.py:300
  72.8 0.0 collective-permute-done.19
  72.8 0.1 add_convert_fusion.2
  72.9 0.1 collective-permute-start.20
  73.0 1.6 %collective-permute-done.9 = bf16[32,4096]{1,0:T(8,128)(2,1)S(1)} collective-permute-done((bf16[32,4096]{1,0:T(8,128)(2,1)S(1)}, bf16[32,4096]{1,0:T(8,128)(2,1)S(1)}, u32[]{:S(2)}, u32[]{:S(2)}) %collective-permute-start.9) | collective-permute-done | bytes 262176 | tf_op jit(solution)/shard_map/ring/ppermute | solution.py:300
  74.6 0.1 add_convert_fusion.9
  74.7 3.8 %collective-permute-start.10 = (bf16[32,4096]{1,0:T(8,128)(2,1)S(1)}, bf16[32,4096]{1,0:T(8,128)(2,1)S(1)}, u32[]{:S(2)}, u32[]{:S(2)}) collective-permute-start(bf16[32,4096]{1,0:T(8,128)(2,1)S(1)} %add_convert_fusion.9), channel_id=1, source_target_pairs={{0,1},{1,2},{2,3},{3,4},{4,5},{5,6},{6,7},{7,0},{8,9},{9,10},{10,1... | collective-permute-start | bytes 786440 | tf_op jit(solution)/shard_map/ring/ppermute | solution.py:300
  78.4 0.0 collective-permute-done.13
  78.4 0.1 add_convert_fusion.6
  78.5 0.1 collective-permute-start.14
  78.6 1.6 %collective-permute-done.17 = bf16[32,4096]{1,0:T(8,128)(2,1)S(1)} collective-permute-done((bf16[32,4096]{1,0:T(8,128)(2,1)S(1)}, bf16[32,4096]{1,0:T(8,128)(2,1)S(1)}, u32[]{:S(2)}, u32[]{:S(2)}) %collective-permute-start.17) | collective-permute-done | bytes 262176 | tf_op jit(solution)/shard_map/ring/ppermute | solution.py:300
  80.2 3.7 %collective-permute-done.20 = bf16[32,4096]{1,0:T(8,128)(2,1)S(1)} collective-permute-done((bf16[32,4096]{1,0:T(8,128)(2,1)S(1)}, bf16[32,4096]{1,0:T(8,128)(2,1)S(1)}, u32[]{:S(2)}, u32[]{:S(2)}) %collective-permute-start.20) | collective-permute-done | bytes 262176 | tf_op jit(solution)/shard_map/ring/ppermute | solution.py:300
  83.9 1.1 %collective-permute-done.10 = bf16[32,4096]{1,0:T(8,128)(2,1)S(1)} collective-permute-done((bf16[32,4096]{1,0:T(8,128)(2,1)S(1)}, bf16[32,4096]{1,0:T(8,128)(2,1)S(1)}, u32[]{:S(2)}, u32[]{:S(2)}) %collective-permute-start.10) | collective-permute-done | bytes 262176 | tf_op jit(solution)/shard_map/ring/ppermute | solution.py:300
  85.0 3.4 %collective-permute-done.14 = bf16[32,4096]{1,0:T(8,128)(2,1)S(1)} collective-permute-done((bf16[32,4096]{1,0:T(8,128)(2,1)S(1)}, bf16[32,4096]{1,0:T(8,128)(2,1)S(1)}, u32[]{:S(2)}, u32[]{:S(2)}) %collective-permute-start.14) | collective-permute-done | bytes 262176 | tf_op jit(solution)/shard_map/ring/ppermute | solution.py:300
  88.5 1.2 %add_convert_fusion = (bf16[32,4096]{1,0:T(8,128)(2,1)S(1)}, bf16[32,4096]{1,0:T(8,128)(2,1)S(1)}) fusion(bf16[32,4096]{1,0:T(8,128)(2,1)} %get-tuple-element.50, bf16[32,4096]{1,0:T(8,128)(2,1)S(1)} %collective-permute-done.17, bf16[32,4096]{1,0:T(8,128)(2,1)S(1)} %collective-permute-done.14, bf16[32,4096]{1,0:T(8,128)(2,1)} %get-tuple-element.47, ...), kind=kLoop, calls=%fused_computation.1 | loop fusion | flops 1572864 | bytes 2097152 | tf_op jit(solution)/shard_map/convert_element_type | solution.py:303
  89.7 0.8 pad_maximum_fusion
  (8 shorter events, 0.1 us)
Async XLA Ops:
  2.4 1.6 %collective-permute-start = (bf16[528,128]{1,0:T(8,128)(2,1)}, bf16[528,128]{1,0:T(8,128)(2,1)S(1)}, u32[]{:S(2)}, u32[]{:S(2)}) collective-permute-start(bf16[528,128]{1,0:T(8,128)(2,1)} %get-tuple-element.29), channel_id=1, source_target_pairs={{0,8},{8,0},{16,24},{24,16},{32,40},{40,32},{48,56},{56,48},{64,72... | collective-permute-start | bytes 405512 | tf_op jit(solution)/shard_map/prior_states/ppermute | solution.py:210
  5.1 8.9 %collective-permute-start.3 = (bf16[528,128]{1,0:T(8,128)(2,1)S(1)}, bf16[528,128]{1,0:T(8,128)(2,1)S(1)}, u32[]{:S(2)}, u32[]{:S(2)}) collective-permute-start(bf16[528,128]{1,0:T(8,128)(2,1)S(1)} %fusion.2), channel_id=1, source_target_pairs={{0,48},{8,56},{16,0},{24,8},{32,16},{40,24},{48,32},{56,40},{64,11... | collective-permute-start | bytes 405512 | tf_op jit(solution)/shard_map/prior_states/ppermute | solution.py:217
  7.9 8.0 %collective-permute-start.2 = (bf16[528,128]{1,0:T(8,128)(2,1)S(1)}, bf16[528,128]{1,0:T(8,128)(2,1)S(1)}, u32[]{:S(2)}, u32[]{:S(2)}) collective-permute-start(bf16[528,128]{1,0:T(8,128)(2,1)S(1)} %fusion.2), channel_id=1, source_target_pairs={{0,32},{8,40},{16,48},{24,56},{32,0},{40,8},{48,16},{56,24},{64,96... | collective-permute-start | bytes 405512 | tf_op jit(solution)/shard_map/prior_states/ppermute | solution.py:217
  8.7 9.0 %collective-permute-start.1 = (bf16[528,128]{1,0:T(8,128)(2,1)S(1)}, bf16[528,128]{1,0:T(8,128)(2,1)S(1)}, u32[]{:S(2)}, u32[]{:S(2)}) collective-permute-start(bf16[528,128]{1,0:T(8,128)(2,1)S(1)} %fusion.2), channel_id=1, source_target_pairs={{0,16},{8,24},{16,32},{24,40},{32,48},{40,56},{48,0},{56,8},{64,80... | collective-permute-start | bytes 405512 | tf_op jit(solution)/shard_map/prior_states/ppermute | solution.py:217
  18.0 6.9 %collective-permute-start.4 = (bf16[528,128]{1,0:T(8,128)(2,1)S(1)}, bf16[528,128]{1,0:T(8,128)(2,1)S(1)}, u32[]{:S(2)}, u32[]{:S(2)}) collective-permute-start(bf16[528,128]{1,0:T(8,128)(2,1)S(1)} %fusion.10), channel_id=1, source_target_pairs={{0,64},{8,72},{16,80},{24,88},{32,96},{40,104},{48,112},{56,120},{... | collective-permute-start | bytes 405512 | tf_op jit(solution)/shard_map/prior_states/ppermute | solution.py:220
  19.6 9.3 %collective-permute-start.5 = (bf16[528,128]{1,0:T(8,128)(2,1)S(1)}, bf16[528,128]{1,0:T(8,128)(2,1)S(1)}, u32[]{:S(2)}, u32[]{:S(2)}) collective-permute-start(bf16[528,128]{1,0:T(8,128)(2,1)S(1)} %fusion.10), channel_id=1, source_target_pairs={{0,128},{8,136},{16,144},{24,152},{32,160},{40,168},{48,176},{56,1... | collective-permute-start | bytes 405512 | tf_op jit(solution)/shard_map/prior_states/ppermute | solution.py:220
  29.3 1.6 %collective-permute-start.6 = (bf16[528,128]{1,0:T(8,128)(2,1)S(1)}, bf16[528,128]{1,0:T(8,128)(2,1)S(1)}, u32[]{:S(2)}, u32[]{:S(2)}) collective-permute-start(bf16[528,128]{1,0:T(8,128)(2,1)S(1)} %get-tuple-element.51), channel_id=1, source_target_pairs={{0,8},{8,0},{16,24},{24,16},{32,40},{40,32},{48,56},{56,48},{64,72... | collective-permute-start | bytes 405512 | tf_op jit(solution)/shard_map/prior_states/ppermute | solution.py:210
  42.2 9.9 %collective-permute-start.7 = (bf16[32,4096]{1,0:T(8,128)(2,1)S(1)}, bf16[32,4096]{1,0:T(8,128)(2,1)S(1)}, u32[]{:S(2)}, u32[]{:S(2)}) collective-permute-start(bf16[32,4096]{1,0:T(8,128)(2,1)S(1)} %get-tuple-element.31), channel_id=1, source_target_pairs={{0,1},{1,2},{2,3},{3,4},{4,5},{5,6},{6,7},{7,0},{8,9},{9,10},{10,1... | collective-permute-start | bytes 786440 | tf_op jit(solution)/shard_map/ring/ppermute | solution.py:300
  45.5 10.7 %collective-permute-start.11 = (bf16[32,4096]{1,0:T(8,128)(2,1)S(1)}, bf16[32,4096]{1,0:T(8,128)(2,1)S(1)}, u32[]{:S(2)}, u32[]{:S(2)}) collective-permute-start(bf16[32,4096]{1,0:T(8,128)(2,1)S(1)} %get-tuple-element.35), channel_id=1, source_target_pairs={{0,7},{1,0},{2,1},{3,2},{4,3},{5,4},{6,5},{7,6},{8,15},{9,8},{10,9... | collective-permute-start | bytes 786440 | tf_op jit(solution)/shard_map/ring/ppermute | solution.py:300
  45.5 12.3 %collective-permute-start.15 = (bf16[32,4096]{1,0:T(8,128)(2,1)S(1)}, bf16[32,4096]{1,0:T(8,128)(2,1)S(1)}, u32[]{:S(2)}, u32[]{:S(2)}) collective-permute-start(bf16[32,4096]{1,0:T(8,128)(2,1)S(1)} %get-tuple-element.39), channel_id=1, source_target_pairs={{0,1},{1,2},{2,3},{3,4},{4,5},{5,6},{6,7},{7,0},{8,9},{9,10},{10,1... | collective-permute-start | bytes 786440 | tf_op jit(solution)/shard_map/ring/ppermute | solution.py:300
  48.7 12.9 %collective-permute-start.18 = (bf16[32,4096]{1,0:T(8,128)(2,1)S(1)}, bf16[32,4096]{1,0:T(8,128)(2,1)S(1)}, u32[]{:S(2)}, u32[]{:S(2)}) collective-permute-start(bf16[32,4096]{1,0:T(8,128)(2,1)S(1)} %get-tuple-element.42), channel_id=1, source_target_pairs={{0,7},{1,0},{2,1},{3,2},{4,3},{5,4},{6,5},{7,6},{8,15},{9,8},{10,9... | collective-permute-start | bytes 786440 | tf_op jit(solution)/shard_map/ring/ppermute | solution.py:300
  52.2 11.2 %collective-permute-start.8 = (bf16[32,4096]{1,0:T(8,128)(2,1)S(1)}, bf16[32,4096]{1,0:T(8,128)(2,1)S(1)}, u32[]{:S(2)}, u32[]{:S(2)}) collective-permute-start(bf16[32,4096]{1,0:T(8,128)(2,1)S(1)} %add_convert_fusion.11), channel_id=1, source_target_pairs={{0,1},{1,2},{2,3},{3,4},{4,5},{5,6},{6,7},{7,0},{8,9},{9,10},{10,1... | collective-permute-start | bytes 786440 | tf_op jit(solution)/shard_map/ring/ppermute | solution.py:300
  56.3 10.9 %collective-permute-start.12 = (bf16[32,4096]{1,0:T(8,128)(2,1)S(1)}, bf16[32,4096]{1,0:T(8,128)(2,1)S(1)}, u32[]{:S(2)}, u32[]{:S(2)}) collective-permute-start(bf16[32,4096]{1,0:T(8,128)(2,1)S(1)} %add_convert_fusion.8), channel_id=1, source_target_pairs={{0,7},{1,0},{2,1},{3,2},{4,3},{5,4},{6,5},{7,6},{8,15},{9,8},{10,9... | collective-permute-start | bytes 786440 | tf_op jit(solution)/shard_map/ring/ppermute | solution.py:300
  57.8 11.2 %collective-permute-start.16 = (bf16[32,4096]{1,0:T(8,128)(2,1)S(1)}, bf16[32,4096]{1,0:T(8,128)(2,1)S(1)}, u32[]{:S(2)}, u32[]{:S(2)}) collective-permute-start(bf16[32,4096]{1,0:T(8,128)(2,1)S(1)} %add_convert_fusion.5), channel_id=1, source_target_pairs={{0,1},{1,2},{2,3},{3,4},{4,5},{5,6},{6,7},{7,0},{8,9},{9,10},{10,1... | collective-permute-start | bytes 786440 | tf_op jit(solution)/shard_map/ring/ppermute | solution.py:300
  61.7 11.2 %collective-permute-start.19 = (bf16[32,4096]{1,0:T(8,128)(2,1)S(1)}, bf16[32,4096]{1,0:T(8,128)(2,1)S(1)}, u32[]{:S(2)}, u32[]{:S(2)}) collective-permute-start(bf16[32,4096]{1,0:T(8,128)(2,1)S(1)} %add_convert_fusion.3), channel_id=1, source_target_pairs={{0,7},{1,0},{2,1},{3,2},{4,3},{5,4},{6,5},{7,6},{8,15},{9,8},{10,9... | collective-permute-start | bytes 786440 | tf_op jit(solution)/shard_map/ring/ppermute | solution.py:300
  63.4 11.2 %collective-permute-start.9 = (bf16[32,4096]{1,0:T(8,128)(2,1)S(1)}, bf16[32,4096]{1,0:T(8,128)(2,1)S(1)}, u32[]{:S(2)}, u32[]{:S(2)}) collective-permute-start(bf16[32,4096]{1,0:T(8,128)(2,1)S(1)} %add_convert_fusion.10), channel_id=1, source_target_pairs={{0,1},{1,2},{2,3},{3,4},{4,5},{5,6},{6,7},{7,0},{8,9},{9,10},{10,1... | collective-permute-start | bytes 786440 | tf_op jit(solution)/shard_map/ring/ppermute | solution.py:300
  67.3 11.2 %collective-permute-start.13 = (bf16[32,4096]{1,0:T(8,128)(2,1)S(1)}, bf16[32,4096]{1,0:T(8,128)(2,1)S(1)}, u32[]{:S(2)}, u32[]{:S(2)}) collective-permute-start(bf16[32,4096]{1,0:T(8,128)(2,1)S(1)} %add_convert_fusion.7), channel_id=1, source_target_pairs={{0,7},{1,0},{2,1},{3,2},{4,3},{5,4},{6,5},{7,6},{8,15},{9,8},{10,9... | collective-permute-start | bytes 786440 | tf_op jit(solution)/shard_map/ring/ppermute | solution.py:300
  69.0 11.2 %collective-permute-start.17 = (bf16[32,4096]{1,0:T(8,128)(2,1)S(1)}, bf16[32,4096]{1,0:T(8,128)(2,1)S(1)}, u32[]{:S(2)}, u32[]{:S(2)}) collective-permute-start(bf16[32,4096]{1,0:T(8,128)(2,1)S(1)} %add_convert_fusion.4), channel_id=1, source_target_pairs={{0,1},{1,2},{2,3},{3,4},{4,5},{5,6},{6,7},{7,0},{8,9},{9,10},{10,1... | collective-permute-start | bytes 786440 | tf_op jit(solution)/shard_map/ring/ppermute | solution.py:300
  72.9 11.1 %collective-permute-start.20 = (bf16[32,4096]{1,0:T(8,128)(2,1)S(1)}, bf16[32,4096]{1,0:T(8,128)(2,1)S(1)}, u32[]{:S(2)}, u32[]{:S(2)}) collective-permute-start(bf16[32,4096]{1,0:T(8,128)(2,1)S(1)} %add_convert_fusion.2), channel_id=1, source_target_pairs={{0,7},{1,0},{2,1},{3,2},{4,3},{5,4},{6,5},{7,6},{8,15},{9,8},{10,9... | collective-permute-start | bytes 786440 | tf_op jit(solution)/shard_map/ring/ppermute | solution.py:300
  74.7 10.4 %collective-permute-start.10 = (bf16[32,4096]{1,0:T(8,128)(2,1)S(1)}, bf16[32,4096]{1,0:T(8,128)(2,1)S(1)}, u32[]{:S(2)}, u32[]{:S(2)}) collective-permute-start(bf16[32,4096]{1,0:T(8,128)(2,1)S(1)} %add_convert_fusion.9), channel_id=1, source_target_pairs={{0,1},{1,2},{2,3},{3,4},{4,5},{5,6},{6,7},{7,0},{8,9},{9,10},{10,1... | collective-permute-start | bytes 786440 | tf_op jit(solution)/shard_map/ring/ppermute | solution.py:300
  78.5 10.0 %collective-permute-start.14 = (bf16[32,4096]{1,0:T(8,128)(2,1)S(1)}, bf16[32,4096]{1,0:T(8,128)(2,1)S(1)}, u32[]{:S(2)}, u32[]{:S(2)}) collective-permute-start(bf16[32,4096]{1,0:T(8,128)(2,1)S(1)} %add_convert_fusion.6), channel_id=1, source_target_pairs={{0,7},{1,0},{2,1},{3,2},{4,3},{5,4},{6,5},{7,6},{8,15},{9,8},{10,9... | collective-permute-start | bytes 786440 | tf_op jit(solution)/shard_map/ring/ppermute | solution.py:300

commit v4 on v3

--- a/solution.py
+++ b/solution.py
@@ -15,7 +15,7 @@
 ROW = 4
 COLUMN = 4
 NOTE = 16
-LIMIT = 50
+LIMIT = 198
 OFFSETS = (4, 3, 5, 2, 6, 1, 7, 0)
 
 ridge_lambda = 0.02
@@ -188,7 +188,7 @@
             pltpu.VMEM((tokens, width), bf16),
             pltpu.SemaphoreType.DMA((len(args),)),
         ],
-        compiler_params=pltpu.CompilerParams(vmem_limit_bytes=LIMIT << 20),
+        compiler_params=pltpu.CompilerParams(vmem_limit_bytes=LIMIT << 18),
         cost_estimate=pl.CostEstimate(
             flops=12_000_000_000, bytes_accessed=12_000_000, transcendentals=0
         ),
@@ -230,7 +230,8 @@
     def named(state, document):
         return jnp.where(counted, state, document).astype(bf16)
 
-    other = across(give)
+    other = across(give).astype(f32)
+    keep = lax.optimization_barrier(keep.astype(f32))
     early = jnp.where(core == 0, keep, other)
     late = jnp.where(core == 0, other, keep)
     chip = named(

time: 91.3 us -> 88.7 us (0.972)
  other arithmetic: 4.65 us -> 3.64 us
    convert_element_type x11, other arithmetic: 1.85 us -> 0.82 us  [add(): return sum((array.astype(f32) for array in arrays)).astype(bf16)]
    ppermute x2, waiting for transfers between devices: 2.75 us -> 1.81 us  [across(): return lax.ppermute(array, 'ctx', [(i, i ^ 1) for i in range(size)])]
    convert_element_type x0 -> x1, other arithmetic: none -> 0.92 us  [prior_states(): keep = lax.optimization_barrier(keep.astype(f32))]
  transfers between devices with their start and end apart: 21 -> 21, of which waited for: 16 -> 16; matrix products, arithmetic and copies ran while one was open for 1% -> 2% of each run, Pallas kernels for 0% -> 0%
where the time goes in v4:
time: 88.7 us; the launch traced here: 87.8 us
  waiting for transfers between devices  35.8 us (40%)
  starting transfers between devices  35.3 us (40%)
  Pallas kernels  12.9 us (15%)
  other arithmetic  3.64 us (4%)
    ppermute x14, starting transfers between devices, hop(): lax.ppermute(array, 'head', [(i, (i + step) % size) for i in range(size)])  25.9 us
    ppermute x14, waiting for transfers between devices, hop(): lax.ppermute(array, 'head', [(i, (i + step) % size) for i in range(size)])  19.6 us
    pallas_call x1, Pallas kernels, solve(): pl.pallas_call(functools.partial(solve_kernel, pieces), out_shape=[jax.Sh...  10.6 us
    ppermute x3, waiting for transfers between devices, along_x(): return lax.ppermute(array, 'ctx', [(i, target(i)) for i in range(size)])  8.07 us
    ppermute x2, waiting for transfers between devices, along_y(): lax.ppermute(array, 'ctx', [(i, (i + step * CORES * ROW) % size) for i in...  6.36 us
    ppermute x2, starting transfers between devices, along_y(): lax.ppermute(array, 'ctx', [(i, (i + step * CORES * ROW) % size) for i in...  4.55 us
    ppermute x3, starting transfers between devices, along_x(): return lax.ppermute(array, 'ctx', [(i, target(i)) for i in range(size)])  4.52 us
    pallas_call x1, Pallas kernels, shards(): pl.pallas_call(tails_kernel, out_shape=[jax.ShapeDtypeStruct((width + NOT...  2.37 us
  transfers between devices with their start and end apart: 21, of which 16 were waited for; matrix products, arithmetic and copies ran while one was open for 2% of the time, Pallas kernels for 0%

profile of v4, /device:TPU:96, one launch (start us, length us, event | category | flops | bytes accessed | tf_op | source)
XLA Modules:
  0.0 87.8 jit_solution(13092601667450732550)
XLA Ops:
  0.0 2.4 %tails.1 = (bf16[528,128]{1,0:T(8,128)(2,1)}, bf16[528,128]{1,0:T(8,128)(2,1)}, bf16[528,256]{1,0:T(8,128)(2,1)}) custom-call(bf16[256,512]{1,0:T(8,128)(2,1)} %refs_1_.1, bf16[256,512]{1,0:T(8,128)(2,1)} %refs_2_.1, s32[1,256]{1,0:T(1,128)} %bitcast.36), custom_call_target="tpu_custom_call" | custom-call | tf_op jit(solution)/shard_map/tails/pallas_call | solution.py:279
  2.4 0.0 collective-permute-start
  2.4 0.9 %convert_element_type.181 = f32[528,128]{1,0:T(8,128)S(1)} convert(bf16[528,128]{1,0:T(8,128)(2,1)} %get-tuple-element.30) | non-fusion elementwise | flops 67584 | bytes 405504 | tf_op jit(solution)/shard_map/prior_states/convert_element_type | solution.py:234
  3.3 0.6 collective-permute-done
  4.0 0.2 select_convert_fusion.2
  4.2 2.8 %collective-permute-start.3 = (bf16[528,128]{1,0:T(8,128)(2,1)S(1)}, bf16[528,128]{1,0:T(8,128)(2,1)S(1)}, u32[]{:S(2)}, u32[]{:S(2)}) collective-permute-start(bf16[528,128]{1,0:T(8,128)(2,1)S(1)} %select_convert_fusion.2), channel_id=1, source_target_pairs={{0,48},{8,56},{16,0},{24,8},{32,16},{40,24},{48,32},{56,40},{64,11... | collective-permute-start | bytes 405512 | tf_op jit(solution)/shard_map/prior_states/ppermute | solution.py:217
  7.0 0.8 collective-permute-start.2
  7.8 0.9 %collective-permute-start.1 = (bf16[528,128]{1,0:T(8,128)(2,1)S(1)}, bf16[528,128]{1,0:T(8,128)(2,1)S(1)}, u32[]{:S(2)}, u32[]{:S(2)}) collective-permute-start(bf16[528,128]{1,0:T(8,128)(2,1)S(1)} %select_convert_fusion.2), channel_id=1, source_target_pairs={{0,16},{8,24},{16,32},{24,40},{32,48},{40,56},{48,0},{56,8},{64,80... | collective-permute-start | bytes 405512 | tf_op jit(solution)/shard_map/prior_states/ppermute | solution.py:217
  8.7 4.4 %collective-permute-done.3 = bf16[528,128]{1,0:T(8,128)(2,1)S(1)} collective-permute-done((bf16[528,128]{1,0:T(8,128)(2,1)S(1)}, bf16[528,128]{1,0:T(8,128)(2,1)S(1)}, u32[]{:S(2)}, u32[]{:S(2)}) %collective-permute-start.3) | collective-permute-done | bytes 135200 | tf_op jit(solution)/shard_map/prior_states/ppermute | solution.py:217
  13.1 1.9 %collective-permute-done.2 = bf16[528,128]{1,0:T(8,128)(2,1)S(1)} collective-permute-done((bf16[528,128]{1,0:T(8,128)(2,1)S(1)}, bf16[528,128]{1,0:T(8,128)(2,1)S(1)}, u32[]{:S(2)}, u32[]{:S(2)}) %collective-permute-start.2) | collective-permute-done | bytes 135200 | tf_op jit(solution)/shard_map/prior_states/ppermute | solution.py:217
  15.0 1.8 %collective-permute-done.1 = bf16[528,128]{1,0:T(8,128)(2,1)S(1)} collective-permute-done((bf16[528,128]{1,0:T(8,128)(2,1)S(1)}, bf16[528,128]{1,0:T(8,128)(2,1)S(1)}, u32[]{:S(2)}, u32[]{:S(2)}) %collective-permute-start.1) | collective-permute-done | bytes 135200 | tf_op jit(solution)/shard_map/prior_states/ppermute | solution.py:217
  16.8 0.3 fusion.4
  17.1 1.7 %collective-permute-start.4 = (bf16[528,128]{1,0:T(8,128)(2,1)S(1)}, bf16[528,128]{1,0:T(8,128)(2,1)S(1)}, u32[]{:S(2)}, u32[]{:S(2)}) collective-permute-start(bf16[528,128]{1,0:T(8,128)(2,1)S(1)} %fusion.4), channel_id=1, source_target_pairs={{0,64},{8,72},{16,80},{24,88},{32,96},{40,104},{48,112},{56,120},{... | collective-permute-start | bytes 405512 | tf_op jit(solution)/shard_map/prior_states/ppermute | solution.py:220
  18.7 2.9 %collective-permute-start.5 = (bf16[528,128]{1,0:T(8,128)(2,1)S(1)}, bf16[528,128]{1,0:T(8,128)(2,1)S(1)}, u32[]{:S(2)}, u32[]{:S(2)}) collective-permute-start(bf16[528,128]{1,0:T(8,128)(2,1)S(1)} %fusion.4), channel_id=1, source_target_pairs={{0,128},{8,136},{16,144},{24,152},{32,160},{40,168},{48,176},{56,1... | collective-permute-start | bytes 405512 | tf_op jit(solution)/shard_map/prior_states/ppermute | solution.py:220
  21.6 2.3 %collective-permute-done.4 = bf16[528,128]{1,0:T(8,128)(2,1)S(1)} collective-permute-done((bf16[528,128]{1,0:T(8,128)(2,1)S(1)}, bf16[528,128]{1,0:T(8,128)(2,1)S(1)}, u32[]{:S(2)}, u32[]{:S(2)}) %collective-permute-start.4) | collective-permute-done | bytes 135200 | tf_op jit(solution)/shard_map/prior_states/ppermute | solution.py:220
  23.9 4.1 %collective-permute-done.5 = bf16[528,128]{1,0:T(8,128)(2,1)S(1)} collective-permute-done((bf16[528,128]{1,0:T(8,128)(2,1)S(1)}, bf16[528,128]{1,0:T(8,128)(2,1)S(1)}, u32[]{:S(2)}, u32[]{:S(2)}) %collective-permute-start.5) | collective-permute-done | bytes 135200 | tf_op jit(solution)/shard_map/prior_states/ppermute | solution.py:220
  28.0 0.4 broadcast_select_fusion
  28.4 0.3 collective-permute-start.6
  28.7 0.1 broadcast_select_fusion.1.refs_4_
  28.9 1.2 %collective-permute-done.6.refs_5_ = bf16[528,128]{1,0:T(8,128)(2,1)S(1)} collective-permute-done((bf16[528,128]{1,0:T(8,128)(2,1)S(1)}, bf16[528,128]{1,0:T(8,128)(2,1)S(1)}, u32[]{:S(2)}, u32[]{:S(2)}) %collective-permute-start.6) | collective-permute-done | bytes 135200 | tf_op jit(solution)/shard_map/prior_states/ppermute | solution.py:210
  30.0 10.6 %solve.1 = (bf16[32,4096]{1,0:T(8,128)(2,1)S(1)}, bf16[32,4096]{1,0:T(8,128)(2,1)S(1)}, bf16[32,4096]{1,0:T(8,128)(2,1)S(1)}, bf16[32,4096]{1,0:T(8,128)(2,1)S(1...) custom-call(bf16[256,512]{1,0:T(8,128)(2,1)} %refs_0_.1, ...), custom_call_target="tpu_custom_call" | custom-call | flops 12000000000 | bytes 12000000 | tf_op jit(solution)/shard_map/solve/pallas_call | solution.py:176
  40.6 3.2 %collective-permute-start.7 = (bf16[32,4096]{1,0:T(8,128)(2,1)S(1)}, bf16[32,4096]{1,0:T(8,128)(2,1)S(1)}, u32[]{:S(2)}, u32[]{:S(2)}) collective-permute-start(bf16[32,4096]{1,0:T(8,128)(2,1)S(1)} %get-tuple-element.31), channel_id=1, source_target_pairs={{0,1},{1,2},{2,3},{3,4},{4,5},{5,6},{6,7},{7,0},{8,9},{9,10},{10,1... | collective-permute-start | bytes 786440 | tf_op jit(solution)/shard_map/ring/ppermute | solution.py:301
  43.8 0.0 collective-permute-start.11
  43.8 3.2 %collective-permute-start.15 = (bf16[32,4096]{1,0:T(8,128)(2,1)S(1)}, bf16[32,4096]{1,0:T(8,128)(2,1)S(1)}, u32[]{:S(2)}, u32[]{:S(2)}) collective-permute-start(bf16[32,4096]{1,0:T(8,128)(2,1)S(1)} %get-tuple-element.39), channel_id=1, source_target_pairs={{0,1},{1,2},{2,3},{3,4},{4,5},{5,6},{6,7},{7,0},{8,9},{9,10},{10,1... | collective-permute-start | bytes 786440 | tf_op jit(solution)/shard_map/ring/ppermute | solution.py:301
  47.1 0.0 collective-permute-start.18
  47.1 3.4 %collective-permute-done.7 = bf16[32,4096]{1,0:T(8,128)(2,1)S(1)} collective-permute-done((bf16[32,4096]{1,0:T(8,128)(2,1)S(1)}, bf16[32,4096]{1,0:T(8,128)(2,1)S(1)}, u32[]{:S(2)}, u32[]{:S(2)}) %collective-permute-start.7) | collective-permute-done | bytes 262176 | tf_op jit(solution)/shard_map/ring/ppermute | solution.py:301
  50.5 0.1 add_convert_fusion.11
  50.6 4.0 %collective-permute-start.8 = (bf16[32,4096]{1,0:T(8,128)(2,1)S(1)}, bf16[32,4096]{1,0:T(8,128)(2,1)S(1)}, u32[]{:S(2)}, u32[]{:S(2)}) collective-permute-start(bf16[32,4096]{1,0:T(8,128)(2,1)S(1)} %add_convert_fusion.11), channel_id=1, source_target_pairs={{0,1},{1,2},{2,3},{3,4},{4,5},{5,6},{6,7},{7,0},{8,9},{9,10},{10,1... | collective-permute-start | bytes 786440 | tf_op jit(solution)/shard_map/ring/ppermute | solution.py:301
  54.6 0.0 collective-permute-done.11
  54.6 0.1 add_convert_fusion.8
  54.6 0.1 collective-permute-start.12
  54.7 1.4 %collective-permute-done.15 = bf16[32,4096]{1,0:T(8,128)(2,1)S(1)} collective-permute-done((bf16[32,4096]{1,0:T(8,128)(2,1)S(1)}, bf16[32,4096]{1,0:T(8,128)(2,1)S(1)}, u32[]{:S(2)}, u32[]{:S(2)}) %collective-permute-start.15) | collective-permute-done | bytes 262176 | tf_op jit(solution)/shard_map/ring/ppermute | solution.py:301
  56.1 0.1 add_convert_fusion.5
  56.2 3.8 %collective-permute-start.16 = (bf16[32,4096]{1,0:T(8,128)(2,1)S(1)}, bf16[32,4096]{1,0:T(8,128)(2,1)S(1)}, u32[]{:S(2)}, u32[]{:S(2)}) collective-permute-start(bf16[32,4096]{1,0:T(8,128)(2,1)S(1)} %add_convert_fusion.5), channel_id=1, source_target_pairs={{0,1},{1,2},{2,3},{3,4},{4,5},{5,6},{6,7},{7,0},{8,9},{9,10},{10,1... | collective-permute-start | bytes 786440 | tf_op jit(solution)/shard_map/ring/ppermute | solution.py:301
  59.9 0.0 collective-permute-done.18
  60.0 0.1 add_convert_fusion.3
  60.0 0.1 collective-permute-start.19
  60.1 1.6 %collective-permute-done.8 = bf16[32,4096]{1,0:T(8,128)(2,1)S(1)} collective-permute-done((bf16[32,4096]{1,0:T(8,128)(2,1)S(1)}, bf16[32,4096]{1,0:T(8,128)(2,1)S(1)}, u32[]{:S(2)}, u32[]{:S(2)}) %collective-permute-start.8) | collective-permute-done | bytes 262176 | tf_op jit(solution)/shard_map/ring/ppermute | solution.py:301
  61.7 0.1 add_convert_fusion.10
  61.8 3.8 %collective-permute-start.9 = (bf16[32,4096]{1,0:T(8,128)(2,1)S(1)}, bf16[32,4096]{1,0:T(8,128)(2,1)S(1)}, u32[]{:S(2)}, u32[]{:S(2)}) collective-permute-start(bf16[32,4096]{1,0:T(8,128)(2,1)S(1)} %add_convert_fusion.10), channel_id=1, source_target_pairs={{0,1},{1,2},{2,3},{3,4},{4,5},{5,6},{6,7},{7,0},{8,9},{9,10},{10,1... | collective-permute-start | bytes 786440 | tf_op jit(solution)/shard_map/ring/ppermute | solution.py:301
  65.6 0.0 collective-permute-done.12
  65.6 0.1 add_convert_fusion.7
  65.6 0.1 collective-permute-start.13
  65.7 1.6 %collective-permute-done.16 = bf16[32,4096]{1,0:T(8,128)(2,1)S(1)} collective-permute-done((bf16[32,4096]{1,0:T(8,128)(2,1)S(1)}, bf16[32,4096]{1,0:T(8,128)(2,1)S(1)}, u32[]{:S(2)}, u32[]{:S(2)}) %collective-permute-start.16) | collective-permute-done | bytes 262176 | tf_op jit(solution)/shard_map/ring/ppermute | solution.py:301
  67.3 0.1 add_convert_fusion.4
  67.4 3.8 %collective-permute-start.17 = (bf16[32,4096]{1,0:T(8,128)(2,1)S(1)}, bf16[32,4096]{1,0:T(8,128)(2,1)S(1)}, u32[]{:S(2)}, u32[]{:S(2)}) collective-permute-start(bf16[32,4096]{1,0:T(8,128)(2,1)S(1)} %add_convert_fusion.4), channel_id=1, source_target_pairs={{0,1},{1,2},{2,3},{3,4},{4,5},{5,6},{6,7},{7,0},{8,9},{9,10},{10,1... | collective-permute-start | bytes 786440 | tf_op jit(solution)/shard_map/ring/ppermute | solution.py:301
  71.2 0.0 collective-permute-done.19
  71.2 0.1 add_convert_fusion.2
  71.3 0.1 collective-permute-start.20
  71.3 1.6 %collective-permute-done.9 = bf16[32,4096]{1,0:T(8,128)(2,1)S(1)} collective-permute-done((bf16[32,4096]{1,0:T(8,128)(2,1)S(1)}, bf16[32,4096]{1,0:T(8,128)(2,1)S(1)}, u32[]{:S(2)}, u32[]{:S(2)}) %collective-permute-start.9) | collective-permute-done | bytes 262176 | tf_op jit(solution)/shard_map/ring/ppermute | solution.py:301
  73.0 0.1 add_convert_fusion.9
  73.0 3.8 %collective-permute-start.10 = (bf16[32,4096]{1,0:T(8,128)(2,1)S(1)}, bf16[32,4096]{1,0:T(8,128)(2,1)S(1)}, u32[]{:S(2)}, u32[]{:S(2)}) collective-permute-start(bf16[32,4096]{1,0:T(8,128)(2,1)S(1)} %add_convert_fusion.9), channel_id=1, source_target_pairs={{0,1},{1,2},{2,3},{3,4},{4,5},{5,6},{6,7},{7,0},{8,9},{9,10},{10,1... | collective-permute-start | bytes 786440 | tf_op jit(solution)/shard_map/ring/ppermute | solution.py:301
  76.8 0.0 collective-permute-done.13
  76.8 0.1 add_convert_fusion.6
  76.9 0.1 collective-permute-start.14
  77.0 1.6 %collective-permute-done.17 = bf16[32,4096]{1,0:T(8,128)(2,1)S(1)} collective-permute-done((bf16[32,4096]{1,0:T(8,128)(2,1)S(1)}, bf16[32,4096]{1,0:T(8,128)(2,1)S(1)}, u32[]{:S(2)}, u32[]{:S(2)}) %collective-permute-start.17) | collective-permute-done | bytes 262176 | tf_op jit(solution)/shard_map/ring/ppermute | solution.py:301
  78.6 3.7 %collective-permute-done.20 = bf16[32,4096]{1,0:T(8,128)(2,1)S(1)} collective-permute-done((bf16[32,4096]{1,0:T(8,128)(2,1)S(1)}, bf16[32,4096]{1,0:T(8,128)(2,1)S(1)}, u32[]{:S(2)}, u32[]{:S(2)}) %collective-permute-start.20) | collective-permute-done | bytes 262176 | tf_op jit(solution)/shard_map/ring/ppermute | solution.py:301
  82.3 1.1 %collective-permute-done.10 = bf16[32,4096]{1,0:T(8,128)(2,1)S(1)} collective-permute-done((bf16[32,4096]{1,0:T(8,128)(2,1)S(1)}, bf16[32,4096]{1,0:T(8,128)(2,1)S(1)}, u32[]{:S(2)}, u32[]{:S(2)}) %collective-permute-start.10) | collective-permute-done | bytes 262176 | tf_op jit(solution)/shard_map/ring/ppermute | solution.py:301
  83.4 3.4 %collective-permute-done.14 = bf16[32,4096]{1,0:T(8,128)(2,1)S(1)} collective-permute-done((bf16[32,4096]{1,0:T(8,128)(2,1)S(1)}, bf16[32,4096]{1,0:T(8,128)(2,1)S(1)}, u32[]{:S(2)}, u32[]{:S(2)}) %collective-permute-start.14) | collective-permute-done | bytes 262176 | tf_op jit(solution)/shard_map/ring/ppermute | solution.py:301
  86.8 0.2 add_convert_fusion
  87.0 0.8 pad_maximum_fusion
  (9 shorter events, 0.1 us)
Async XLA Ops:
  2.4 1.6 %collective-permute-start = (bf16[528,128]{1,0:T(8,128)(2,1)}, bf16[528,128]{1,0:T(8,128)(2,1)S(1)}, u32[]{:S(2)}, u32[]{:S(2)}) collective-permute-start(bf16[528,128]{1,0:T(8,128)(2,1)} %get-tuple-element.29), channel_id=1, source_target_pairs={{0,8},{8,0},{16,24},{24,16},{32,40},{40,32},{48,56},{56,48},{64,72... | collective-permute-start | bytes 405512 | tf_op jit(solution)/shard_map/prior_states/ppermute | solution.py:210
  4.2 8.9 %collective-permute-start.3 = (bf16[528,128]{1,0:T(8,128)(2,1)S(1)}, bf16[528,128]{1,0:T(8,128)(2,1)S(1)}, u32[]{:S(2)}, u32[]{:S(2)}) collective-permute-start(bf16[528,128]{1,0:T(8,128)(2,1)S(1)} %select_convert_fusion.2), channel_id=1, source_target_pairs={{0,48},{8,56},{16,0},{24,8},{32,16},{40,24},{48,32},{56,40},{64,11... | collective-permute-start | bytes 405512 | tf_op jit(solution)/shard_map/prior_states/ppermute | solution.py:217
  7.0 8.0 %collective-permute-start.2 = (bf16[528,128]{1,0:T(8,128)(2,1)S(1)}, bf16[528,128]{1,0:T(8,128)(2,1)S(1)}, u32[]{:S(2)}, u32[]{:S(2)}) collective-permute-start(bf16[528,128]{1,0:T(8,128)(2,1)S(1)} %select_convert_fusion.2), channel_id=1, source_target_pairs={{0,32},{8,40},{16,48},{24,56},{32,0},{40,8},{48,16},{56,24},{64,96... | collective-permute-start | bytes 405512 | tf_op jit(solution)/shard_map/prior_states/ppermute | solution.py:217
  7.8 9.0 %collective-permute-start.1 = (bf16[528,128]{1,0:T(8,128)(2,1)S(1)}, bf16[528,128]{1,0:T(8,128)(2,1)S(1)}, u32[]{:S(2)}, u32[]{:S(2)}) collective-permute-start(bf16[528,128]{1,0:T(8,128)(2,1)S(1)} %select_convert_fusion.2), channel_id=1, source_target_pairs={{0,16},{8,24},{16,32},{24,40},{32,48},{40,56},{48,0},{56,8},{64,80... | collective-permute-start | bytes 405512 | tf_op jit(solution)/shard_map/prior_states/ppermute | solution.py:217
  17.1 6.9 %collective-permute-start.4 = (bf16[528,128]{1,0:T(8,128)(2,1)S(1)}, bf16[528,128]{1,0:T(8,128)(2,1)S(1)}, u32[]{:S(2)}, u32[]{:S(2)}) collective-permute-start(bf16[528,128]{1,0:T(8,128)(2,1)S(1)} %fusion.4), channel_id=1, source_target_pairs={{0,64},{8,72},{16,80},{24,88},{32,96},{40,104},{48,112},{56,120},{... | collective-permute-start | bytes 405512 | tf_op jit(solution)/shard_map/prior_states/ppermute | solution.py:220
  18.7 9.3 %collective-permute-start.5 = (bf16[528,128]{1,0:T(8,128)(2,1)S(1)}, bf16[528,128]{1,0:T(8,128)(2,1)S(1)}, u32[]{:S(2)}, u32[]{:S(2)}) collective-permute-start(bf16[528,128]{1,0:T(8,128)(2,1)S(1)} %fusion.4), channel_id=1, source_target_pairs={{0,128},{8,136},{16,144},{24,152},{32,160},{40,168},{48,176},{56,1... | collective-permute-start | bytes 405512 | tf_op jit(solution)/shard_map/prior_states/ppermute | solution.py:220
  28.4 1.6 %collective-permute-start.6 = (bf16[528,128]{1,0:T(8,128)(2,1)S(1)}, bf16[528,128]{1,0:T(8,128)(2,1)S(1)}, u32[]{:S(2)}, u32[]{:S(2)}) collective-permute-start(bf16[528,128]{1,0:T(8,128)(2,1)S(1)} %get-tuple-element.51), channel_id=1, source_target_pairs={{0,8},{8,0},{16,24},{24,16},{32,40},{40,32},{48,56},{56,48},{64,72... | collective-permute-start | bytes 405512 | tf_op jit(solution)/shard_map/prior_states/ppermute | solution.py:210
  40.6 9.9 %collective-permute-start.7 = (bf16[32,4096]{1,0:T(8,128)(2,1)S(1)}, bf16[32,4096]{1,0:T(8,128)(2,1)S(1)}, u32[]{:S(2)}, u32[]{:S(2)}) collective-permute-start(bf16[32,4096]{1,0:T(8,128)(2,1)S(1)} %get-tuple-element.31), channel_id=1, source_target_pairs={{0,1},{1,2},{2,3},{3,4},{4,5},{5,6},{6,7},{7,0},{8,9},{9,10},{10,1... | collective-permute-start | bytes 786440 | tf_op jit(solution)/shard_map/ring/ppermute | solution.py:301
  43.8 10.7 %collective-permute-start.11 = (bf16[32,4096]{1,0:T(8,128)(2,1)S(1)}, bf16[32,4096]{1,0:T(8,128)(2,1)S(1)}, u32[]{:S(2)}, u32[]{:S(2)}) collective-permute-start(bf16[32,4096]{1,0:T(8,128)(2,1)S(1)} %get-tuple-element.35), channel_id=1, source_target_pairs={{0,7},{1,0},{2,1},{3,2},{4,3},{5,4},{6,5},{7,6},{8,15},{9,8},{10,9... | collective-permute-start | bytes 786440 | tf_op jit(solution)/shard_map/ring/ppermute | solution.py:301
  43.8 12.3 %collective-permute-start.15 = (bf16[32,4096]{1,0:T(8,128)(2,1)S(1)}, bf16[32,4096]{1,0:T(8,128)(2,1)S(1)}, u32[]{:S(2)}, u32[]{:S(2)}) collective-permute-start(bf16[32,4096]{1,0:T(8,128)(2,1)S(1)} %get-tuple-element.39), channel_id=1, source_target_pairs={{0,1},{1,2},{2,3},{3,4},{4,5},{5,6},{6,7},{7,0},{8,9},{9,10},{10,1... | collective-permute-start | bytes 786440 | tf_op jit(solution)/shard_map/ring/ppermute | solution.py:301
  47.1 12.9 %collective-permute-start.18 = (bf16[32,4096]{1,0:T(8,128)(2,1)S(1)}, bf16[32,4096]{1,0:T(8,128)(2,1)S(1)}, u32[]{:S(2)}, u32[]{:S(2)}) collective-permute-start(bf16[32,4096]{1,0:T(8,128)(2,1)S(1)} %get-tuple-element.42), channel_id=1, source_target_pairs={{0,7},{1,0},{2,1},{3,2},{4,3},{5,4},{6,5},{7,6},{8,15},{9,8},{10,9... | collective-permute-start | bytes 786440 | tf_op jit(solution)/shard_map/ring/ppermute | solution.py:301
  50.6 11.2 %collective-permute-start.8 = (bf16[32,4096]{1,0:T(8,128)(2,1)S(1)}, bf16[32,4096]{1,0:T(8,128)(2,1)S(1)}, u32[]{:S(2)}, u32[]{:S(2)}) collective-permute-start(bf16[32,4096]{1,0:T(8,128)(2,1)S(1)} %add_convert_fusion.11), channel_id=1, source_target_pairs={{0,1},{1,2},{2,3},{3,4},{4,5},{5,6},{6,7},{7,0},{8,9},{9,10},{10,1... | collective-permute-start | bytes 786440 | tf_op jit(solution)/shard_map/ring/ppermute | solution.py:301
  54.6 10.9 %collective-permute-start.12 = (bf16[32,4096]{1,0:T(8,128)(2,1)S(1)}, bf16[32,4096]{1,0:T(8,128)(2,1)S(1)}, u32[]{:S(2)}, u32[]{:S(2)}) collective-permute-start(bf16[32,4096]{1,0:T(8,128)(2,1)S(1)} %add_convert_fusion.8), channel_id=1, source_target_pairs={{0,7},{1,0},{2,1},{3,2},{4,3},{5,4},{6,5},{7,6},{8,15},{9,8},{10,9... | collective-permute-start | bytes 786440 | tf_op jit(solution)/shard_map/ring/ppermute | solution.py:301
  56.2 11.2 %collective-permute-start.16 = (bf16[32,4096]{1,0:T(8,128)(2,1)S(1)}, bf16[32,4096]{1,0:T(8,128)(2,1)S(1)}, u32[]{:S(2)}, u32[]{:S(2)}) collective-permute-start(bf16[32,4096]{1,0:T(8,128)(2,1)S(1)} %add_convert_fusion.5), channel_id=1, source_target_pairs={{0,1},{1,2},{2,3},{3,4},{4,5},{5,6},{6,7},{7,0},{8,9},{9,10},{10,1... | collective-permute-start | bytes 786440 | tf_op jit(solution)/shard_map/ring/ppermute | solution.py:301
  60.0 11.2 %collective-permute-start.19 = (bf16[32,4096]{1,0:T(8,128)(2,1)S(1)}, bf16[32,4096]{1,0:T(8,128)(2,1)S(1)}, u32[]{:S(2)}, u32[]{:S(2)}) collective-permute-start(bf16[32,4096]{1,0:T(8,128)(2,1)S(1)} %add_convert_fusion.3), channel_id=1, source_target_pairs={{0,7},{1,0},{2,1},{3,2},{4,3},{5,4},{6,5},{7,6},{8,15},{9,8},{10,9... | collective-permute-start | bytes 786440 | tf_op jit(solution)/shard_map/ring/ppermute | solution.py:301
  61.8 11.2 %collective-permute-start.9 = (bf16[32,4096]{1,0:T(8,128)(2,1)S(1)}, bf16[32,4096]{1,0:T(8,128)(2,1)S(1)}, u32[]{:S(2)}, u32[]{:S(2)}) collective-permute-start(bf16[32,4096]{1,0:T(8,128)(2,1)S(1)} %add_convert_fusion.10), channel_id=1, source_target_pairs={{0,1},{1,2},{2,3},{3,4},{4,5},{5,6},{6,7},{7,0},{8,9},{9,10},{10,1... | collective-permute-start | bytes 786440 | tf_op jit(solution)/shard_map/ring/ppermute | solution.py:301
  65.6 11.2 %collective-permute-start.13 = (bf16[32,4096]{1,0:T(8,128)(2,1)S(1)}, bf16[32,4096]{1,0:T(8,128)(2,1)S(1)}, u32[]{:S(2)}, u32[]{:S(2)}) collective-permute-start(bf16[32,4096]{1,0:T(8,128)(2,1)S(1)} %add_convert_fusion.7), channel_id=1, source_target_pairs={{0,7},{1,0},{2,1},{3,2},{4,3},{5,4},{6,5},{7,6},{8,15},{9,8},{10,9... | collective-permute-start | bytes 786440 | tf_op jit(solution)/shard_map/ring/ppermute | solution.py:301
  67.4 11.2 %collective-permute-start.17 = (bf16[32,4096]{1,0:T(8,128)(2,1)S(1)}, bf16[32,4096]{1,0:T(8,128)(2,1)S(1)}, u32[]{:S(2)}, u32[]{:S(2)}) collective-permute-start(bf16[32,4096]{1,0:T(8,128)(2,1)S(1)} %add_convert_fusion.4), channel_id=1, source_target_pairs={{0,1},{1,2},{2,3},{3,4},{4,5},{5,6},{6,7},{7,0},{8,9},{9,10},{10,1... | collective-permute-start | bytes 786440 | tf_op jit(solution)/shard_map/ring/ppermute | solution.py:301
  71.3 11.1 %collective-permute-start.20 = (bf16[32,4096]{1,0:T(8,128)(2,1)S(1)}, bf16[32,4096]{1,0:T(8,128)(2,1)S(1)}, u32[]{:S(2)}, u32[]{:S(2)}) collective-permute-start(bf16[32,4096]{1,0:T(8,128)(2,1)S(1)} %add_convert_fusion.2), channel_id=1, source_target_pairs={{0,7},{1,0},{2,1},{3,2},{4,3},{5,4},{6,5},{7,6},{8,15},{9,8},{10,9... | collective-permute-start | bytes 786440 | tf_op jit(solution)/shard_map/ring/ppermute | solution.py:301
  73.0 10.4 %collective-permute-start.10 = (bf16[32,4096]{1,0:T(8,128)(2,1)S(1)}, bf16[32,4096]{1,0:T(8,128)(2,1)S(1)}, u32[]{:S(2)}, u32[]{:S(2)}) collective-permute-start(bf16[32,4096]{1,0:T(8,128)(2,1)S(1)} %add_convert_fusion.9), channel_id=1, source_target_pairs={{0,1},{1,2},{2,3},{3,4},{4,5},{5,6},{6,7},{7,0},{8,9},{9,10},{10,1... | collective-permute-start | bytes 786440 | tf_op jit(solution)/shard_map/ring/ppermute | solution.py:301
  76.9 10.0 %collective-permute-start.14 = (bf16[32,4096]{1,0:T(8,128)(2,1)S(1)}, bf16[32,4096]{1,0:T(8,128)(2,1)S(1)}, u32[]{:S(2)}, u32[]{:S(2)}) collective-permute-start(bf16[32,4096]{1,0:T(8,128)(2,1)S(1)} %add_convert_fusion.6), channel_id=1, source_target_pairs={{0,7},{1,0},{2,1},{3,2},{4,3},{5,4},{6,5},{7,6},{8,15},{9,8},{10,9... | collective-permute-start | bytes 786440 | tf_op jit(solution)/shard_map/ring/ppermute | solution.py:301

commit v5 on v4

--- a/solution.py
+++ b/solution.py
@@ -79,14 +79,15 @@
     outs, refs = refs[: len(pieces)], refs[len(pieces) :]
     held, (right, weight, p_ref, r_ref, x_ref, y_ref, sems) = refs[:7], refs[7:]
     loads = [pltpu.make_async_copy(a, b, sems.at[i]) for i, (a, b) in enumerate(zip(hbm, held))]
-    for load in loads:
+    q_load, k_load, v_load, kt_load, mine_load, back_load, w_load = loads
+    for load in (kt_load, mine_load, back_load, q_load, k_load, v_load, w_load):
         load.start()
     q_ref, k_ref, v_ref, kt_ref, mine_ref, back_ref, w_vmem = held
     tokens, width = q_ref.shape
     heads = width // DH
     share = tokens // N_HEAD
-    for load in loads[:-1]:
-        load.wait()
+    kt_load.wait()
+    mine_load.wait()
 
     first_core = lax.rem(lax.axis_index("ctx"), CORES) == 0
     doc = kt_ref[width : width + NOTE, :].astype(f32)[:1]
@@ -104,6 +105,8 @@
     prior_inverse = prior * inverse
     inside_inverse = inside * jnp.concatenate([inverse] * (tokens // DH), axis=1)
 
+    back_load.wait()
+    q_load.wait()
     scales = []
     for h in range(heads):
         cols = slice(h * DH, (h + 1) * DH)
@@ -127,6 +130,7 @@
         both = dot(split(field), right[h])
         return dot((both[:, :tokens] * times).astype(bf16), rows), both[:, tokens:]
 
+    k_load.wait()
     factor = radius / center
     for _ in range(ITERS):
         factor_new = 1.0 / (2.0 * center / radius - factor)
@@ -140,6 +144,7 @@
             x_ref[h] = x_ref[h] + p
         factor = factor_new
 
+    v_load.wait()
     for h in range(heads):
         cols = slice(h * DH, (h + 1) * DH)
         scale = scales[h]
@@ -158,7 +163,7 @@
         ],
         axis=0,
     )
-    loads[-1].wait()
+    w_load.wait()
     model = w_vmem.shape[1]
     tile = 1024
     for c in range(0, model, tile):

time: 88.7 us -> 88.5 us (level)
  no operation moved by 1% of the time
where the time goes in v5:
time: 88.5 us; the launch traced here: 87.7 us
  waiting for transfers between devices  35.8 us (40%)
  starting transfers between devices  35.3 us (40%)
  Pallas kernels  12.8 us (14%)
  other arithmetic  3.64 us (4%)
    ppermute x14, starting transfers between devices, hop(): lax.ppermute(array, 'head', [(i, (i + step) % size) for i in range(size)])  25.9 us
    ppermute x14, waiting for transfers between devices, hop(): lax.ppermute(array, 'head', [(i, (i + step) % size) for i in range(size)])  19.6 us
    pallas_call x1, Pallas kernels, solve(): pl.pallas_call(functools.partial(solve_kernel, pieces), out_shape=[jax.Sh...  10.4 us
    ppermute x3, waiting for transfers between devices, along_x(): return lax.ppermute(array, 'ctx', [(i, target(i)) for i in range(size)])  8.07 us
    ppermute x2, waiting for transfers between devices, along_y(): lax.ppermute(array, 'ctx', [(i, (i + step * CORES * ROW) % size) for i in...  6.36 us
    ppermute x2, starting transfers between devices, along_y(): lax.ppermute(array, 'ctx', [(i, (i + step * CORES * ROW) % size) for i in...  4.55 us
    ppermute x3, starting transfers between devices, along_x(): return lax.ppermute(array, 'ctx', [(i, target(i)) for i in range(size)])  4.52 us
    pallas_call x1, Pallas kernels, shards(): pl.pallas_call(tails_kernel, out_shape=[jax.ShapeDtypeStruct((width + NOT...  2.37 us
  transfers between devices with their start and end apart: 21, of which 16 were waited for; matrix products, arithmetic and copies ran while one was open for 2% of the time, Pallas kernels for 0%

profile of v5, /device:TPU:96, one launch (start us, length us, event | category | flops | bytes accessed | tf_op | source)
XLA Modules:
  0.0 87.7 jit_solution(11811779841048187266)
XLA Ops:
  0.0 2.4 %tails.1 = (bf16[528,128]{1,0:T(8,128)(2,1)}, bf16[528,128]{1,0:T(8,128)(2,1)}, bf16[528,256]{1,0:T(8,128)(2,1)}) custom-call(bf16[256,512]{1,0:T(8,128)(2,1)} %refs_1_.1, bf16[256,512]{1,0:T(8,128)(2,1)} %refs_2_.1, s32[1,256]{1,0:T(1,128)} %bitcast.36), custom_call_target="tpu_custom_call" | custom-call | tf_op jit(solution)/shard_map/tails/pallas_call | solution.py:284
  2.4 0.0 collective-permute-start
  2.4 0.9 %convert_element_type.181 = f32[528,128]{1,0:T(8,128)S(1)} convert(bf16[528,128]{1,0:T(8,128)(2,1)} %get-tuple-element.30) | non-fusion elementwise | flops 67584 | bytes 405504 | tf_op jit(solution)/shard_map/prior_states/convert_element_type | solution.py:239
  3.3 0.6 collective-permute-done
  4.0 0.2 select_convert_fusion.2
  4.2 2.8 %collective-permute-start.3 = (bf16[528,128]{1,0:T(8,128)(2,1)S(1)}, bf16[528,128]{1,0:T(8,128)(2,1)S(1)}, u32[]{:S(2)}, u32[]{:S(2)}) collective-permute-start(bf16[528,128]{1,0:T(8,128)(2,1)S(1)} %select_convert_fusion.2), channel_id=1, source_target_pairs={{0,48},{8,56},{16,0},{24,8},{32,16},{40,24},{48,32},{56,40},{64,11... | collective-permute-start | bytes 405512 | tf_op jit(solution)/shard_map/prior_states/ppermute | solution.py:222
  7.0 0.8 collective-permute-start.2
  7.8 0.9 %collective-permute-start.1 = (bf16[528,128]{1,0:T(8,128)(2,1)S(1)}, bf16[528,128]{1,0:T(8,128)(2,1)S(1)}, u32[]{:S(2)}, u32[]{:S(2)}) collective-permute-start(bf16[528,128]{1,0:T(8,128)(2,1)S(1)} %select_convert_fusion.2), channel_id=1, source_target_pairs={{0,16},{8,24},{16,32},{24,40},{32,48},{40,56},{48,0},{56,8},{64,80... | collective-permute-start | bytes 405512 | tf_op jit(solution)/shard_map/prior_states/ppermute | solution.py:222
  8.7 4.4 %collective-permute-done.3 = bf16[528,128]{1,0:T(8,128)(2,1)S(1)} collective-permute-done((bf16[528,128]{1,0:T(8,128)(2,1)S(1)}, bf16[528,128]{1,0:T(8,128)(2,1)S(1)}, u32[]{:S(2)}, u32[]{:S(2)}) %collective-permute-start.3) | collective-permute-done | bytes 135200 | tf_op jit(solution)/shard_map/prior_states/ppermute | solution.py:222
  13.1 1.9 %collective-permute-done.2 = bf16[528,128]{1,0:T(8,128)(2,1)S(1)} collective-permute-done((bf16[528,128]{1,0:T(8,128)(2,1)S(1)}, bf16[528,128]{1,0:T(8,128)(2,1)S(1)}, u32[]{:S(2)}, u32[]{:S(2)}) %collective-permute-start.2) | collective-permute-done | bytes 135200 | tf_op jit(solution)/shard_map/prior_states/ppermute | solution.py:222
  15.0 1.8 %collective-permute-done.1 = bf16[528,128]{1,0:T(8,128)(2,1)S(1)} collective-permute-done((bf16[528,128]{1,0:T(8,128)(2,1)S(1)}, bf16[528,128]{1,0:T(8,128)(2,1)S(1)}, u32[]{:S(2)}, u32[]{:S(2)}) %collective-permute-start.1) | collective-permute-done | bytes 135200 | tf_op jit(solution)/shard_map/prior_states/ppermute | solution.py:222
  16.8 0.3 fusion.4
  17.1 1.7 %collective-permute-start.4 = (bf16[528,128]{1,0:T(8,128)(2,1)S(1)}, bf16[528,128]{1,0:T(8,128)(2,1)S(1)}, u32[]{:S(2)}, u32[]{:S(2)}) collective-permute-start(bf16[528,128]{1,0:T(8,128)(2,1)S(1)} %fusion.4), channel_id=1, source_target_pairs={{0,64},{8,72},{16,80},{24,88},{32,96},{40,104},{48,112},{56,120},{... | collective-permute-start | bytes 405512 | tf_op jit(solution)/shard_map/prior_states/ppermute | solution.py:225
  18.7 2.9 %collective-permute-start.5 = (bf16[528,128]{1,0:T(8,128)(2,1)S(1)}, bf16[528,128]{1,0:T(8,128)(2,1)S(1)}, u32[]{:S(2)}, u32[]{:S(2)}) collective-permute-start(bf16[528,128]{1,0:T(8,128)(2,1)S(1)} %fusion.4), channel_id=1, source_target_pairs={{0,128},{8,136},{16,144},{24,152},{32,160},{40,168},{48,176},{56,1... | collective-permute-start | bytes 405512 | tf_op jit(solution)/shard_map/prior_states/ppermute | solution.py:225
  21.6 2.3 %collective-permute-done.4 = bf16[528,128]{1,0:T(8,128)(2,1)S(1)} collective-permute-done((bf16[528,128]{1,0:T(8,128)(2,1)S(1)}, bf16[528,128]{1,0:T(8,128)(2,1)S(1)}, u32[]{:S(2)}, u32[]{:S(2)}) %collective-permute-start.4) | collective-permute-done | bytes 135200 | tf_op jit(solution)/shard_map/prior_states/ppermute | solution.py:225
  23.9 4.1 %collective-permute-done.5 = bf16[528,128]{1,0:T(8,128)(2,1)S(1)} collective-permute-done((bf16[528,128]{1,0:T(8,128)(2,1)S(1)}, bf16[528,128]{1,0:T(8,128)(2,1)S(1)}, u32[]{:S(2)}, u32[]{:S(2)}) %collective-permute-start.5) | collective-permute-done | bytes 135200 | tf_op jit(solution)/shard_map/prior_states/ppermute | solution.py:225
  28.0 0.4 broadcast_select_fusion
  28.4 0.3 collective-permute-start.6
  28.7 0.1 broadcast_select_fusion.1.refs_4_
  28.9 1.2 %collective-permute-done.6.refs_5_ = bf16[528,128]{1,0:T(8,128)(2,1)S(1)} collective-permute-done((bf16[528,128]{1,0:T(8,128)(2,1)S(1)}, bf16[528,128]{1,0:T(8,128)(2,1)S(1)}, u32[]{:S(2)}, u32[]{:S(2)}) %collective-permute-start.6) | collective-permute-done | bytes 135200 | tf_op jit(solution)/shard_map/prior_states/ppermute | solution.py:215
  30.0 10.4 %solve.1 = (bf16[32,4096]{1,0:T(8,128)(2,1)S(1)}, bf16[32,4096]{1,0:T(8,128)(2,1)S(1)}, bf16[32,4096]{1,0:T(8,128)(2,1)S(1)}, bf16[32,4096]{1,0:T(8,128)(2,1)S(1...) custom-call(bf16[256,512]{1,0:T(8,128)(2,1)} %refs_0_.1, ...), custom_call_target="tpu_custom_call" | custom-call | flops 12000000000 | bytes 12000000 | tf_op jit(solution)/shard_map/solve/pallas_call | solution.py:181
  40.4 3.2 %collective-permute-start.7 = (bf16[32,4096]{1,0:T(8,128)(2,1)S(1)}, bf16[32,4096]{1,0:T(8,128)(2,1)S(1)}, u32[]{:S(2)}, u32[]{:S(2)}) collective-permute-start(bf16[32,4096]{1,0:T(8,128)(2,1)S(1)} %get-tuple-element.31), channel_id=1, source_target_pairs={{0,1},{1,2},{2,3},{3,4},{4,5},{5,6},{6,7},{7,0},{8,9},{9,10},{10,1... | collective-permute-start | bytes 786440 | tf_op jit(solution)/shard_map/ring/ppermute | solution.py:306
  43.6 0.0 collective-permute-start.11
  43.7 3.2 %collective-permute-start.15 = (bf16[32,4096]{1,0:T(8,128)(2,1)S(1)}, bf16[32,4096]{1,0:T(8,128)(2,1)S(1)}, u32[]{:S(2)}, u32[]{:S(2)}) collective-permute-start(bf16[32,4096]{1,0:T(8,128)(2,1)S(1)} %get-tuple-element.39), channel_id=1, source_target_pairs={{0,1},{1,2},{2,3},{3,4},{4,5},{5,6},{6,7},{7,0},{8,9},{9,10},{10,1... | collective-permute-start | bytes 786440 | tf_op jit(solution)/shard_map/ring/ppermute | solution.py:306
  46.9 0.0 collective-permute-start.18
  46.9 3.4 %collective-permute-done.7 = bf16[32,4096]{1,0:T(8,128)(2,1)S(1)} collective-permute-done((bf16[32,4096]{1,0:T(8,128)(2,1)S(1)}, bf16[32,4096]{1,0:T(8,128)(2,1)S(1)}, u32[]{:S(2)}, u32[]{:S(2)}) %collective-permute-start.7) | collective-permute-done | bytes 262176 | tf_op jit(solution)/shard_map/ring/ppermute | solution.py:306
  50.3 0.1 add_convert_fusion.11
  50.4 4.0 %collective-permute-start.8 = (bf16[32,4096]{1,0:T(8,128)(2,1)S(1)}, bf16[32,4096]{1,0:T(8,128)(2,1)S(1)}, u32[]{:S(2)}, u32[]{:S(2)}) collective-permute-start(bf16[32,4096]{1,0:T(8,128)(2,1)S(1)} %add_convert_fusion.11), channel_id=1, source_target_pairs={{0,1},{1,2},{2,3},{3,4},{4,5},{5,6},{6,7},{7,0},{8,9},{9,10},{10,1... | collective-permute-start | bytes 786440 | tf_op jit(solution)/shard_map/ring/ppermute | solution.py:306
  54.4 0.0 collective-permute-done.11
  54.4 0.1 add_convert_fusion.8
  54.4 0.1 collective-permute-start.12
  54.5 1.4 %collective-permute-done.15 = bf16[32,4096]{1,0:T(8,128)(2,1)S(1)} collective-permute-done((bf16[32,4096]{1,0:T(8,128)(2,1)S(1)}, bf16[32,4096]{1,0:T(8,128)(2,1)S(1)}, u32[]{:S(2)}, u32[]{:S(2)}) %collective-permute-start.15) | collective-permute-done | bytes 262176 | tf_op jit(solution)/shard_map/ring/ppermute | solution.py:306
  55.9 0.1 add_convert_fusion.5
  56.0 3.8 %collective-permute-start.16 = (bf16[32,4096]{1,0:T(8,128)(2,1)S(1)}, bf16[32,4096]{1,0:T(8,128)(2,1)S(1)}, u32[]{:S(2)}, u32[]{:S(2)}) collective-permute-start(bf16[32,4096]{1,0:T(8,128)(2,1)S(1)} %add_convert_fusion.5), channel_id=1, source_target_pairs={{0,1},{1,2},{2,3},{3,4},{4,5},{5,6},{6,7},{7,0},{8,9},{9,10},{10,1... | collective-permute-start | bytes 786440 | tf_op jit(solution)/shard_map/ring/ppermute | solution.py:306
  59.8 0.0 collective-permute-done.18
  59.8 0.1 add_convert_fusion.3
  59.8 0.1 collective-permute-start.19
  59.9 1.6 %collective-permute-done.8 = bf16[32,4096]{1,0:T(8,128)(2,1)S(1)} collective-permute-done((bf16[32,4096]{1,0:T(8,128)(2,1)S(1)}, bf16[32,4096]{1,0:T(8,128)(2,1)S(1)}, u32[]{:S(2)}, u32[]{:S(2)}) %collective-permute-start.8) | collective-permute-done | bytes 262176 | tf_op jit(solution)/shard_map/ring/ppermute | solution.py:306
  61.6 0.1 add_convert_fusion.10
  61.6 3.8 %collective-permute-start.9 = (bf16[32,4096]{1,0:T(8,128)(2,1)S(1)}, bf16[32,4096]{1,0:T(8,128)(2,1)S(1)}, u32[]{:S(2)}, u32[]{:S(2)}) collective-permute-start(bf16[32,4096]{1,0:T(8,128)(2,1)S(1)} %add_convert_fusion.10), channel_id=1, source_target_pairs={{0,1},{1,2},{2,3},{3,4},{4,5},{5,6},{6,7},{7,0},{8,9},{9,10},{10,1... | collective-permute-start | bytes 786440 | tf_op jit(solution)/shard_map/ring/ppermute | solution.py:306
  65.4 0.0 collective-permute-done.12
  65.4 0.1 add_convert_fusion.7
  65.5 0.1 collective-permute-start.13
  65.5 1.6 %collective-permute-done.16 = bf16[32,4096]{1,0:T(8,128)(2,1)S(1)} collective-permute-done((bf16[32,4096]{1,0:T(8,128)(2,1)S(1)}, bf16[32,4096]{1,0:T(8,128)(2,1)S(1)}, u32[]{:S(2)}, u32[]{:S(2)}) %collective-permute-start.16) | collective-permute-done | bytes 262176 | tf_op jit(solution)/shard_map/ring/ppermute | solution.py:306
  67.2 0.1 add_convert_fusion.4
  67.2 3.8 %collective-permute-start.17 = (bf16[32,4096]{1,0:T(8,128)(2,1)S(1)}, bf16[32,4096]{1,0:T(8,128)(2,1)S(1)}, u32[]{:S(2)}, u32[]{:S(2)}) collective-permute-start(bf16[32,4096]{1,0:T(8,128)(2,1)S(1)} %add_convert_fusion.4), channel_id=1, source_target_pairs={{0,1},{1,2},{2,3},{3,4},{4,5},{5,6},{6,7},{7,0},{8,9},{9,10},{10,1... | collective-permute-start | bytes 786440 | tf_op jit(solution)/shard_map/ring/ppermute | solution.py:306
  71.0 0.0 collective-permute-done.19
  71.0 0.1 add_convert_fusion.2
  71.1 0.1 collective-permute-start.20
  71.2 1.6 %collective-permute-done.9 = bf16[32,4096]{1,0:T(8,128)(2,1)S(1)} collective-permute-done((bf16[32,4096]{1,0:T(8,128)(2,1)S(1)}, bf16[32,4096]{1,0:T(8,128)(2,1)S(1)}, u32[]{:S(2)}, u32[]{:S(2)}) %collective-permute-start.9) | collective-permute-done | bytes 262176 | tf_op jit(solution)/shard_map/ring/ppermute | solution.py:306
  72.8 0.1 add_convert_fusion.9
  72.9 3.8 %collective-permute-start.10 = (bf16[32,4096]{1,0:T(8,128)(2,1)S(1)}, bf16[32,4096]{1,0:T(8,128)(2,1)S(1)}, u32[]{:S(2)}, u32[]{:S(2)}) collective-permute-start(bf16[32,4096]{1,0:T(8,128)(2,1)S(1)} %add_convert_fusion.9), channel_id=1, source_target_pairs={{0,1},{1,2},{2,3},{3,4},{4,5},{5,6},{6,7},{7,0},{8,9},{9,10},{10,1... | collective-permute-start | bytes 786440 | tf_op jit(solution)/shard_map/ring/ppermute | solution.py:306
  76.6 0.0 collective-permute-done.13
  76.6 0.1 add_convert_fusion.6
  76.7 0.1 collective-permute-start.14
  76.8 1.6 %collective-permute-done.17 = bf16[32,4096]{1,0:T(8,128)(2,1)S(1)} collective-permute-done((bf16[32,4096]{1,0:T(8,128)(2,1)S(1)}, bf16[32,4096]{1,0:T(8,128)(2,1)S(1)}, u32[]{:S(2)}, u32[]{:S(2)}) %collective-permute-start.17) | collective-permute-done | bytes 262176 | tf_op jit(solution)/shard_map/ring/ppermute | solution.py:306
  78.4 3.7 %collective-permute-done.20 = bf16[32,4096]{1,0:T(8,128)(2,1)S(1)} collective-permute-done((bf16[32,4096]{1,0:T(8,128)(2,1)S(1)}, bf16[32,4096]{1,0:T(8,128)(2,1)S(1)}, u32[]{:S(2)}, u32[]{:S(2)}) %collective-permute-start.20) | collective-permute-done | bytes 262176 | tf_op jit(solution)/shard_map/ring/ppermute | solution.py:306
  82.1 1.1 %collective-permute-done.10 = bf16[32,4096]{1,0:T(8,128)(2,1)S(1)} collective-permute-done((bf16[32,4096]{1,0:T(8,128)(2,1)S(1)}, bf16[32,4096]{1,0:T(8,128)(2,1)S(1)}, u32[]{:S(2)}, u32[]{:S(2)}) %collective-permute-start.10) | collective-permute-done | bytes 262176 | tf_op jit(solution)/shard_map/ring/ppermute | solution.py:306
  83.2 3.4 %collective-permute-done.14 = bf16[32,4096]{1,0:T(8,128)(2,1)S(1)} collective-permute-done((bf16[32,4096]{1,0:T(8,128)(2,1)S(1)}, bf16[32,4096]{1,0:T(8,128)(2,1)S(1)}, u32[]{:S(2)}, u32[]{:S(2)}) %collective-permute-start.14) | collective-permute-done | bytes 262176 | tf_op jit(solution)/shard_map/ring/ppermute | solution.py:306
  86.6 0.2 add_convert_fusion
  86.8 0.8 pad_maximum_fusion
  (9 shorter events, 0.1 us)
Async XLA Ops:
  2.4 1.6 %collective-permute-start = (bf16[528,128]{1,0:T(8,128)(2,1)}, bf16[528,128]{1,0:T(8,128)(2,1)S(1)}, u32[]{:S(2)}, u32[]{:S(2)}) collective-permute-start(bf16[528,128]{1,0:T(8,128)(2,1)} %get-tuple-element.29), channel_id=1, source_target_pairs={{0,8},{8,0},{16,24},{24,16},{32,40},{40,32},{48,56},{56,48},{64,72... | collective-permute-start | bytes 405512 | tf_op jit(solution)/shard_map/prior_states/ppermute | solution.py:215
  4.2 8.9 %collective-permute-start.3 = (bf16[528,128]{1,0:T(8,128)(2,1)S(1)}, bf16[528,128]{1,0:T(8,128)(2,1)S(1)}, u32[]{:S(2)}, u32[]{:S(2)}) collective-permute-start(bf16[528,128]{1,0:T(8,128)(2,1)S(1)} %select_convert_fusion.2), channel_id=1, source_target_pairs={{0,48},{8,56},{16,0},{24,8},{32,16},{40,24},{48,32},{56,40},{64,11... | collective-permute-start | bytes 405512 | tf_op jit(solution)/shard_map/prior_states/ppermute | solution.py:222
  7.0 8.0 %collective-permute-start.2 = (bf16[528,128]{1,0:T(8,128)(2,1)S(1)}, bf16[528,128]{1,0:T(8,128)(2,1)S(1)}, u32[]{:S(2)}, u32[]{:S(2)}) collective-permute-start(bf16[528,128]{1,0:T(8,128)(2,1)S(1)} %select_convert_fusion.2), channel_id=1, source_target_pairs={{0,32},{8,40},{16,48},{24,56},{32,0},{40,8},{48,16},{56,24},{64,96... | collective-permute-start | bytes 405512 | tf_op jit(solution)/shard_map/prior_states/ppermute | solution.py:222
  7.8 9.0 %collective-permute-start.1 = (bf16[528,128]{1,0:T(8,128)(2,1)S(1)}, bf16[528,128]{1,0:T(8,128)(2,1)S(1)}, u32[]{:S(2)}, u32[]{:S(2)}) collective-permute-start(bf16[528,128]{1,0:T(8,128)(2,1)S(1)} %select_convert_fusion.2), channel_id=1, source_target_pairs={{0,16},{8,24},{16,32},{24,40},{32,48},{40,56},{48,0},{56,8},{64,80... | collective-permute-start | bytes 405512 | tf_op jit(solution)/shard_map/prior_states/ppermute | solution.py:222
  17.1 6.9 %collective-permute-start.4 = (bf16[528,128]{1,0:T(8,128)(2,1)S(1)}, bf16[528,128]{1,0:T(8,128)(2,1)S(1)}, u32[]{:S(2)}, u32[]{:S(2)}) collective-permute-start(bf16[528,128]{1,0:T(8,128)(2,1)S(1)} %fusion.4), channel_id=1, source_target_pairs={{0,64},{8,72},{16,80},{24,88},{32,96},{40,104},{48,112},{56,120},{... | collective-permute-start | bytes 405512 | tf_op jit(solution)/shard_map/prior_states/ppermute | solution.py:225
  18.7 9.3 %collective-permute-start.5 = (bf16[528,128]{1,0:T(8,128)(2,1)S(1)}, bf16[528,128]{1,0:T(8,128)(2,1)S(1)}, u32[]{:S(2)}, u32[]{:S(2)}) collective-permute-start(bf16[528,128]{1,0:T(8,128)(2,1)S(1)} %fusion.4), channel_id=1, source_target_pairs={{0,128},{8,136},{16,144},{24,152},{32,160},{40,168},{48,176},{56,1... | collective-permute-start | bytes 405512 | tf_op jit(solution)/shard_map/prior_states/ppermute | solution.py:225
  28.4 1.6 %collective-permute-start.6 = (bf16[528,128]{1,0:T(8,128)(2,1)S(1)}, bf16[528,128]{1,0:T(8,128)(2,1)S(1)}, u32[]{:S(2)}, u32[]{:S(2)}) collective-permute-start(bf16[528,128]{1,0:T(8,128)(2,1)S(1)} %get-tuple-element.51), channel_id=1, source_target_pairs={{0,8},{8,0},{16,24},{24,16},{32,40},{40,32},{48,56},{56,48},{64,72... | collective-permute-start | bytes 405512 | tf_op jit(solution)/shard_map/prior_states/ppermute | solution.py:215
  40.4 9.9 %collective-permute-start.7 = (bf16[32,4096]{1,0:T(8,128)(2,1)S(1)}, bf16[32,4096]{1,0:T(8,128)(2,1)S(1)}, u32[]{:S(2)}, u32[]{:S(2)}) collective-permute-start(bf16[32,4096]{1,0:T(8,128)(2,1)S(1)} %get-tuple-element.31), channel_id=1, source_target_pairs={{0,1},{1,2},{2,3},{3,4},{4,5},{5,6},{6,7},{7,0},{8,9},{9,10},{10,1... | collective-permute-start | bytes 786440 | tf_op jit(solution)/shard_map/ring/ppermute | solution.py:306
  43.6 10.7 %collective-permute-start.11 = (bf16[32,4096]{1,0:T(8,128)(2,1)S(1)}, bf16[32,4096]{1,0:T(8,128)(2,1)S(1)}, u32[]{:S(2)}, u32[]{:S(2)}) collective-permute-start(bf16[32,4096]{1,0:T(8,128)(2,1)S(1)} %get-tuple-element.35), channel_id=1, source_target_pairs={{0,7},{1,0},{2,1},{3,2},{4,3},{5,4},{6,5},{7,6},{8,15},{9,8},{10,9... | collective-permute-start | bytes 786440 | tf_op jit(solution)/shard_map/ring/ppermute | solution.py:306
  43.7 12.3 %collective-permute-start.15 = (bf16[32,4096]{1,0:T(8,128)(2,1)S(1)}, bf16[32,4096]{1,0:T(8,128)(2,1)S(1)}, u32[]{:S(2)}, u32[]{:S(2)}) collective-permute-start(bf16[32,4096]{1,0:T(8,128)(2,1)S(1)} %get-tuple-element.39), channel_id=1, source_target_pairs={{0,1},{1,2},{2,3},{3,4},{4,5},{5,6},{6,7},{7,0},{8,9},{9,10},{10,1... | collective-permute-start | bytes 786440 | tf_op jit(solution)/shard_map/ring/ppermute | solution.py:306
  46.9 12.9 %collective-permute-start.18 = (bf16[32,4096]{1,0:T(8,128)(2,1)S(1)}, bf16[32,4096]{1,0:T(8,128)(2,1)S(1)}, u32[]{:S(2)}, u32[]{:S(2)}) collective-permute-start(bf16[32,4096]{1,0:T(8,128)(2,1)S(1)} %get-tuple-element.42), channel_id=1, source_target_pairs={{0,7},{1,0},{2,1},{3,2},{4,3},{5,4},{6,5},{7,6},{8,15},{9,8},{10,9... | collective-permute-start | bytes 786440 | tf_op jit(solution)/shard_map/ring/ppermute | solution.py:306
  50.4 11.2 %collective-permute-start.8 = (bf16[32,4096]{1,0:T(8,128)(2,1)S(1)}, bf16[32,4096]{1,0:T(8,128)(2,1)S(1)}, u32[]{:S(2)}, u32[]{:S(2)}) collective-permute-start(bf16[32,4096]{1,0:T(8,128)(2,1)S(1)} %add_convert_fusion.11), channel_id=1, source_target_pairs={{0,1},{1,2},{2,3},{3,4},{4,5},{5,6},{6,7},{7,0},{8,9},{9,10},{10,1... | collective-permute-start | bytes 786440 | tf_op jit(solution)/shard_map/ring/ppermute | solution.py:306
  54.4 10.9 %collective-permute-start.12 = (bf16[32,4096]{1,0:T(8,128)(2,1)S(1)}, bf16[32,4096]{1,0:T(8,128)(2,1)S(1)}, u32[]{:S(2)}, u32[]{:S(2)}) collective-permute-start(bf16[32,4096]{1,0:T(8,128)(2,1)S(1)} %add_convert_fusion.8), channel_id=1, source_target_pairs={{0,7},{1,0},{2,1},{3,2},{4,3},{5,4},{6,5},{7,6},{8,15},{9,8},{10,9... | collective-permute-start | bytes 786440 | tf_op jit(solution)/shard_map/ring/ppermute | solution.py:306
  56.0 11.2 %collective-permute-start.16 = (bf16[32,4096]{1,0:T(8,128)(2,1)S(1)}, bf16[32,4096]{1,0:T(8,128)(2,1)S(1)}, u32[]{:S(2)}, u32[]{:S(2)}) collective-permute-start(bf16[32,4096]{1,0:T(8,128)(2,1)S(1)} %add_convert_fusion.5), channel_id=1, source_target_pairs={{0,1},{1,2},{2,3},{3,4},{4,5},{5,6},{6,7},{7,0},{8,9},{9,10},{10,1... | collective-permute-start | bytes 786440 | tf_op jit(solution)/shard_map/ring/ppermute | solution.py:306
  59.8 11.2 %collective-permute-start.19 = (bf16[32,4096]{1,0:T(8,128)(2,1)S(1)}, bf16[32,4096]{1,0:T(8,128)(2,1)S(1)}, u32[]{:S(2)}, u32[]{:S(2)}) collective-permute-start(bf16[32,4096]{1,0:T(8,128)(2,1)S(1)} %add_convert_fusion.3), channel_id=1, source_target_pairs={{0,7},{1,0},{2,1},{3,2},{4,3},{5,4},{6,5},{7,6},{8,15},{9,8},{10,9... | collective-permute-start | bytes 786440 | tf_op jit(solution)/shard_map/ring/ppermute | solution.py:306
  61.6 11.2 %collective-permute-start.9 = (bf16[32,4096]{1,0:T(8,128)(2,1)S(1)}, bf16[32,4096]{1,0:T(8,128)(2,1)S(1)}, u32[]{:S(2)}, u32[]{:S(2)}) collective-permute-start(bf16[32,4096]{1,0:T(8,128)(2,1)S(1)} %add_convert_fusion.10), channel_id=1, source_target_pairs={{0,1},{1,2},{2,3},{3,4},{4,5},{5,6},{6,7},{7,0},{8,9},{9,10},{10,1... | collective-permute-start | bytes 786440 | tf_op jit(solution)/shard_map/ring/ppermute | solution.py:306
  65.5 11.2 %collective-permute-start.13 = (bf16[32,4096]{1,0:T(8,128)(2,1)S(1)}, bf16[32,4096]{1,0:T(8,128)(2,1)S(1)}, u32[]{:S(2)}, u32[]{:S(2)}) collective-permute-start(bf16[32,4096]{1,0:T(8,128)(2,1)S(1)} %add_convert_fusion.7), channel_id=1, source_target_pairs={{0,7},{1,0},{2,1},{3,2},{4,3},{5,4},{6,5},{7,6},{8,15},{9,8},{10,9... | collective-permute-start | bytes 786440 | tf_op jit(solution)/shard_map/ring/ppermute | solution.py:306
  67.2 11.2 %collective-permute-start.17 = (bf16[32,4096]{1,0:T(8,128)(2,1)S(1)}, bf16[32,4096]{1,0:T(8,128)(2,1)S(1)}, u32[]{:S(2)}, u32[]{:S(2)}) collective-permute-start(bf16[32,4096]{1,0:T(8,128)(2,1)S(1)} %add_convert_fusion.4), channel_id=1, source_target_pairs={{0,1},{1,2},{2,3},{3,4},{4,5},{5,6},{6,7},{7,0},{8,9},{9,10},{10,1... | collective-permute-start | bytes 786440 | tf_op jit(solution)/shard_map/ring/ppermute | solution.py:306
  71.1 11.1 %collective-permute-start.20 = (bf16[32,4096]{1,0:T(8,128)(2,1)S(1)}, bf16[32,4096]{1,0:T(8,128)(2,1)S(1)}, u32[]{:S(2)}, u32[]{:S(2)}) collective-permute-start(bf16[32,4096]{1,0:T(8,128)(2,1)S(1)} %add_convert_fusion.2), channel_id=1, source_target_pairs={{0,7},{1,0},{2,1},{3,2},{4,3},{5,4},{6,5},{7,6},{8,15},{9,8},{10,9... | collective-permute-start | bytes 786440 | tf_op jit(solution)/shard_map/ring/ppermute | solution.py:306
  72.9 10.4 %collective-permute-start.10 = (bf16[32,4096]{1,0:T(8,128)(2,1)S(1)}, bf16[32,4096]{1,0:T(8,128)(2,1)S(1)}, u32[]{:S(2)}, u32[]{:S(2)}) collective-permute-start(bf16[32,4096]{1,0:T(8,128)(2,1)S(1)} %add_convert_fusion.9), channel_id=1, source_target_pairs={{0,1},{1,2},{2,3},{3,4},{4,5},{5,6},{6,7},{7,0},{8,9},{9,10},{10,1... | collective-permute-start | bytes 786440 | tf_op jit(solution)/shard_map/ring/ppermute | solution.py:306
  76.7 10.0 %collective-permute-start.14 = (bf16[32,4096]{1,0:T(8,128)(2,1)S(1)}, bf16[32,4096]{1,0:T(8,128)(2,1)S(1)}, u32[]{:S(2)}, u32[]{:S(2)}) collective-permute-start(bf16[32,4096]{1,0:T(8,128)(2,1)S(1)} %add_convert_fusion.6), channel_id=1, source_target_pairs={{0,7},{1,0},{2,1},{3,2},{4,3},{5,4},{6,5},{7,6},{8,15},{9,8},{10,9... | collective-permute-start | bytes 786440 | tf_op jit(solution)/shard_map/ring/ppermute | solution.py:306
